TPU v7x, 32 devices: a whole 2x2x4 slice. The times are simulated.
32 devices in a mesh: fsdp: 8 (over y, x, core), rep: 4 (over z).
Axes of the slice: x: 2, y: 2, z: 4, core: 2. Of those that a mesh axis runs over, the one named last changes fastest.
Arguments:
- tokens: bfloat16 [64, 237, 768], P(('fsdp', 'rep')), may hold values from -6 to 6
- out_grad: bfloat16 [64, 237, 768], P(('fsdp', 'rep')), may hold values from -6 to 6
- masked: int32 [64, 40], P(('fsdp', 'rep')), may hold values from 0 to 1, as said below
- lengths: int32 [64], P(('fsdp', 'rep')), may hold values from 8 to 40, as said below
- mask_vec: bfloat16 [768], P('fsdp'), may hold values from -6 to 6
- norm1_gain: bfloat16 [768], P('fsdp'), may hold values from 0.099609375 to 1.8984375
- norm1_shift: bfloat16 [768], P('fsdp'), may hold values from -4 to 4
- w_qkv: bfloat16 [768, 2304], P('fsdp'), may hold values from -0.21875 to 0.21875
- query_bias: bfloat16 [768], P('fsdp'), may hold values from -4 to 4
- value_bias: bfloat16 [768], P('fsdp'), may hold values from -4 to 4
- w_out: bfloat16 [768, 768], P('fsdp'), may hold values from -0.875 to 0.875
- out_bias: bfloat16 [768], P('fsdp'), may hold values from -4 to 4
- norm2_gain: bfloat16 [768], P('fsdp'), may hold values from 0.099609375 to 1.8984375
- norm2_shift: bfloat16 [768], P('fsdp'), may hold values from -4 to 4
- vision_up: bfloat16 [768, 3072], P('fsdp'), may hold values from -0.21875 to 0.21875
- vision_up_bias: bfloat16 [3072], P('fsdp'), may hold values from -4 to 4
- vision_down: bfloat16 [3072, 768], P('fsdp'), may hold values from -0.21875 to 0.21875
- vision_down_bias: bfloat16 [768], P('fsdp'), may hold values from -4 to 4
- text_up: bfloat16 [768, 3072], P('fsdp'), may hold values from -0.21875 to 0.21875
- text_up_bias: bfloat16 [3072], P('fsdp'), may hold values from -4 to 4
- text_down: bfloat16 [3072, 768], P('fsdp'), may hold values from -0.21875 to 0.21875
- text_down_bias: bfloat16 [768], P('fsdp'), may hold values from -4 to 4
Outputs:
- mixed: bfloat16 [64, 237, 768], P(('fsdp', 'rep'))
- grad_tokens: float32 [64, 237, 768], P(('fsdp', 'rep'))
- grad_mask_vec: float32 [768], P('fsdp')
- grad_norm1_gain: float32 [768], P('fsdp')
- grad_norm1_shift: float32 [768], P('fsdp')
- grad_w_qkv: float32 [768, 2304], P('fsdp')
- grad_query_bias: float32 [768], P('fsdp')
- grad_value_bias: float32 [768], P('fsdp')
- grad_w_out: float32 [768, 768], P('fsdp')
- grad_out_bias: float32 [768], P('fsdp')
- grad_norm2_gain: float32 [768], P('fsdp')
- grad_norm2_shift: float32 [768], P('fsdp')
- grad_vision_up: float32 [768, 3072], P('fsdp')
- grad_vision_up_bias: float32 [3072], P('fsdp')
- grad_vision_down: float32 [3072, 768], P('fsdp')
- grad_vision_down_bias: float32 [768], P('fsdp')
- grad_text_up: float32 [768, 3072], P('fsdp')
- grad_text_up_bias: float32 [3072], P('fsdp')
- grad_text_down: float32 [3072, 768], P('fsdp')
- grad_text_down_bias: float32 [768], P('fsdp')
Inputs may be any that keep to these rules, and one draw needn't show every extreme that they name: A caption fills the first lengths slots of its item; in every draw some item fills all 40 slots. Only slots below the item's length are masked; an item masks between 15 and 80 percent of its length, rounded down, and at least one slot.
All inputs are finite; a program needn't handle non-finite values.
Results may differ from a plain program's by a relative error of at most 0.017.
Values may be sent and summed in bfloat16 or wider, within the bound.
No kernel may reach another device: no remote copies, remote signals or barrier semaphores. Data moves between devices by JAX's collectives and lax.ppermute only.
A program may use at most 192 MiB of HBM per device.

v0:
```python
import jax
import jax.numpy as jnp
from jax import lax
from jax.sharding import PartitionSpec as P

HEAD_DIM = 64


epsilon = 1e-06


def layer_norm(hidden, gain, shift):
    center = hidden - jnp.mean(hidden, axis=-1, keepdims=True)
    spread = jnp.mean(center * center, axis=-1, keepdims=True)
    return center * lax.rsqrt(spread + epsilon) * gain + shift


def exact_gelu(values):
    return jax.nn.gelu(values, approximate=False)


def expert_forward(rows_in, up_matrix, up_shift, down_matrix, down_shift):
    upper = jnp.dot(rows_in, up_matrix, preferred_element_type=jnp.float32) + up_shift.astype(
        jnp.float32
    )
    active, gelu_pull = jax.vjp(exact_gelu, upper)
    active_b = active.astype(jnp.bfloat16)
    result = jnp.dot(active_b, down_matrix, preferred_element_type=jnp.float32) + down_shift.astype(
        jnp.float32
    )
    return (result, active_b, gelu_pull)


def expert_backward(rows_in, active_b, gelu_pull, up_matrix, down_matrix, grad_b):
    grad_down = jnp.einsum("rf,rd->fd", active_b, grad_b, preferred_element_type=jnp.float32)
    grad_down_shift = jnp.sum(grad_b.astype(jnp.float32), axis=0)
    grad_active = jnp.einsum("rd,fd->rf", grad_b, down_matrix, preferred_element_type=jnp.float32)
    (grad_upper,) = gelu_pull(grad_active)
    upper_b = grad_upper.astype(jnp.bfloat16)
    grad_up = jnp.einsum("rd,rf->df", rows_in, upper_b, preferred_element_type=jnp.float32)
    grad_up_shift = jnp.sum(upper_b.astype(jnp.float32), axis=0)
    grad_rows = jnp.einsum("rf,df->rd", upper_b, up_matrix, preferred_element_type=jnp.float32)
    return (grad_up, grad_up_shift, grad_down, grad_down_shift, grad_rows)


def local(
    tokens,
    out_grad,
    masked,
    lengths,
    mask_vec,
    norm1_gain,
    norm1_shift,
    w_qkv,
    query_bias,
    value_bias,
    w_out,
    out_bias,
    norm2_gain,
    norm2_shift,
    vision_up,
    vision_up_bias,
    vision_down,
    vision_down_bias,
    text_up,
    text_up_bias,
    text_down,
    text_down_bias,
):
    item_count, row_count, model_width = tokens.shape
    slot_count = masked.shape[1]
    patches = row_count - slot_count
    head_count = model_width // HEAD_DIM
    split_shape = (item_count, row_count, head_count, HEAD_DIM)

    def fetch_attention():
        return (
            lax.all_gather(mask_vec, "fsdp", axis=0, tiled=True),
            lax.all_gather(norm1_gain, "fsdp", axis=0, tiled=True),
            lax.all_gather(norm1_shift, "fsdp", axis=0, tiled=True),
            lax.all_gather(w_qkv, "fsdp", axis=0, tiled=True),
            lax.all_gather(query_bias, "fsdp", axis=0, tiled=True),
            lax.all_gather(value_bias, "fsdp", axis=0, tiled=True),
            lax.all_gather(w_out, "fsdp", axis=0, tiled=True),
            lax.all_gather(out_bias, "fsdp", axis=0, tiled=True),
        )

    def fetch_feedforward():
        return (
            lax.all_gather(norm2_gain, "fsdp", axis=0, tiled=True),
            lax.all_gather(norm2_shift, "fsdp", axis=0, tiled=True),
            lax.all_gather(vision_up, "fsdp", axis=0, tiled=True),
            lax.all_gather(vision_up_bias, "fsdp", axis=0, tiled=True),
            lax.all_gather(vision_down, "fsdp", axis=0, tiled=True),
            lax.all_gather(vision_down_bias, "fsdp", axis=0, tiled=True),
            lax.all_gather(text_up, "fsdp", axis=0, tiled=True),
            lax.all_gather(text_up_bias, "fsdp", axis=0, tiled=True),
            lax.all_gather(text_down, "fsdp", axis=0, tiled=True),
            lax.all_gather(text_down_bias, "fsdp", axis=0, tiled=True),
        )

    attn_full = fetch_attention()
    full_mask, gain_one, shift_one, qkv_matrix, query_shift, value_shift, out_matrix, out_shift = (
        attn_full
    )
    mask_rows = jnp.concatenate(
        [jnp.zeros((item_count, patches), jnp.float32), masked.astype(jnp.float32)], axis=1
    )[:, :, None]
    hidden0 = mask_rows * full_mask.astype(jnp.float32) + (1.0 - mask_rows) * tokens.astype(
        jnp.float32
    )
    normed1, first_pull = jax.vjp(
        layer_norm, hidden0, gain_one.astype(jnp.float32), shift_one.astype(jnp.float32)
    )
    first_in = normed1.astype(jnp.bfloat16).reshape(item_count * row_count, model_width)
    projected = jnp.dot(first_in, qkv_matrix, preferred_element_type=jnp.float32)
    query_b = (
        ((projected[:, :model_width] + query_shift.astype(jnp.float32)) * 0.125)
        .astype(jnp.bfloat16)
        .reshape(split_shape)
    )
    key_b = projected[:, model_width : 2 * model_width].astype(jnp.bfloat16).reshape(split_shape)
    value_b = (
        (projected[:, 2 * model_width :] + value_shift.astype(jnp.float32))
        .astype(jnp.bfloat16)
        .reshape(split_shape)
    )
    key_index = jnp.arange(row_count, dtype=jnp.int32)
    valid_keys = (key_index[None, :] < patches + lengths[:, None])[:, None, None, :]

    def scores_of():
        raw_scores = jnp.einsum(
            "iqhd,ikhd->ihqk", query_b, key_b, preferred_element_type=jnp.float32
        )
        return jnp.where(valid_keys, raw_scores, -1000000000.0)

    scores = scores_of()
    top_score = jnp.max(scores, axis=-1, keepdims=True)
    expo = jnp.exp(scores - top_score)
    totals = jnp.sum(expo, axis=-1, keepdims=True)
    probs = expo / totals
    log_total = top_score + jnp.log(totals)
    context = jnp.einsum(
        "ihqk,ikhd->iqhd", probs.astype(jnp.bfloat16), value_b, preferred_element_type=jnp.float32
    )
    context_b = context.reshape(item_count * row_count, model_width).astype(jnp.bfloat16)
    attended = jnp.dot(
        context_b, out_matrix, preferred_element_type=jnp.float32
    ) + out_shift.astype(jnp.float32)
    hidden1 = hidden0 + attended.reshape(item_count, row_count, model_width)
    ffn_full = fetch_feedforward()
    (
        gain_two,
        shift_two,
        vision_upm,
        vision_upb,
        vision_downm,
        vision_downb,
        text_upm,
        text_upb,
        text_downm,
        text_downb,
    ) = ffn_full
    normed2, second_pull = jax.vjp(
        layer_norm, hidden1, gain_two.astype(jnp.float32), shift_two.astype(jnp.float32)
    )
    second_in = normed2.astype(jnp.bfloat16)
    patch_in = second_in[:, :patches].reshape(-1, model_width)
    text_in = second_in[:, patches:].reshape(-1, model_width)
    vision_out, vision_act, vision_pull = expert_forward(
        patch_in, vision_upm, vision_upb, vision_downm, vision_downb
    )
    text_out, text_act, text_pull = expert_forward(
        text_in, text_upm, text_upb, text_downm, text_downb
    )
    mixed = hidden1 + jnp.concatenate(
        [
            vision_out.reshape(item_count, patches, model_width),
            text_out.reshape(item_count, slot_count, model_width),
        ],
        axis=1,
    )
    cotangent = out_grad.astype(jnp.float32)
    branch_b = cotangent.astype(jnp.bfloat16)
    ffn_back = fetch_feedforward()
    vision_grads = expert_backward(
        patch_in,
        vision_act,
        vision_pull,
        ffn_back[2],
        ffn_back[4],
        branch_b[:, :patches].reshape(-1, model_width),
    )
    text_grads = expert_backward(
        text_in,
        text_act,
        text_pull,
        ffn_back[6],
        ffn_back[8],
        branch_b[:, patches:].reshape(-1, model_width),
    )
    grad_normed2 = jnp.concatenate(
        [
            vision_grads[4].reshape(item_count, patches, model_width),
            text_grads[4].reshape(item_count, slot_count, model_width),
        ],
        axis=1,
    )
    grad_hidden1_norm, grad_gain_two, grad_shift_two = second_pull(grad_normed2)
    grad_hidden1 = cotangent + grad_hidden1_norm
    attn_back = fetch_attention()
    grad_attn_b = grad_hidden1.reshape(-1, model_width).astype(jnp.bfloat16)
    grad_out_matrix = jnp.einsum(
        "rd,re->de", context_b, grad_attn_b, preferred_element_type=jnp.float32
    )
    grad_out_shift = jnp.sum(grad_attn_b.astype(jnp.float32), axis=0)
    grad_context = jnp.einsum(
        "re,de->rd", grad_attn_b, attn_back[6], preferred_element_type=jnp.float32
    )
    grad_context_b = grad_context.astype(jnp.bfloat16).reshape(split_shape)
    again_probs = jnp.exp(scores_of() - log_total)
    grad_probs = jnp.einsum(
        "iqhd,ikhd->ihqk", grad_context_b, value_b, preferred_element_type=jnp.float32
    )
    grad_value = jnp.einsum(
        "ihqk,iqhd->ikhd",
        again_probs.astype(jnp.bfloat16),
        grad_context_b,
        preferred_element_type=jnp.float32,
    )
    row_inner = jnp.sum(again_probs * grad_probs, axis=-1, keepdims=True)
    grad_scores_b = (again_probs * (grad_probs - row_inner)).astype(jnp.bfloat16)
    grad_query = jnp.einsum(
        "ihqk,ikhd->iqhd", grad_scores_b, key_b, preferred_element_type=jnp.float32
    )
    grad_key = jnp.einsum(
        "ihqk,iqhd->ikhd", grad_scores_b, query_b, preferred_element_type=jnp.float32
    )
    grad_query_b = grad_query.astype(jnp.bfloat16) * jnp.bfloat16(0.125)
    stacked = jnp.concatenate(
        [
            grad_query_b.reshape(-1, model_width),
            grad_key.astype(jnp.bfloat16).reshape(-1, model_width),
            grad_value.astype(jnp.bfloat16).reshape(-1, model_width),
        ],
        axis=1,
    )
    grad_qkv = jnp.einsum("rd,re->de", first_in, stacked, preferred_element_type=jnp.float32)
    grad_query_shift = jnp.sum(stacked[:, :model_width].astype(jnp.float32), axis=0)
    grad_value_shift = jnp.sum(stacked[:, 2 * model_width :].astype(jnp.float32), axis=0)
    grad_normed1 = jnp.einsum(
        "re,de->rd", stacked, attn_back[3], preferred_element_type=jnp.float32
    )
    grad_hidden0_norm, grad_gain_one, grad_shift_one = first_pull(
        grad_normed1.reshape(item_count, row_count, model_width)
    )
    grad_hidden0 = grad_hidden1 + grad_hidden0_norm
    grad_tokens = grad_hidden0 * (1.0 - mask_rows)
    grad_mask = jnp.sum(grad_hidden0 * mask_rows, axis=(0, 1))
    ffn_share = (
        lax.psum_scatter(grad_gain_two, "fsdp", scatter_dimension=0, tiled=True),
        lax.psum_scatter(grad_shift_two, "fsdp", scatter_dimension=0, tiled=True),
        lax.psum_scatter(vision_grads[0], "fsdp", scatter_dimension=0, tiled=True),
        lax.psum_scatter(vision_grads[1], "fsdp", scatter_dimension=0, tiled=True),
        lax.psum_scatter(vision_grads[2], "fsdp", scatter_dimension=0, tiled=True),
        lax.psum_scatter(vision_grads[3], "fsdp", scatter_dimension=0, tiled=True),
        lax.psum_scatter(text_grads[0], "fsdp", scatter_dimension=0, tiled=True),
        lax.psum_scatter(text_grads[1], "fsdp", scatter_dimension=0, tiled=True),
        lax.psum_scatter(text_grads[2], "fsdp", scatter_dimension=0, tiled=True),
        lax.psum_scatter(text_grads[3], "fsdp", scatter_dimension=0, tiled=True),
    )
    attn_share = (
        lax.psum_scatter(grad_mask, "fsdp", scatter_dimension=0, tiled=True),
        lax.psum_scatter(grad_gain_one, "fsdp", scatter_dimension=0, tiled=True),
        lax.psum_scatter(grad_shift_one, "fsdp", scatter_dimension=0, tiled=True),
        lax.psum_scatter(grad_qkv, "fsdp", scatter_dimension=0, tiled=True),
        lax.psum_scatter(grad_query_shift, "fsdp", scatter_dimension=0, tiled=True),
        lax.psum_scatter(grad_value_shift, "fsdp", scatter_dimension=0, tiled=True),
        lax.psum_scatter(grad_out_matrix, "fsdp", scatter_dimension=0, tiled=True),
        lax.psum_scatter(grad_out_shift, "fsdp", scatter_dimension=0, tiled=True),
    )
    quarter = (
        lax.psum_scatter(
            attn_share[0].astype(jnp.bfloat16), "rep", scatter_dimension=0, tiled=True
        ).astype(jnp.float32),
        lax.psum_scatter(
            attn_share[1].astype(jnp.bfloat16), "rep", scatter_dimension=0, tiled=True
        ).astype(jnp.float32),
        lax.psum_scatter(
            attn_share[2].astype(jnp.bfloat16), "rep", scatter_dimension=0, tiled=True
        ).astype(jnp.float32),
        lax.psum_scatter(
            attn_share[3].astype(jnp.bfloat16), "rep", scatter_dimension=0, tiled=True
        ).astype(jnp.float32),
        lax.psum_scatter(
            attn_share[4].astype(jnp.bfloat16), "rep", scatter_dimension=0, tiled=True
        ).astype(jnp.float32),
        lax.psum_scatter(
            attn_share[5].astype(jnp.bfloat16), "rep", scatter_dimension=0, tiled=True
        ).astype(jnp.float32),
        lax.psum_scatter(
            attn_share[6].astype(jnp.bfloat16), "rep", scatter_dimension=0, tiled=True
        ).astype(jnp.float32),
        lax.psum_scatter(
            attn_share[7].astype(jnp.bfloat16), "rep", scatter_dimension=0, tiled=True
        ).astype(jnp.float32),
        lax.psum_scatter(
            ffn_share[0].astype(jnp.bfloat16), "rep", scatter_dimension=0, tiled=True
        ).astype(jnp.float32),
        lax.psum_scatter(
            ffn_share[1].astype(jnp.bfloat16), "rep", scatter_dimension=0, tiled=True
        ).astype(jnp.float32),
        lax.psum_scatter(
            ffn_share[2].astype(jnp.bfloat16), "rep", scatter_dimension=0, tiled=True
        ).astype(jnp.float32),
        lax.psum_scatter(
            ffn_share[3].astype(jnp.bfloat16), "rep", scatter_dimension=0, tiled=True
        ).astype(jnp.float32),
        lax.psum_scatter(
            ffn_share[4].astype(jnp.bfloat16), "rep", scatter_dimension=0, tiled=True
        ).astype(jnp.float32),
        lax.psum_scatter(
            ffn_share[5].astype(jnp.bfloat16), "rep", scatter_dimension=0, tiled=True
        ).astype(jnp.float32),
        lax.psum_scatter(
            ffn_share[6].astype(jnp.bfloat16), "rep", scatter_dimension=0, tiled=True
        ).astype(jnp.float32),
        lax.psum_scatter(
            ffn_share[7].astype(jnp.bfloat16), "rep", scatter_dimension=0, tiled=True
        ).astype(jnp.float32),
        lax.psum_scatter(
            ffn_share[8].astype(jnp.bfloat16), "rep", scatter_dimension=0, tiled=True
        ).astype(jnp.float32),
        lax.psum_scatter(
            ffn_share[9].astype(jnp.bfloat16), "rep", scatter_dimension=0, tiled=True
        ).astype(jnp.float32),
    )
    summed = (
        lax.all_gather(quarter[0].astype(jnp.bfloat16), "rep", axis=0, tiled=True).astype(
            jnp.float32
        ),
        lax.all_gather(quarter[1].astype(jnp.bfloat16), "rep", axis=0, tiled=True).astype(
            jnp.float32
        ),
        lax.all_gather(quarter[2].astype(jnp.bfloat16), "rep", axis=0, tiled=True).astype(
            jnp.float32
        ),
        lax.all_gather(quarter[3].astype(jnp.bfloat16), "rep", axis=0, tiled=True).astype(
            jnp.float32
        ),
        lax.all_gather(quarter[4].astype(jnp.bfloat16), "rep", axis=0, tiled=True).astype(
            jnp.float32
        ),
        lax.all_gather(quarter[5].astype(jnp.bfloat16), "rep", axis=0, tiled=True).astype(
            jnp.float32
        ),
        lax.all_gather(quarter[6].astype(jnp.bfloat16), "rep", axis=0, tiled=True).astype(
            jnp.float32
        ),
        lax.all_gather(quarter[7].astype(jnp.bfloat16), "rep", axis=0, tiled=True).astype(
            jnp.float32
        ),
        lax.all_gather(quarter[8].astype(jnp.bfloat16), "rep", axis=0, tiled=True).astype(
            jnp.float32
        ),
        lax.all_gather(quarter[9].astype(jnp.bfloat16), "rep", axis=0, tiled=True).astype(
            jnp.float32
        ),
        lax.all_gather(quarter[10].astype(jnp.bfloat16), "rep", axis=0, tiled=True).astype(
            jnp.float32
        ),
        lax.all_gather(quarter[11].astype(jnp.bfloat16), "rep", axis=0, tiled=True).astype(
            jnp.float32
        ),
        lax.all_gather(quarter[12].astype(jnp.bfloat16), "rep", axis=0, tiled=True).astype(
            jnp.float32
        ),
        lax.all_gather(quarter[13].astype(jnp.bfloat16), "rep", axis=0, tiled=True).astype(
            jnp.float32
        ),
        lax.all_gather(quarter[14].astype(jnp.bfloat16), "rep", axis=0, tiled=True).astype(
            jnp.float32
        ),
        lax.all_gather(quarter[15].astype(jnp.bfloat16), "rep", axis=0, tiled=True).astype(
            jnp.float32
        ),
        lax.all_gather(quarter[16].astype(jnp.bfloat16), "rep", axis=0, tiled=True).astype(
            jnp.float32
        ),
        lax.all_gather(quarter[17].astype(jnp.bfloat16), "rep", axis=0, tiled=True).astype(
            jnp.float32
        ),
    )
    return (
        mixed.astype(jnp.bfloat16),
        grad_tokens,
        summed[0],
        summed[1],
        summed[2],
        summed[3],
        summed[4],
        summed[5],
        summed[6],
        summed[7],
        summed[8],
        summed[9],
        summed[10],
        summed[11],
        summed[12],
        summed[13],
        summed[14],
        summed[15],
        summed[16],
        summed[17],
    )


def solution(mesh):
    return jax.shard_map(
        local,
        mesh=mesh,
        in_specs=(
            P(("fsdp", "rep"), None, None),
            P(("fsdp", "rep"), None, None),
            P(("fsdp", "rep"), None),
            P(("fsdp", "rep")),
            P("fsdp"),
            P("fsdp"),
            P("fsdp"),
            P("fsdp", None),
            P("fsdp"),
            P("fsdp"),
            P("fsdp", None),
            P("fsdp"),
            P("fsdp"),
            P("fsdp"),
            P("fsdp", None),
            P("fsdp"),
            P("fsdp", None),
            P("fsdp"),
            P("fsdp", None),
            P("fsdp"),
            P("fsdp", None),
            P("fsdp"),
        ),
        out_specs=(
            P(("fsdp", "rep"), None, None),
            P(("fsdp", "rep"), None, None),
            P("fsdp"),
            P("fsdp"),
            P("fsdp"),
            P("fsdp", None),
            P("fsdp"),
            P("fsdp"),
            P("fsdp", None),
            P("fsdp"),
            P("fsdp"),
            P("fsdp"),
            P("fsdp", None),
            P("fsdp"),
            P("fsdp", None),
            P("fsdp"),
            P("fsdp", None),
            P("fsdp"),
            P("fsdp", None),
            P("fsdp"),
        ),
        check_vma=False,
    )
```

profile of v0, /device:TPU:0, one launch (start us, length us, event | category | flops | bytes accessed | tf_op | source)
XLA Modules:
  0.0 888.9 jit_solution(4440265537240704992)
XLA Ops:
  16.1 26.0 %all-reduce.48 = (bf16[768]{0:T(1024)(128)(2,1)S(1)}, bf16[768]{0:T(1024)(128)(2,1)S(1)}, bf16[768]{0:T(1024)(128)(2,1)S(1)}, bf16[768]{0:T(1024)(128)(2,1)S(1)}...) all-reduce(bf16[768]{0:T(1024)(128)(2,1)S(1)} %dynamic-update-slice, ...), channel_id=1, replica_groups=mesh['fsdp'=8,'rep'=4] {'fsdp'}, use_global_device_ids=true, to_apply=%add.3 | all-reduce | flops 7680 | bytes 30720
  42.3 7.8 all-gather.1
  50.1 9.0 %all-gather = bf16[8,1,384]{2,1,0:T(2,128)(2,1)S(1)} all-gather(bf16[1,1,384]{2,1,0:T(2,128)(2,1)S(1)} %reshape.291), channel_id=1, replica_groups=mesh['fsdp'=8,'rep'=4] {'fsdp'}, dimensions={0}, use_global_device_ids=true | all-gather | bytes 6912 | tf_op jit(solution)/shard_map/all_gather | solution.py:93
  63.0 3.9 fusion.67
  72.4 2.6 copy.91
  75.0 3.0 reshape.209
  84.7 3.4 convolution_add_fusion.1
  88.1 2.7 reshape.211
  94.3 2.0 reshape.212
  96.3 17.3 %all-gather.17.cloned.1.call-done = bf16[768,3072]{1,0:T(8,128)(2,1)} async-done(((bf16[96,3072]{1,0:T(8,128)(2,1)}), bf16[768,3072]{1,0:T(8,128)(2,1)}) %all-gather.17.cloned.1.call-update) | async-done | bytes 4718608 | tf_op jit(solution)/shard_map/all_gather | solution.py:96
  113.6 4.2 convolution_add_fusion
  117.8 36.5 %all-gather.13.cloned.1.call-done = bf16[768,3072]{1,0:T(8,128)(2,1)} async-done(((bf16[96,3072]{1,0:T(8,128)(2,1)}), bf16[768,3072]{1,0:T(8,128)(2,1)}) %all-gather.13.cloned.1.call-update) | async-done | bytes 4718608 | tf_op jit(solution)/shard_map/all_gather | solution.py:92
  154.3 6.9 fusion.68
  161.2 33.8 %all-gather.19.cloned.1.call-done = bf16[3072,768]{1,0:T(8,128)(2,1)} async-done(((bf16[384,768]{1,0:T(8,128)(2,1)}), bf16[3072,768]{1,0:T(8,128)(2,1)}) %all-gather.19.cloned.1.call-update) | async-done | bytes 4718608 | tf_op jit(solution)/shard_map/all_gather | solution.py:98
  195.0 7.0 convert_reduce_fusion.5
  202.9 32.8 %all-gather.15.cloned.1.call-done = bf16[3072,768]{1,0:T(8,128)(2,1)} async-done(((bf16[384,768]{1,0:T(8,128)(2,1)}), bf16[3072,768]{1,0:T(8,128)(2,1)}) %all-gather.15.cloned.1.call-update) | async-done | bytes 4718608 | tf_op jit(solution)/shard_map/all_gather | solution.py:94
  235.7 15.7 %convert_reduce_fusion = (f32[3072]{0:T(1024)S(1)}, bf16[394,3072]{1,0:T(8,128)(2,1)}, f32[394,3072]{1,0:T(8,128)S(1)}) fusion(f32[394,3072]{1,0:T(8,128)} %fusion.68, f32[3072]{0:T(1024)S(1)} %bitcast.82, bf16[394,768]{1,0:T(8,128)(2,1)} %reshape.216, bf16[3072,768]{1,0:T(8,128)(2,1)} %all-gather.15.cloned.1.call-done), kind=kOutput, calls=%fused_computation.8 | convolution fusion | flops 1949899776 | bytes 17452032 | tf_op jit(solution)/shard_map/rd,fd->rf/dot_general | solution.py:37
  251.4 3.8 multiply_convert_fusion.1
  256.7 3.1 convolution_add_fusion.2
  259.8 2.5 reshape.213
  262.3 6.2 fusion.65
  268.5 2.5 reshape.217
  271.0 4.1 fusion.66
  276.2 3.3 convolution_add_fusion.3
  283.5 3.4 fusion.70
  287.2 2.0 convolution_convert_fusion.2
  290.0 4.6 convert_reduce_fusion.1
  296.3 3.3 reshape.223
  299.6 5.4 multiply_reduce_fusion
  311.2 2.5 reshape.222
  313.7 2.6 convert_reduce_fusion.2
  318.0 3.5 reshape.221
  324.3 4.9 fusion.69
  330.3 8.1 fusion.72
  339.6 7.8 fusion.71
  348.5 5.1 fusion.74
  354.6 5.7 fusion.73
  362.1 36.9 %reduce-scatter.13.cloned.1.call-done = f32[96,2304]{1,0:T(8,128)} async-done(((f32[768,2304]{1,0:T(8,128)}), f32[96,2304]{1,0:T(8,128)}) %reduce-scatter.13.cloned.1.call-update) | async-done | bytes 884752 | tf_op jit(solution)/shard_map/reduce_scatter | solution.py:276
  399.0 2.0 convert_element_type.335
  401.1 78.0 %reduce-scatter.25.cloned.1.call-done = f32[384,768]{1,0:T(8,128)} async-done(((f32[3072,768]{1,0:T(8,128)}), f32[384,768]{1,0:T(8,128)}) %reduce-scatter.25.cloned.1.call-update) | async-done | bytes 1179664 | tf_op jit(solution)/shard_map/reduce_scatter | solution.py:265
  479.0 2.1 convert_element_type.357
  481.2 77.6 %reduce-scatter.21.cloned.1.call-done = f32[96,3072]{1,0:T(8,128)} async-done(((f32[768,3072]{1,0:T(8,128)}), f32[96,3072]{1,0:T(8,128)}) %reduce-scatter.21.cloned.1.call-update) | async-done | bytes 1179664 | tf_op jit(solution)/shard_map/reduce_scatter | solution.py:263
  558.9 2.2 convert_element_type.352
  566.8 6.7 fusion.64
  575.3 63.6 %reduce-scatter.33.cloned.1.call-done = f32[384,768]{1,0:T(8,128)} async-done(((f32[3072,768]{1,0:T(8,128)}), f32[384,768]{1,0:T(8,128)}) %reduce-scatter.33.cloned.1.call-update) | async-done | bytes 1179664 | tf_op jit(solution)/shard_map/reduce_scatter | solution.py:269
  638.9 2.1 convert_element_type.367
  647.1 23.9 %all-reduce.47 = (bf16[768]{0:T(1024)(128)(2,1)S(1)}, bf16[768]{0:T(1024)(128)(2,1)S(1)}, bf16[768]{0:T(1024)(128)(2,1)S(1)}, bf16[768]{0:T(1024)(128)(2,1)S(1)}...) all-reduce(f32[768]{0:T(1024)S(1)} %get-tuple-element.118, ...), channel_id=2, replica_groups=mesh['fsdp'=8,'rep'=4] {'fsdp'}, use_global_device_ids=true, to_apply=%region_12.13.clone | all-reduce | flops 13824 | bytes 82944
  671.9 11.8 %all-reduce.50 = (bf16[96]{0:T(256)(128)(2,1)S(1)}, bf16[96]{0:T(256)(128)(2,1)S(1)}, bf16[96]{0:T(256)(128)(2,1)S(1)}, bf16[96]{0:T(256)(128)(2,1)S(1)}, bf16[9...) all-reduce(bf16[96]{0:T(256)(128)(2,1)S(1)} %dynamic-slice.93, ...), channel_id=3, replica_groups=mesh['fsdp'=8,'rep'=4] {'rep'}, use_global_device_ids=true, to_apply=%region_13.14.clone | all-reduce | flops 1728 | bytes 6912
  687.3 8.5 all-reduce.49
  702.0 16.8 %reduce-scatter.29.cloned.1.call-done = f32[96,3072]{1,0:T(8,128)} async-done(((f32[768,3072]{1,0:T(8,128)}), f32[96,3072]{1,0:T(8,128)}) %reduce-scatter.29.cloned.1.call-update) | async-done | bytes 1179664 | tf_op jit(solution)/shard_map/reduce_scatter | solution.py:267
  718.8 2.1 convert_element_type.362
  721.1 2.2 copy.114
  723.4 17.6 %reduce-scatter.19.cloned.1.call-done = bf16[24,768]{1,0:T(8,128)(2,1)} async-done(((bf16[96,768]{1,0:T(8,128)(2,1)}), bf16[24,768]{1,0:T(8,128)(2,1)}) %reduce-scatter.19.cloned.1.call-update) | async-done | bytes 36880 | tf_op jit(solution)/shard_map/reduce_scatter | solution.py:301
  740.9 14.1 %all_gather.138 = bf16[96,768]{1,0:T(8,128)(2,1)S(1)} all-gather(bf16[24,768]{1,0:T(8,128)(2,1)} %reduce-scatter.19.cloned.1.call-done), channel_id=1, replica_groups=mesh['fsdp'=8,'rep'=4] {'rep'}, dimensions={0}, use_global_device_ids=true | all-gather | bytes 184320 | tf_op jit(solution)/shard_map/all_gather | solution.py:357
  755.7 7.0 reduce-scatter.15.cloned.1.call-done
  762.7 18.0 %all_gather.135 = bf16[96,2304]{1,0:T(8,128)(2,1)S(1)} all-gather(bf16[24,2304]{1,0:T(8,128)(2,1)} %reduce-scatter.15.cloned.1.call-done), channel_id=1, replica_groups=mesh['fsdp'=8,'rep'=4] {'rep'}, dimensions={0}, use_global_device_ids=true | all-gather | bytes 552960 | tf_op jit(solution)/shard_map/all_gather | solution.py:348
  781.7 5.2 reduce-scatter.27.cloned.1.call-done
  786.9 20.0 %all_gather.144 = bf16[384,768]{1,0:T(8,128)(2,1)S(1)} all-gather(bf16[96,768]{1,0:T(8,128)(2,1)} %reduce-scatter.27.cloned.1.call-done), channel_id=1, replica_groups=mesh['fsdp'=8,'rep'=4] {'rep'}, dimensions={0}, use_global_device_ids=true | all-gather | bytes 737280 | tf_op jit(solution)/shard_map/all_gather | solution.py:375
  808.0 4.9 reduce-scatter.23.cloned.1.call-done
  813.0 20.0 %all_gather.142 = bf16[96,3072]{1,0:T(8,128)(2,1)S(1)} all-gather(bf16[24,3072]{1,0:T(8,128)(2,1)} %reduce-scatter.23.cloned.1.call-done), channel_id=1, replica_groups=mesh['fsdp'=8,'rep'=4] {'rep'}, dimensions={0}, use_global_device_ids=true | all-gather | bytes 737280 | tf_op jit(solution)/shard_map/all_gather | solution.py:369
  834.0 4.7 reduce-scatter.35.cloned.1.call-done
  838.7 20.2 %all_gather.148 = bf16[384,768]{1,0:T(8,128)(2,1)S(1)} all-gather(bf16[96,768]{1,0:T(8,128)(2,1)} %reduce-scatter.35.cloned.1.call-done), channel_id=1, replica_groups=mesh['fsdp'=8,'rep'=4] {'rep'}, dimensions={0}, use_global_device_ids=true | all-gather | bytes 737280 | tf_op jit(solution)/shard_map/all_gather | solution.py:387
  860.0 4.2 reduce-scatter.31.cloned.1.call-done
  864.2 16.4 %all_gather.146 = bf16[96,3072]{1,0:T(8,128)(2,1)S(1)} all-gather(bf16[24,3072]{1,0:T(8,128)(2,1)} %reduce-scatter.31.cloned.1.call-done), channel_id=1, replica_groups=mesh['fsdp'=8,'rep'=4] {'rep'}, dimensions={0}, use_global_device_ids=true | all-gather | bytes 737280 | tf_op jit(solution)/shard_map/all_gather | solution.py:381
  (321 shorter events, 80.7 us)
Async XLA Ops:
  7.2 4.2 copy-start.3
  7.2 55.8 %all-gather.9.cloned.1.call-start = ((), (), s32[]{:S(2)}) async-start(), calls=%async_computation.12 | async-start | bytes 3981312 | tf_op jit(solution)/shard_map/all_gather | solution.py:81
  7.9 76.7 %all-gather.11.cloned.1.call-start = ((), (), s32[]{:S(2)}) async-start(), calls=%async_computation.13 | async-start | bytes 1327104 | tf_op jit(solution)/shard_map/all_gather | solution.py:84
  8.7 3.7 copy-start.40
  8.7 3.7 copy-start.41
  8.7 3.7 copy-start.42
  8.7 3.7 copy-start.38
  8.7 3.7 copy-start.39
  8.7 5.0 copy-start.44
  8.8 5.2 copy-start.45
  8.8 5.4 copy-start.46
  8.8 5.7 copy-start.47
  8.8 5.9 copy-start.48
  8.8 6.1 copy-start.49
  8.8 6.3 copy-start.50
  8.8 6.6 copy-start.51
  8.8 6.8 copy-start.52
  8.8 7.0 copy-start.53
  8.8 104.8 %all-gather.17.cloned.1.call-start = ((), (), s32[]{:S(2)}) async-start(), calls=%async_computation.16 | async-start | bytes 5308416 | tf_op jit(solution)/shard_map/all_gather | solution.py:96
  9.6 49.5 %slice-start.2 = ((bf16[2,237,768]{2,0,1:T(2,128)(2,1)}), bf16[2,197,768]{2,0,1:T(2,128)(2,1)S(1)}, s32[]{:S(2)}) async-start(bf16[2,237,768]{2,0,1:T(2,128)(2,1)} %param.23), calls=%async_computation.32 | async-start | bytes 1210368 | tf_op jit(solution)/shard_map/slice | solution.py:192
  9.6 144.7 %all-gather.13.cloned.1.call-start = ((), (), s32[]{:S(2)}) async-start(), calls=%async_computation.14 | async-start | bytes 5308416 | tf_op jit(solution)/shard_map/all_gather | solution.py:92
  10.2 184.8 %all-gather.19.cloned.1.call-start = ((), (), s32[]{:S(2)}) async-start(), calls=%async_computation.17 | async-start | bytes 5308416 | tf_op jit(solution)/shard_map/all_gather | solution.py:98
  10.8 224.9 %all-gather.15.cloned.1.call-start = ((), (), s32[]{:S(2)}) async-start(), calls=%async_computation.15 | async-start | bytes 5308416 | tf_op jit(solution)/shard_map/all_gather | solution.py:94
  11.3 349.1 %reduce-scatter.17.cloned.1.call-start = ((), (), s32[]{:S(2)}) async-start(), calls=%async_computation.20 | async-start | bytes 2654208 | tf_op jit(solution)/shard_map/reduce_scatter | solution.py:279
  11.4 48.7 %copy-start.1 = (bf16[2,237,768]{2,0,1:T(2,128)(2,1)S(1)}, bf16[2,237,768]{2,0,1:T(2,128)(2,1)}, u32[]{:S(2)}) copy-start(bf16[2,237,768]{2,0,1:T(2,128)(2,1)} %param.22) | copy-start | bytes 2184196
  42.2 19.4 %copy-start.30 = (f32[768]{0:T(1024)}, f32[768]{0:T(1024)S(1)}, u32[]{:S(2)}) copy-start(f32[768]{0:T(1024)S(1)} %convert_element_type.294) | copy-start | bytes 9220
  60.1 2.8 copy-start.54
  60.5 6.3 copy-start.32
  61.1 5.8 copy-start.36
  61.1 5.8 copy-start.34
  61.8 5.2 copy-start.23
  72.4 6.9 copy-start.7
  79.4 2.6 copy-start
  79.4 2.6 copy-start.17
  84.6 3.5 copy-start.20
  195.0 7.0 copy-start.16
  251.4 5.2 copy-start.43
  271.0 4.2 copy-start.6
  276.2 3.4 copy-start.14
  281.1 2.4 copy-start.21
  283.5 3.7 copy-start.25
  286.9 112.1 %reduce-scatter.13.cloned.1.call-start = ((), (), s32[]{:S(2)}) async-start(), calls=%async_computation.18 | async-start | bytes 7962624 | tf_op jit(solution)/shard_map/reduce_scatter | solution.py:276
  290.0 4.6 copy-start.18
  296.3 8.8 slice-start
  299.6 5.5 slice-start.1
  305.1 3.4 copy-start.10
  309.5 4.2 copy-start.8
  318.0 4.8 copy-start.19
  321.5 2.8 copy-start.24
  329.2 149.8 %reduce-scatter.25.cloned.1.call-start = ((), (), s32[]{:S(2)}) async-start(), calls=%async_computation.24 | async-start | bytes 10616832 | tf_op jit(solution)/shard_map/reduce_scatter | solution.py:265
  338.4 220.5 %reduce-scatter.21.cloned.1.call-start = ((), (), s32[]{:S(2)}) async-start(), calls=%async_computation.22 | async-start | bytes 10616832 | tf_op jit(solution)/shard_map/reduce_scatter | solution.py:263
  347.4 291.5 %reduce-scatter.33.cloned.1.call-start = ((), (), s32[]{:S(2)}) async-start(), calls=%async_computation.28 | async-start | bytes 10616832 | tf_op jit(solution)/shard_map/reduce_scatter | solution.py:269
  353.6 365.2 %reduce-scatter.29.cloned.1.call-start = ((), (), s32[]{:S(2)}) async-start(), calls=%async_computation.26 | async-start | bytes 10616832 | tf_op jit(solution)/shard_map/reduce_scatter | solution.py:267
  360.4 380.6 %reduce-scatter.19.cloned.1.call-start = ((), (), s32[]{:S(2)}) async-start(), calls=%async_computation.21 | async-start | bytes 184320 | tf_op jit(solution)/shard_map/reduce_scatter | solution.py:301
  362.1 400.6 %reduce-scatter.15.cloned.1.call-start = ((), (), s32[]{:S(2)}) async-start(), calls=%async_computation.19 | async-start | bytes 552960 | tf_op jit(solution)/shard_map/reduce_scatter | solution.py:292
  401.0 385.9 %reduce-scatter.27.cloned.1.call-start = ((), (), s32[]{:S(2)}) async-start(), calls=%async_computation.25 | async-start | bytes 737280 | tf_op jit(solution)/shard_map/reduce_scatter | solution.py:319
  481.2 331.8 %reduce-scatter.23.cloned.1.call-start = ((), (), s32[]{:S(2)}) async-start(), calls=%async_computation.23 | async-start | bytes 737280 | tf_op jit(solution)/shard_map/reduce_scatter | solution.py:313
  561.1 277.6 %reduce-scatter.35.cloned.1.call-start = ((), (), s32[]{:S(2)}) async-start(), calls=%async_computation.29 | async-start | bytes 737280 | tf_op jit(solution)/shard_map/reduce_scatter | solution.py:331
  573.5 67.6 %copy-start.31 = (f32[768]{0:T(1024)S(1)}, f32[768]{0:T(1024)}, u32[]{:S(2)}) copy-start(f32[768]{0:T(1024)} %copy-done.30) | copy-start | bytes 9220
  573.5 67.7 %copy-start.33 = (f32[2,237]{1,0:T(2,128)S(1)}, f32[2,237]{1,0:T(2,128)}, u32[]{:S(2)}) copy-start(f32[2,237]{1,0:T(2,128)} %copy-done.32) | copy-start | bytes 5692
  641.1 2.8 copy-start.37
  641.1 2.8 copy-start.35
  641.1 223.1 %reduce-scatter.31.cloned.1.call-start = ((), (), s32[]{:S(2)}) async-start(), calls=%async_computation.27 | async-start | bytes 737280 | tf_op jit(solution)/shard_map/reduce_scatter | solution.py:325
  647.1 73.9 %copy-start.13 = (f32[2,237,768]{2,1,0:T(8,128)S(1)}, f32[2,237,768]{2,1,0:T(8,128)}, u32[]{:S(2)}) copy-start(f32[2,237,768]{2,1,0:T(8,128)} %get-tuple-element.119) | copy-start | bytes 4368388
  (12 other events, 14.9 us)
Sparse Core Ops, SparseCore 0:
  9.9 36.8 all-gather.8
  48.7 24.0 all-gather.10
  74.7 38.9 all-gather.16
  115.4 38.9 all-gather.12
  156.0 38.9 all-gather.18
  196.7 38.9 all-gather.14
  287.0 42.4 reduce-scatter.16
  333.5 65.4 reduce-scatter.12
  402.5 76.4 reduce-scatter.24
  482.4 76.4 reduce-scatter.20
  562.4 76.4 reduce-scatter.32
  642.3 76.4 reduce-scatter.28
  721.6 19.2 reduce-scatter.18
  743.7 18.9 reduce-scatter.14
  765.4 21.4 reduce-scatter.26
  789.6 23.2 reduce-scatter.22
  815.1 23.5 reduce-scatter.34
  840.8 23.2 reduce-scatter.30
where the time goes:
time: 898 us; the launch traced here: 889 us
  waiting for transfers between devices  441 us (49%)
  blocking collectives  196 us (22%)
  matrix products  118 us (13%)
  local copies, waits for them, and re-layouts  67.9 us (8%)
  other arithmetic  45.2 us (5%)
  between operations  20.3 us (2%)
    reduce_scatter x1, waiting for transfers between devices, local(): lax.psum_scatter(vision_grads[2], 'fsdp', scatter_dimension=0, tiled=True)  78 us
    reduce_scatter x1, waiting for transfers between devices, local(): lax.psum_scatter(vision_grads[0], 'fsdp', scatter_dimension=0, tiled=True)  77.6 us
    unnamed x4, blocking collectives  70.2 us
    reduce_scatter x1, waiting for transfers between devices, local(): lax.psum_scatter(text_grads[2], 'fsdp', scatter_dimension=0, tiled=True)  63.6 us
    reduce_scatter x1, waiting for transfers between devices, local(): lax.psum_scatter(grad_qkv, 'fsdp', scatter_dimension=0, tiled=True)  36.9 us
    all_gather x1, waiting for transfers between devices, fetch_feedforward(): lax.all_gather(vision_up, 'fsdp', axis=0, tiled=True)  36.5 us
    all_gather x1, waiting for transfers between devices, fetch_feedforward(): lax.all_gather(text_down, 'fsdp', axis=0, tiled=True)  33.8 us
    all_gather x1, waiting for transfers between devices, fetch_feedforward(): lax.all_gather(vision_down, 'fsdp', axis=0, tiled=True)  32.8 us
  transfers between devices with their start and end apart: 18, of which 15 were waited for; matrix products, arithmetic and copies ran while one was open for 19% of the time, Pallas kernels for 0%

commit v1 on v0

--- a/solution.py
+++ b/solution.py
@@ -1,12 +1,717 @@
+import functools
+import math
+
 import jax
 import jax.numpy as jnp
 from jax import lax
+from jax.experimental import pallas as pl
+from jax.experimental.pallas import tpu as pltpu
 from jax.sharding import PartitionSpec as P
 
 HEAD_DIM = 64
-
-
+BF = jnp.bfloat16
+F32 = jnp.float32
 epsilon = 1e-06
+VMEM_LIMIT = 58 * 1024 * 1024
+
+ITEM = 256
+TEXT_AT = 208
+
+
+def cdiv(a, b):
+    return -(-a // b)
+
+
+def dot_nn(a, b):
+    return lax.dot_general(a, b, (((1,), (0,)), ((), ())), preferred_element_type=F32)
+
+
+def dot_nt(a, b):
+    return lax.dot_general(a, b, (((1,), (1,)), ((), ())), preferred_element_type=F32)
+
+
+def dot_tn(a, b):
+    return lax.dot_general(a, b, (((0,), (0,)), ((), ())), preferred_element_type=F32)
+
+
+def gelu_parts(upper):
+    half = 0.5 * (1.0 + lax.erf(upper * math.sqrt(0.5)))
+    slope = half + upper * (jnp.exp(-0.5 * upper * upper) * (1.0 / math.sqrt(2.0 * math.pi)))
+    return upper * half, slope
+
+
+def normalize(hidden):
+    center = hidden - jnp.mean(hidden, axis=-1, keepdims=True)
+    spread = jnp.mean(center * center, axis=-1, keepdims=True)
+    scale = lax.rsqrt(spread + epsilon)
+    return center * scale, scale
+
+
+def start_rows(pieces, target, me, sems):
+    block = target.shape[0] // 8
+    copies = []
+    for index, (slot, first, ref) in enumerate(pieces):
+        row = pl.multiple_of((me ^ slot) * block + first, 16)
+        copy = pltpu.make_async_copy(ref, target.at[pl.ds(row, ref.shape[0])], sems.at[index])
+        copy.start()
+        copies.append(copy)
+    return copies
+
+
+def mixed_in(tok, mask, vec, rows):
+    keep = mask[rows, :]
+    return keep * vec[0:1, :] + (1.0 - keep) * tok[rows, :].astype(F32)
+
+
+def attn_fwd_kernel(slots, info, tok, mask, vec, bias, *refs):
+    count = len(slots)
+    pieces, (n1, qkv, probs, ctx, weight, sems) = refs[:count], refs[count:]
+    me = info[0]
+    width = tok.shape[1]
+    copies = start_rows([(s, f, r) for (s, f), r in zip(slots, pieces)], weight, me, sems)
+
+    @pl.loop(0, tok.shape[0] // 64)
+    def _(step):
+        rows = pl.ds(pl.multiple_of(step * 64, 64), 64)
+        normal, _unused = normalize(mixed_in(tok, mask, vec, rows))
+        n1[rows, :] = (normal * vec[1:2, :] + vec[2:3, :]).astype(BF)
+
+    for copy in copies:
+        copy.wait()
+
+    @pl.loop(0, 3 * width // 256)
+    def _(step):
+        cols = pl.ds(pl.multiple_of(step * 256, 256), 256)
+        factor = jnp.where(step < width // 256, 0.125, 1.0).astype(F32)
+        out = dot_nn(n1[...], weight[:, cols])
+        qkv[:, cols] = ((out + bias[0:1, cols]) * factor).astype(BF)
+
+    pairs = width // 128
+    patches = info[3]
+
+    @pl.loop(0, (tok.shape[0] // ITEM) * pairs)
+    def _(step):
+        item, pair = step // pairs, step % pairs
+        rows = pl.ds(pl.multiple_of(item * ITEM, ITEM), ITEM)
+        lane = lambda part: pl.ds(pl.multiple_of(part * width + pair * 128, 128), 128)
+        q2, k2, v2 = qkv[rows, lane(0)], qkv[rows, lane(1)], qkv[rows, lane(2)]
+        low = lax.broadcasted_iota(jnp.int32, (ITEM, 128), 1) < HEAD_DIM
+        zero = jnp.zeros_like(q2)
+        both = jnp.concatenate([jnp.where(low, q2, zero), jnp.where(low, zero, q2)], axis=0)
+        scores = dot_nt(both, k2)
+        col = lax.broadcasted_iota(jnp.int32, (1, ITEM), 1)
+        valid = (col < patches) | ((col >= TEXT_AT) & (col < TEXT_AT + info[1 + item]))
+        scores = jnp.where(valid, scores, -1000000000.0)
+        expo = jnp.exp(scores - jnp.max(scores, axis=-1, keepdims=True))
+        prob = (expo * (1.0 / jnp.sum(expo, axis=-1, keepdims=True))).astype(BF)
+        probs[step] = prob
+        wide = jnp.concatenate([prob[:ITEM], prob[ITEM:]], axis=1)
+        values = jnp.concatenate([jnp.where(low, v2, zero), jnp.where(low, zero, v2)], axis=0)
+        ctx[rows, pl.ds(pl.multiple_of(pair * 128, 128), 128)] = dot_nn(wide, values).astype(BF)
+
+
+def out_proj_kernel(slots, text_rows, info, tok, mask, vec, ctx, *refs):
+    count = len(slots)
+    pieces, (h1, n2, n2t, weight, sems) = refs[:count], refs[count:]
+    copies = start_rows([(s, f, r) for (s, f), r in zip(slots, pieces)], weight, info[0], sems)
+    for copy in copies:
+        copy.wait()
+
+    @pl.loop(0, tok.shape[0] // 128)
+    def _(step):
+        rows = pl.ds(pl.multiple_of(step * 128, 128), 128)
+        attended = dot_nn(ctx[rows, :], weight[...]) + vec[5:6, :]
+        hidden = mixed_in(tok, mask, vec, rows) + attended
+        h1[rows, :] = hidden
+        normal, _unused = normalize(hidden)
+        n2[rows, :] = (normal * vec[6:7, :] + vec[7:8, :]).astype(BF)
+
+    items = tok.shape[0] // ITEM
+    text = [n2[i * ITEM + TEXT_AT : i * ITEM + ITEM, :].astype(F32)[:text_rows] for i in range(items)]
+    n2t[...] = jnp.concatenate(text, axis=0).astype(BF)
+
+
+def vision_kernel(info, n2, grad, h1, vec, up_bias, *refs):
+    ups, downs = refs[:8], refs[8:16]
+    mixed, gn2, up_keep, up_send, down_keep, down_send, bias_sums = refs[16:23]
+    up_w, down_w, left, left_t, right, act, low, acc, sems = refs[23:]
+    me = info[0]
+    width = n2.shape[1]
+    items = n2.shape[0] // ITEM
+    chunk = 2 * downs[0].shape[0]
+    copies = start_rows([(s, 0, r) for s, r in enumerate(ups)], up_w, me, sems)
+    copies += start_rows([(s, 0, r) for s, r in enumerate(downs)], down_w, me, sems.at[pl.ds(8, 8)])
+    for i in range(items):
+        left[pl.ds(i * TEXT_AT, TEXT_AT), :] = n2[pl.ds(i * ITEM, TEXT_AT), :]
+        right[pl.ds(i * TEXT_AT, TEXT_AT), :] = grad[pl.ds(i * ITEM, TEXT_AT), :]
+    turned = left[...].T
+    block = width // 8
+    for b in range(8):
+        place = pl.multiple_of((me ^ b) * block, 16)
+        left_t[pl.ds(place, block), :] = turned[b * block : (b + 1) * block]
+    acc[...] = jnp.zeros_like(acc)
+    gn2[...] = jnp.zeros_like(gn2)
+    for copy in copies:
+        copy.wait()
+
+    @pl.loop(0, 4)
+    def _(step):
+        chip = (me // 2) ^ step
+        at = pl.multiple_of(chip * chunk, chunk)
+        up_c = up_w[:, pl.ds(at, chunk)]
+        down_c = down_w[pl.ds(at, chunk), :]
+        upper = dot_nn(left[...], up_c) + up_bias[0:1, pl.ds(at, chunk)]
+        active, slope = gelu_parts(upper)
+        act[...] = active.astype(BF)
+        grad_upper = dot_nt(right[...], down_c) * slope
+        low[...] = grad_upper.astype(BF)
+        bias_sums[0:1, pl.ds(at, chunk)] = jnp.sum(low[...].astype(F32), axis=0, keepdims=True)
+        acc[...] += dot_nn(act[...], down_c)
+        gn2[...] += dot_nt(low[...], up_c)
+        grad_down = dot_tn(act[...], right[...]).astype(BF)
+        half = chunk // 2
+
+        @pl.when(me % 2 == 0)
+        def _():
+            down_keep[step] = grad_down[:half]
+            down_send[step] = grad_down[half:]
+
+        @pl.when(me % 2 == 1)
+        def _():
+            down_keep[step] = grad_down[half:]
+            down_send[step] = grad_down[:half]
+
+        grad_up = dot_nn(left_t[...], low[...]).astype(BF)
+        for b in range(4):
+            up_keep[b, :, pl.ds(at, chunk)] = grad_up[2 * b * block : (2 * b + 1) * block]
+            up_send[b, :, pl.ds(at, chunk)] = grad_up[(2 * b + 1) * block : (2 * b + 2) * block]
+
+    for i in range(items):
+        rows = pl.ds(i * TEXT_AT, TEXT_AT)
+        mixed[rows, :] = (h1[pl.ds(i * ITEM, TEXT_AT), :] + acc[rows, :] + vec[8:9, :]).astype(BF)
+
+
+def text_kernel(info, up_mine, up_other, down, up_bias, *refs):
+    ins, grads = refs[:8], refs[8:16]
+    (branch_keep, branch_send, gn2_keep, gn2_send, up_keep, up_send, grad_down, bias_sums) = refs[16:24]
+    up_w, left, right, left_t = refs[24:]
+    me = info[0]
+    block = up_mine.shape[1]
+    rows = ins[0].shape[0]
+    for s in range(4):
+        up_w[pl.ds(pl.multiple_of((me ^ (2 * s)) * block, 16), block), :] = up_mine[s]
+        up_w[pl.ds(pl.multiple_of((me ^ (2 * s + 1)) * block, 16), block), :] = up_other[s]
+    for s in range(8):
+        left[pl.ds(s * rows, rows), :] = ins[s][...]
+        right[pl.ds(s * rows, rows), :] = grads[s][...]
+    turned = left[...].T
+    for b in range(8):
+        place = pl.multiple_of((me ^ b) * block, 16)
+        left_t[pl.ds(place, block), :] = turned[b * block : (b + 1) * block]
+    upper = dot_nn(left[...], up_w[...]) + up_bias[...]
+    active, slope = gelu_parts(upper)
+    act = active.astype(BF)
+    low = (dot_nt(right[...], down[...]) * slope).astype(BF)
+    bias_sums[...] = jnp.sum(low.astype(F32), axis=0, keepdims=True)
+    gn2 = dot_nt(low, up_w[...]).astype(BF)
+    for s in range(4):
+        gn2_keep[s] = gn2[2 * s * rows : (2 * s + 1) * rows]
+        gn2_send[s] = gn2[(2 * s + 1) * rows : (2 * s + 2) * rows]
+    branch = dot_nn(act, down[...]).astype(BF)
+    for s in range(4):
+        branch_keep[s] = branch[2 * s * rows : (2 * s + 1) * rows]
+        branch_send[s] = branch[(2 * s + 1) * rows : (2 * s + 2) * rows]
+    grad_down[...] = dot_tn(act, right[...]).astype(BF)
+    grad_up = dot_nn(left_t[...], low).astype(BF)
+    for b in range(4):
+        up_keep[b] = grad_up[2 * b * block : (2 * b + 1) * block]
+        up_send[b] = grad_up[(2 * b + 1) * block : (2 * b + 2) * block]
+
+
+def attn_bwd_kernel(slots, text_rows, info, gn2v, t0, t1, t2, t3, grad, h1, vec, ctx, qkv, probs, n1, *refs):
+    count = len(slots)
+    pieces, refs = refs[:count], refs[count:]
+    a_keep, a_send, b_keep, b_send, gh1, stacked, sums, bias_sums = refs[:8]
+    weight, gn2, low, gctx, n1_t, ctx_t, sems = refs[8:]
+    me = info[0]
+    total, width = h1.shape
+    items = total // ITEM
+    copies = start_rows([(s, f, r) for (s, f), r in zip(slots, pieces)], weight, me, sems)
+    text = (
+        t0[...].astype(F32) + t1[...].astype(F32) + t2[...].astype(F32) + t3[...].astype(F32)
+    )
+    for i in range(items):
+        gn2[pl.ds(i * ITEM, TEXT_AT), :] = gn2v[pl.ds(i * TEXT_AT, TEXT_AT), :]
+        gn2[pl.ds(i * ITEM + TEXT_AT, text_rows), :] = text[i * text_rows : (i + 1) * text_rows]
+        pad = ITEM - TEXT_AT - text_rows
+        gn2[pl.ds(i * ITEM + TEXT_AT + text_rows, pad), :] = jnp.zeros((pad, width), F32)
+    sums[...] = jnp.zeros_like(sums)
+
+    @pl.loop(0, total // 64)
+    def _(step):
+        rows = pl.ds(pl.multiple_of(step * 64, 64), 64)
+        normal, scale = normalize(h1[rows, :])
+        above = gn2[rows, :]
+        inner = above * vec[6:7, :]
+        back = scale * (
+            inner
+            - jnp.mean(inner, axis=-1, keepdims=True)
+            - normal * jnp.mean(inner * normal, axis=-1, keepdims=True)
+        )
+        out = grad[rows, :].astype(F32)
+        hidden = out + back
+        gh1[rows, :] = hidden
+        low[rows, :] = hidden.astype(BF)
+        sums[0:1, :] += jnp.sum(above * normal, axis=0, keepdims=True)
+        sums[1:2, :] += jnp.sum(above, axis=0, keepdims=True)
+        sums[2:3, :] += jnp.sum(hidden.astype(BF).astype(F32), axis=0, keepdims=True)
+
+    block = width // 8
+    for source, target in ((n1, n1_t), (ctx, ctx_t)):
+        turned = source[...].T
+        for b in range(8):
+            place = pl.multiple_of((me ^ b) * block, 16)
+            target[pl.ds(place, block), :] = turned[b * block : (b + 1) * block]
+
+    for copy in copies:
+        copy.wait()
+    gctx[...] = dot_nt(low[...], weight[...]).astype(BF)
+    pairs = width // 128
+
+    @pl.loop(0, items * pairs)
+    def _(step):
+        item, pair = step // pairs, step % pairs
+        rows = pl.ds(pl.multiple_of(item * ITEM, ITEM), ITEM)
+        lane = lambda part: pl.ds(pl.multiple_of(part * width + pair * 128, 128), 128)
+        q2, k2, v2 = qkv[rows, lane(0)], qkv[rows, lane(1)], qkv[rows, lane(2)]
+        g2 = gctx[rows, pl.ds(pl.multiple_of(pair * 128, 128), 128)]
+        lower = lax.broadcasted_iota(jnp.int32, (ITEM, 128), 1) < HEAD_DIM
+        zero = jnp.zeros_like(q2)
+        split = lambda a: jnp.concatenate([jnp.where(lower, a, zero), jnp.where(lower, zero, a)], axis=0)
+        both_g = split(g2)
+        prob_b = probs[step]
+        prob = prob_b.astype(F32)
+        gprob = dot_nt(both_g, v2)
+        weighted = prob * gprob
+        gscore = (weighted - prob * jnp.sum(weighted, axis=-1, keepdims=True)).astype(BF)
+        stacked[rows, lane(2)] = dot_tn(prob_b, both_g).astype(BF)
+        stacked[rows, lane(1)] = dot_tn(gscore, split(q2)).astype(BF)
+        wide = jnp.concatenate([gscore[:ITEM], gscore[ITEM:]], axis=1)
+        gquery = dot_nn(wide, split(k2)).astype(BF).astype(F32) * 0.125
+        stacked[rows, lane(0)] = gquery.astype(BF)
+
+    def put(keep, send, value, cols):
+        for b in range(4):
+            keep[b, :, cols] = value[2 * b * block : (2 * b + 1) * block]
+            send[b, :, cols] = value[(2 * b + 1) * block : (2 * b + 2) * block]
+
+    for part in range(2):
+        cols = pl.ds(part * width, width)
+        put(a_keep, a_send, dot_nn(n1_t[...], stacked[:, cols]).astype(BF), cols)
+    first = pl.ds(0, width)
+    put(b_keep, b_send, dot_nn(n1_t[...], stacked[:, 2 * width : 3 * width]).astype(BF), first)
+    put(b_keep, b_send, dot_nn(ctx_t[...], low[...]).astype(BF), pl.ds(width, width))
+
+    for part in range(3):
+        cols = stacked[:, part * width : (part + 1) * width].astype(F32)
+        bias_sums[0:1, part * width : (part + 1) * width] = jnp.sum(cols, axis=0, keepdims=True)
+
+
+def last_kernel(slots, info, stacked, gh1, tok, mask, vec, *refs):
+    count = len(slots)
+    pieces, (gtok, sums, weight, sems) = refs[:count], refs[count:]
+    copies = start_rows([(s, f, r) for (s, f), r in zip(slots, pieces)], weight, info[0], sems)
+    sums[...] = jnp.zeros_like(sums)
+    for copy in copies:
+        copy.wait()
+
+    @pl.loop(0, tok.shape[0] // 128)
+    def _(step):
+        rows = pl.ds(pl.multiple_of(step * 128, 128), 128)
+        above = dot_nt(stacked[rows, :], weight[...])
+        normal, scale = normalize(mixed_in(tok, mask, vec, rows))
+        inner = above * vec[1:2, :]
+        back = scale * (
+            inner
+            - jnp.mean(inner, axis=-1, keepdims=True)
+            - normal * jnp.mean(inner * normal, axis=-1, keepdims=True)
+        )
+        hidden = gh1[rows, :] + back
+        keep = mask[rows, :]
+        gtok[rows, :] = hidden * (1.0 - keep)
+        sums[0:1, :] += jnp.sum(hidden * keep, axis=0, keepdims=True)
+        sums[1:2, :] += jnp.sum(above * normal, axis=0, keepdims=True)
+        sums[2:3, :] += jnp.sum(above, axis=0, keepdims=True)
+
+
+def call(kernel, outs, scratch, args, pieces=(), flops=0, moved=0):
+    spec = lambda a: pl.BlockSpec(memory_space=pltpu.VMEM)
+    in_specs = [pl.BlockSpec(memory_space=pltpu.SMEM)] + [spec(a) for a in args[1:]]
+    in_specs += [pl.BlockSpec(memory_space=pl.ANY)] * len(pieces)
+    return pl.pallas_call(
+        kernel,
+        out_shape=[jax.ShapeDtypeStruct(s, d) for s, d in outs],
+        in_specs=in_specs,
+        out_specs=[pl.BlockSpec(memory_space=pltpu.VMEM)] * len(outs),
+        scratch_shapes=scratch,
+        compiler_params=pltpu.CompilerParams(vmem_limit_bytes=VMEM_LIMIT),
+        cost_estimate=pl.CostEstimate(flops=flops, bytes_accessed=moved, transcendentals=0),
+    )(*args, *pieces)
+
+
+def swap(array, mask, count=8):
+    return lax.ppermute(array, "fsdp", [(i, i ^ mask) for i in range(count)])
+
+
+def swap_rep(array, mask, count):
+    return lax.ppermute(array, "rep", [(i, i ^ mask) for i in range(count)])
+
+
+def gather(own, order):
+    x, y = swap(own, 2), swap(own, 4)
+    if order == "xy":
+        far = [(6, 0, swap(x, 4))]
+    elif order == "yx":
+        far = [(6, 0, swap(y, 2))]
+    else:
+        half = own.shape[0] // 2
+        far = [(6, 0, swap(x[:half], 4)), (6, half, swap(y[half:], 2))]
+    here = [(0, 0, own), (2, 0, x), (4, 0, y)] + far
+    return here + [(slot + 1, first, swap(a, 1)) for slot, first, a in here]
+
+
+def add(*terms):
+    out = terms[0].astype(F32)
+    for term in terms[1:]:
+        out = out + term.astype(F32)
+    return out.astype(BF)
+
+
+def scatter(keep, send, order):
+    got = swap(send, 1)
+    one, two = (2, 4) if order == "xy" else (4, 2)
+    i, j = one // 2, two // 2
+    there = swap(add(jnp.stack([keep[i], keep[3]]), jnp.stack([got[i], got[3]])), one)
+    far = swap(add(keep[j], got[j], there[1]), two)
+    return add(keep[0], got[0], there[0], far)
+
+
+def planned(
+    rep_count,
+    tokens,
+    out_grad,
+    masked,
+    lengths,
+    mask_vec,
+    norm1_gain,
+    norm1_shift,
+    w_qkv,
+    query_bias,
+    value_bias,
+    w_out,
+    out_bias,
+    norm2_gain,
+    norm2_shift,
+    vision_up,
+    vision_up_bias,
+    vision_down,
+    vision_down_bias,
+    text_up,
+    text_up_bias,
+    text_down,
+    text_down_bias,
+):
+    items, row_count, width = tokens.shape
+    text_rows = masked.shape[1]
+    patches = row_count - text_rows
+    block = width // 8
+    hidden_block = vision_down.shape[0]
+    hidden = 8 * hidden_block
+    total = items * ITEM
+    me = lax.axis_index("fsdp").astype(jnp.int32)
+    rep = lax.axis_index("rep").astype(jnp.int32)
+    core = me % 2
+    chip = me // 2
+
+    def padded(array):
+        z = lambda n: jnp.zeros((items, n, width), BF)
+        parts = [array[:, :patches], z(TEXT_AT - patches), array[:, patches:], z(ITEM - TEXT_AT - text_rows)]
+        return jnp.concatenate(parts, axis=1).reshape(total, width)
+
+    tok = padded(tokens)
+    grad = padded(out_grad)
+    mask = jnp.concatenate(
+        [
+            jnp.zeros((items, TEXT_AT), F32),
+            masked.astype(F32),
+            jnp.zeros((items, ITEM - TEXT_AT - text_rows), F32),
+        ],
+        axis=1,
+    ).reshape(total, 1)
+    info = jnp.concatenate([me[None], lengths, jnp.full((1,), patches, jnp.int32)])
+
+    names = (
+        mask_vec,
+        norm1_gain,
+        norm1_shift,
+        query_bias,
+        value_bias,
+        out_bias,
+        norm2_gain,
+        norm2_shift,
+        vision_down_bias,
+        text_down_bias,
+    )
+    own_vec = jnp.concatenate([jnp.stack(names), vision_up_bias.reshape(-1, block)], axis=0)
+    own_vec = jnp.pad(own_vec, ((0, 16 - own_vec.shape[0]), (0, 128 - block)))
+    vec_slots = jnp.stack([own_vec] + [swap(own_vec, m) for m in range(1, 8)])
+    vec8 = jnp.take(vec_slots, me ^ jnp.arange(8, dtype=jnp.int32), axis=0)[:, :, :block]
+    vec8 = vec8.astype(F32)
+    vec = vec8.transpose(1, 0, 2).reshape(16, width)
+    up_bias = vec8[:, 10 : 10 + hidden_block // block].reshape(1, hidden)
+    qkv_bias = jnp.concatenate([vec[3:4], jnp.zeros((1, width), F32), vec[4:5]], axis=1)
+
+    qkv_pieces = gather(w_qkv, "split")
+    out_pieces = gather(w_out, "split")
+    up_pieces = sorted(gather(vision_up, "xy"), key=lambda p: p[0])
+    down_pieces = sorted(gather(vision_down, "yx"), key=lambda p: p[0])
+    slots_of = lambda pieces: tuple((p[0], p[1]) for p in pieces)
+    arrays_of = lambda pieces: [p[2] for p in pieces]
+
+    pair = 2 * hidden_block
+    column = lambda s: lax.dynamic_slice_in_dim(text_up, (chip ^ s) * pair, pair, axis=1)
+    strips = jnp.stack([column(0)] + [swap(column(s), 2 * s) for s in (1, 2, 3)])
+    strips = strips.reshape(4, block, 2, hidden_block)
+    take = lambda k: lax.dynamic_index_in_dim(strips, k, axis=2, keepdims=False)
+    text_up_mine, text_up_other = take(core), swap(take(1 - core), 1)
+    grad_text = out_grad[:, patches:].reshape(-1, width)
+
+    sem = lambda n: pltpu.SemaphoreType.DMA((n,))
+    n1, qkv, probs, ctx = call(
+        functools.partial(attn_fwd_kernel, slots_of(qkv_pieces)),
+        [
+            ((total, width), BF),
+            ((total, 3 * width), BF),
+            ((items * width // 128, 2 * ITEM, ITEM), BF),
+            ((total, width), BF),
+        ],
+        [pltpu.VMEM((width, 3 * width), BF), sem(len(qkv_pieces))],
+        [info, tok, mask, vec, qkv_bias],
+        arrays_of(qkv_pieces),
+        flops=2 * total * width * 3 * width * 2,
+        moved=20_000_000,
+    )
+    h1, n2, n2t = call(
+        functools.partial(out_proj_kernel, slots_of(out_pieces), text_rows),
+        [((total, width), F32), ((total, width), BF), ((items * text_rows, width), BF)],
+        [pltpu.VMEM((width, width), BF), sem(len(out_pieces))],
+        [info, tok, mask, vec, ctx],
+        arrays_of(out_pieces),
+        flops=2 * total * width * width,
+        moved=6_000_000,
+    )
+
+    text_in = [p[2] for p in sorted(gather_direct(n2t), key=lambda p: p[0])]
+    text_grad = [p[2] for p in sorted(gather_direct(grad_text), key=lambda p: p[0])]
+    slot_rows = items * text_rows
+    quad = lambda r, c: ((4, r, c), BF)
+    (branch_keep, branch_send, gn2_keep, gn2_send, tu_keep, tu_send, text_down_sum, text_bias_sum) = call(
+        text_kernel,
+        [
+            quad(slot_rows, width),
+            quad(slot_rows, width),
+            quad(slot_rows, width),
+            quad(slot_rows, width),
+            quad(block, hidden_block),
+            quad(block, hidden_block),
+            ((hidden_block, width), BF),
+            ((1, hidden_block), F32),
+        ],
+        [
+            pltpu.VMEM((width, hidden_block), BF),
+            pltpu.VMEM((8 * slot_rows, width), BF),
+            pltpu.VMEM((8 * slot_rows, width), BF),
+            pltpu.VMEM((width, 8 * slot_rows), BF),
+        ],
+        [
+            info,
+            text_up_mine,
+            text_up_other,
+            text_down,
+            text_up_bias.astype(F32).reshape(1, hidden_block),
+            *text_in,
+            *text_grad,
+        ],
+        flops=12 * 8 * slot_rows * width * hidden_block,
+        moved=8_000_000,
+    )
+    vision_rows = items * TEXT_AT
+    mixed_v, gn2_v, vu_keep, vu_send, vd_keep, vd_send, vu_bias_sum = call(
+        vision_kernel,
+        [
+            ((vision_rows, width), BF),
+            ((vision_rows, width), F32),
+            quad(block, hidden),
+            quad(block, hidden),
+            quad(hidden_block, width),
+            quad(hidden_block, width),
+            ((1, hidden), F32),
+        ],
+        [
+            pltpu.VMEM((width, hidden), BF),
+            pltpu.VMEM((hidden, width), BF),
+            pltpu.VMEM((vision_rows, width), BF),
+            pltpu.VMEM((width, vision_rows), BF),
+            pltpu.VMEM((vision_rows, width), BF),
+            pltpu.VMEM((vision_rows, pair), BF),
+            pltpu.VMEM((vision_rows, pair), BF),
+            pltpu.VMEM((vision_rows, width), F32),
+            sem(16),
+        ],
+        [info, n2, grad, h1, vec, up_bias],
+        [p[2] for p in up_pieces + down_pieces],
+        flops=12 * vision_rows * width * hidden,
+        moved=25_000_000,
+    )
+
+    def scatter_direct(keep, send):
+        own = add(keep, swap(send, 1))
+        return [own[0]] + [swap(own[s], 2 * s) for s in (1, 2, 3)]
+
+    gn2_text = scatter_direct(gn2_keep, gn2_send)
+    a_keep, a_send, b_keep, b_send, gh1, stacked, sums_two, qkv_sums = call(
+        functools.partial(attn_bwd_kernel, slots_of(out_pieces), text_rows),
+        [
+            quad(block, 2 * width),
+            quad(block, 2 * width),
+            quad(block, 2 * width),
+            quad(block, 2 * width),
+            ((total, width), F32),
+            ((total, 3 * width), BF),
+            ((8, width), F32),
+            ((1, 3 * width), F32),
+        ],
+        [
+            pltpu.VMEM((width, width), BF),
+            pltpu.VMEM((total, width), F32),
+            pltpu.VMEM((total, width), BF),
+            pltpu.VMEM((total, width), BF),
+            pltpu.VMEM((width, total), BF),
+            pltpu.VMEM((width, total), BF),
+            sem(len(out_pieces)),
+        ],
+        [info, gn2_v, *gn2_text, grad, h1, vec, ctx, qkv, probs, n1],
+        arrays_of(out_pieces),
+        flops=2 * total * width * 5 * width + 40_000_000_00,
+        moved=30_000_000,
+    )
+    gtok, sums_one = call(
+        functools.partial(last_kernel, slots_of(qkv_pieces)),
+        [((total, width), F32), ((8, width), F32)],
+        [pltpu.VMEM((width, 3 * width), BF), sem(len(qkv_pieces))],
+        [info, stacked, gh1, tok, mask, vec],
+        arrays_of(qkv_pieces),
+        flops=2 * total * width * 3 * width,
+        moved=12_000_000,
+    )
+
+    flip = rep % 2
+
+    def rep_sum(array):
+        halves = array.reshape((2, array.shape[0] // 2) + array.shape[1:])
+        pick = lambda k: lax.dynamic_index_in_dim(halves, k, axis=0, keepdims=False)
+        part = add(pick(flip), swap_rep(pick(1 - flip), 1, rep_count))
+        part = add(part, swap_rep(part, 2, rep_count))
+        other = swap_rep(part, 1, rep_count)
+        ordered = jnp.where(flip == 0, jnp.stack([part, other]), jnp.stack([other, part]))
+        return ordered.reshape(array.shape)
+
+    tu_keep, tu_send = (
+        rep_sum(jnp.concatenate([tu_keep, tu_send], axis=0)).reshape(2, 4, block, hidden_block)
+    )
+    tu_got = swap(tu_send, 1)
+    tu_wide = jnp.where(
+        core == 0,
+        jnp.concatenate([tu_keep, tu_got], axis=-1),
+        jnp.concatenate([tu_got, tu_keep], axis=-1),
+    )
+    tu_all = jnp.stack([tu_wide[0]] + [swap(tu_wide[s], 2 * s) for s in (1, 2, 3)])
+    tu_all = jnp.take(tu_all, chip ^ jnp.arange(4, dtype=jnp.int32), axis=0)
+    grad_text_up = tu_all.transpose(1, 0, 2).reshape(block, hidden).astype(F32)
+    grad_text_down = rep_sum(text_down_sum).astype(F32)
+    grad_vision_up = rep_sum(scatter(vu_keep, vu_send, "xy")).astype(F32)
+    grad_vision_down = rep_sum(scatter(vd_keep, vd_send, "yx")).astype(F32)
+    grad_a = rep_sum(scatter(a_keep, a_send, "xy")).astype(F32)
+    grad_b = rep_sum(scatter(b_keep, b_send, "yx")).astype(F32)
+    grad_w_qkv = jnp.concatenate([grad_a, grad_b[:, :width]], axis=1)
+    grad_w_out = grad_b[:, width:]
+
+    grad_rows = out_grad.astype(F32)
+    vd_bias_sum = jnp.sum(grad_rows[:, :patches], axis=(0, 1))[None]
+    td_bias_sum = jnp.sum(grad_rows[:, patches:], axis=(0, 1))[None]
+    qs = qkv_sums.reshape(3, width)
+    flat = jnp.concatenate(
+        [
+            sums_one[0:3],
+            qs[0:1],
+            qs[2:3],
+            sums_two[2:3],
+            sums_two[0:2],
+            vd_bias_sum,
+            td_bias_sum,
+            vu_bias_sum.reshape(8, hidden_block // block, block).transpose(1, 0, 2).reshape(-1, width),
+        ],
+        axis=0,
+    )
+    for m in (1, 2, 4):
+        flat = flat + swap(flat, m)
+    mine = lax.dynamic_slice_in_dim(flat, me * block, block, axis=1)
+    mine = jnp.concatenate([mine, text_bias_sum.reshape(-1, block)], axis=0)
+    for m in (1, 2):
+        mine = mine + swap_rep(mine, m, rep_count)
+    hid = hidden_block // block
+    count = len(names)
+    vec_grad = {i: mine[i] for i in range(count)}
+    vu_bias_grad = mine[count : count + hid].reshape(-1)
+    tu_bias_grad = mine[count + hid : count + 2 * hid].reshape(-1)
+
+    mixed_v = mixed_v.reshape(items, TEXT_AT, width)[:, :patches]
+    branch = scatter_direct(branch_keep, branch_send)
+    branch = sum(b.astype(F32) for b in branch).reshape(items, text_rows, width)
+    h1_text = h1.reshape(items, ITEM, width)[:, TEXT_AT : TEXT_AT + text_rows]
+    mixed_t = (h1_text + branch + vec[9][None, None]).astype(BF)
+    mixed = jnp.concatenate([mixed_v, mixed_t], axis=1)
+    gtok = gtok.reshape(items, ITEM, width)
+    grad_tokens = jnp.concatenate(
+        [gtok[:, :patches], gtok[:, TEXT_AT : TEXT_AT + text_rows]], axis=1
+    )
+    return (
+        mixed,
+        grad_tokens,
+        vec_grad[0],
+        vec_grad[1],
+        vec_grad[2],
+        grad_w_qkv,
+        vec_grad[3],
+        vec_grad[4],
+        grad_w_out,
+        vec_grad[5],
+        vec_grad[6],
+        vec_grad[7],
+        grad_vision_up,
+        vu_bias_grad,
+        grad_vision_down,
+        vec_grad[8],
+        grad_text_up,
+        tu_bias_grad,
+        grad_text_down,
+        vec_grad[9],
+    )
+
+
+def gather_direct(own):
+    here = [(0, 0, own)] + [(m, 0, swap(own, m)) for m in (2, 4, 6)]
+    return here + [(slot + 1, first, swap(a, 1)) for slot, first, a in here]
 
 
 def layer_norm(hidden, gain, shift):
@@ -43,7 +748,7 @@
     return (grad_up, grad_up_shift, grad_down, grad_down_shift, grad_rows)
 
 
-def local(
+def general(
     tokens,
     out_grad,
     masked,
@@ -416,8 +1121,12 @@
 
 
 def solution(mesh):
+    if mesh.shape["fsdp"] == 8 and mesh.shape["rep"] == 4:
+        body = functools.partial(planned, mesh.shape["rep"])
+    else:
+        body = general
     return jax.shard_map(
-        local,
+        body,
         mesh=mesh,
         in_specs=(
             P(("fsdp", "rep"), None, None),

time: 898 us -> 434 us (0.48)
  waiting for transfers between devices: 441 us -> 158 us
  blocking collectives: 196 us -> 0 us
  matrix products: 118 us -> 0 us
  Pallas kernels: 0 us -> 99.8 us
  starting transfers between devices: 1.15 us -> 87.5 us
  local copies, waits for them, and re-layouts: 67.9 us -> 46.4 us
  between operations: 20.3 us -> 2.18 us
    reduce_scatter x12 -> x0, waiting for transfers between devices: 316 us -> none  [the longest x1 78 us: local(): lax.psum_scatter(vision_grads[2], 'fsdp', scatter_dimension=0, tiled=True)]
    ppermute x0 -> x104, waiting for transfers between devices: none -> 158 us  [the longest x84 101 us: swap(): return lax.ppermute(array, 'fsdp', [(i, i ^ mask) for i in range(count)])]
    all_gather x8 -> x0, blocking collectives: 125 us -> none  [the longest x1 20.2 us: local(): lax.all_gather(quarter[16].astype(jnp.bfloat16), 'rep', axis=0, tiled=True)]
    all_gather x6 -> x0, waiting for transfers between devices: 120 us -> none  [the longest x1 36.5 us: fetch_feedforward(): lax.all_gather(vision_up, 'fsdp', axis=0, tiled=True)]
    dot_general x24 -> x0, matrix products: 118 us -> none  [the longest x2 22.7 us: expert_backward(): jnp.einsum('rd,fd->rf', grad_b, down_matrix, preferred_element_type=jnp.f...]
    pallas_call x0 -> x6, Pallas kernels: none -> 99.8 us  [call(): pl.pallas_call(kernel, out_shape=[jax.ShapeDtypeStruct(s, d) for s, d in...]
    ppermute x0 -> x104, starting transfers between devices: none -> 87.5 us  [the longest x84 62.4 us: swap(): return lax.ppermute(array, 'fsdp', [(i, i ^ mask) for i in range(count)])]
    unnamed x4 -> x0, blocking collectives: 70.2 us -> none
  transfers between devices with their start and end apart: 18 -> 104, of which waited for: 15 -> 35; matrix products, arithmetic and copies ran while one was open for 19% -> 18% of each run, Pallas kernels for 0% -> 23%
where the time goes in v1:
time: 434 us; the launch traced here: 432 us
  waiting for transfers between devices  158 us (36%)
  Pallas kernels  99.8 us (23%)
  starting transfers between devices  87.5 us (20%)
  local copies, waits for them, and re-layouts  46.4 us (11%)
  other arithmetic  37.7 us (9%)
    ppermute x84, waiting for transfers between devices, swap(): return lax.ppermute(array, 'fsdp', [(i, i ^ mask) for i in range(count)])  101 us
    pallas_call x6, Pallas kernels, call(): pl.pallas_call(kernel, out_shape=[jax.ShapeDtypeStruct(s, d) for s, d in...  99.8 us
    ppermute x84, starting transfers between devices, swap(): return lax.ppermute(array, 'fsdp', [(i, i ^ mask) for i in range(count)])  62.4 us
    ppermute x20, waiting for transfers between devices, swap_rep(): return lax.ppermute(array, 'rep', [(i, i ^ mask) for i in range(count)])  56.7 us
    ppermute x20, starting transfers between devices, swap_rep(): return lax.ppermute(array, 'rep', [(i, i ^ mask) for i in range(count)])  25.2 us
    convert_element_type x26, other arithmetic, add(): return out.astype(BF)  10.9 us
    unnamed x155, local copies, waits for them, and re-layouts  9.21 us
  transfers between devices with their start and end apart: 104, of which 35 were waited for; matrix products, arithmetic and copies ran while one was open for 18% of the time, Pallas kernels for 23%

profile of v1, /device:TPU:0, one launch (start us, length us, event | category | flops | bytes accessed | tf_op | source)
XLA Modules:
  0.0 431.8 jit_solution(3347095797273137756)
XLA Ops:
  1.4 1.5 concatenate.46
  3.4 2.6 collective-permute-start.1
  6.1 1.8 collective-permute-start.3
  11.6 5.2 %maximum_maximum_fusion.1 = (bf16[2,256,768]{2,0,1:T(2,128)(2,1)S(1)}, bf16[2,256,768]{2,0,1:T(2,128)(2,1)S(1)}) fusion(bf16[2,40,768]{2,0,1:T(2,128)(2,1)S(1)} %slice.280, bf16[2,197,768]{2,0,1:T(2,128)(2,1)S(1)} %slice-done, bf16[256]{0:T(256)(128)(2,1)S(1)} %pad.68.clone, bf16[256]{0:T(256)(128)(2,1)S(1)} %pad.66.clone, ...), kind=kLoop, calls=%fused_computation.19 | loop fusion | flops 2359296 | bytes 3030016 | tf_op jit(solution)/shard_map/concatenate | solution.py:439
  18.0 1.6 convert_element_type.407
  22.0 2.6 collective-permute-start.5
  24.8 1.6 collective-permute-start.7
  26.4 1.5 collective-permute-start.8
  28.9 1.6 collective-permute-start.16
  30.5 10.1 %collective-permute-done.51.refs_10_ = bf16[80,768]{1,0:T(8,128)(2,1)S(1)} collective-permute-done((bf16[80,768]{1,0:T(8,128)(2,1)}, bf16[80,768]{1,0:T(8,128)(2,1)S(1)}, u32[]{:S(2)}, u32[]{:S(2)}) %collective-permute-start.51) | collective-permute-done | bytes 122912 | tf_op jit(solution)/shard_map/ppermute | solution.py:363
  40.6 1.7 collective-permute-start.17
  44.3 4.1 collective-permute-done.55.refs_14_
  50.4 1.5 collective-permute-start.41
  52.8 1.6 slice.361
  54.4 1.5 slice.362
  59.8 1.6 stack.212
  61.4 1.6 stack.213
  65.1 1.6 collective-permute-start.9
  69.9 3.0 collective-permute-done.9.refs_3_
  78.2 17.4 %shard_map.365 = (bf16[512,768]{1,0:T(8,128)(2,1)}, bf16[512,2304]{1,0:T(8,128)(2,1)}, bf16[12,512,256]{2,1,0:T(8,128)(2,1)}, bf16[512,768]{1,0:T(8,128)(2,1)}) custom-call(s32[4]{0:T(128)} %pad_add_fusion.info, bf16[512,768]{1,0:T(8,128)(2,1)} %bitcast.195, f32[512,1]{1,0:T(8,128)} %bitcast.198, f32[16,768]{1,0:T(8,128)} %reshape.269.vec, ...), custom_call_target="tpu_custom_call" | custom-call | flops 3623878656 | bytes 20000000 | tf_op jit(solution)/shard_map/pallas_call | solution.py:351
  96.5 6.3 %shard_map.366 = (f32[512,768]{1,0:T(8,128)}, bf16[512,768]{1,0:T(8,128)(2,1)}, bf16[80,768]{1,0:T(8,128)(2,1)}) custom-call(s32[4]{0:T(128)} %pad_add_fusion.info, bf16[512,768]{1,0:T(8,128)(2,1)} %bitcast.196, f32[512,1]{1,0:T(8,128)} %bitcast.199, f32[16,768]{1,0:T(8,128)} %reshape.269.vec, bf16[512,768]{1,0:T(8,128)(2,1)} %get-tuple-element.52.ctx, ...), custom_call_target="tpu_custom_call" | custom-call | flops 603979776 | bytes 6000000 | tf_op jit(solution)/shard_map/pallas_call | solution.py:351
  102.8 1.6 collective-permute-start.44
  106.8 2.0 collective-permute-done.44.refs_2_
  108.8 3.7 collective-permute-done.46.refs_4_
  117.2 6.2 %shard_map.368 = (bf16[4,80,768]{2,1,0:T(8,128)(2,1)}, bf16[4,80,768]{2,1,0:T(8,128)(2,1)}, bf16[4,80,768]{2,1,0:T(8,128)(2,1)}, bf16[4,80,768]{2,1,0:T(8,128)(2...) custom-call(s32[4]{0:T(128)} %pad_add_fusion.info, ...), custom_call_target="tpu_custom_call" | custom-call | flops 2264924160 | bytes 8000000 | tf_op jit(solution)/shard_map/pallas_call | solution.py:351
  124.6 1.6 collective-permute-start.94
  129.8 3.4 collective-permute-done.94
  133.2 1.6 collective-permute-start.101
  138.5 1.7 slice.365
  141.2 1.6 collective-permute-start.33
  145.1 2.7 collective-permute-start.95
  147.8 9.8 %collective-permute-done.33.refs_10_ = bf16[384,768]{1,0:T(8,128)(2,1)S(1)} collective-permute-done((bf16[384,768]{1,0:T(8,128)(2,1)}, bf16[384,768]{1,0:T(8,128)(2,1)S(1)}, u32[]{:S(2)}, u32[]{:S(2)}) %collective-permute-start.33) | collective-permute-done | bytes 589856 | tf_op jit(solution)/shard_map/ppermute | solution.py:363
  157.6 2.6 collective-permute-start.102
  161.6 1.6 collective-permute-start.59
  163.2 7.0 %collective-permute-done.37.refs_14_ = bf16[384,768]{1,0:T(8,128)(2,1)S(1)} collective-permute-done((bf16[384,768]{1,0:T(8,128)(2,1)}, bf16[384,768]{1,0:T(8,128)(2,1)S(1)}, u32[]{:S(2)}, u32[]{:S(2)}) %collective-permute-start.37) | collective-permute-done | bytes 589856 | tf_op jit(solution)/shard_map/ppermute | solution.py:363
  170.2 1.5 collective-permute-start.58
  182.4 25.4 %shard_map.367 = (bf16[416,768]{1,0:T(8,128)(2,1)}, f32[416,768]{1,0:T(8,128)}, bf16[4,96,3072]{2,1,0:T(8,128)(2,1)}, bf16[4,96,3072]{2,1,0:T(8,128)(2,1)}, bf16...) custom-call(s32[4]{0:T(128)} %pad_add_fusion.info, ...), custom_call_target="tpu_custom_call" | custom-call | flops 11777605632 | bytes 25000000 | tf_op jit(solution)/shard_map/pallas_call | solution.py:351
  208.6 32.9 %shard_map.369 = (bf16[4,96,1536]{2,1,0:T(8,128)(2,1)}, bf16[4,96,1536]{2,1,0:T(8,128)(2,1)}, bf16[4,96,1536]{2,1,0:T(8,128)(2,1)}, bf16[4,96,1536]{2,1,0:T(8,12...) custom-call(s32[4]{0:T(128)} %pad_add_fusion.info, ...), custom_call_target="tpu_custom_call" | custom-call | flops 7019898880 | bytes 30000000 | tf_op jit(solution)/shard_map/pallas_call | solution.py:351
  243.0 11.6 %shard_map.370 = (f32[512,768]{1,0:T(8,128)}, f32[8,768]{1,0:T(8,128)}) custom-call(s32[4]{0:T(128)} %pad_add_fusion.info, bf16[512,2304]{1,0:T(8,128)(2,1)} %get-tuple-element.65.stacked, f32[512,768]{1,0:T(8,128)} %get-tuple-element.66.gh1, bf16[512,768]{1,0:T(8,128)(2,1)} %bitcast.197, f32[512,1]{1,0:T(8,128)} %bitcast.200, f32[16,768]{1,0:T(8,128)} %reshape.269.vec, ...), custom_call_target="tpu_custom_call" | custom-call | flops 1811939328 | bytes 12000000 | tf_op jit(solution)/shard_map/pallas_call | solution.py:351
  262.5 1.7 collective-permute-start.67
  264.2 1.7 pad_maximum_fusion
  268.1 2.8 collective-permute-done.68
  270.9 2.7 collective-permute-start.69
  273.6 1.8 pad_maximum_fusion.2
  284.8 3.0 collective-permute-done.100
  287.8 2.7 collective-permute-done.99
  291.5 2.7 gather_fusion.1
  300.1 11.2 %collective-permute-done.77 = bf16[2,96,1536]{2,1,0:T(8,128)(2,1)S(1)} collective-permute-done((bf16[2,96,1536]{2,1,0:T(8,128)(2,1)S(1)}, bf16[2,96,1536]{2,1,0:T(8,128)(2,1)S(1)}, u32[]{:S(2)}, u32[]{:S(2)}) %collective-permute-start.77) | collective-permute-done | bytes 589856 | tf_op jit(solution)/shard_map/ppermute | solution.py:363
  315.6 5.5 %collective-permute-done.78 = bf16[96,1536]{1,0:T(8,128)(2,1)S(1)} collective-permute-done((bf16[96,1536]{1,0:T(8,128)(2,1)S(1)}, bf16[96,1536]{1,0:T(8,128)(2,1)S(1)}, u32[]{:S(2)}, u32[]{:S(2)}) %collective-permute-start.78) | collective-permute-done | bytes 294944 | tf_op jit(solution)/shard_map/ppermute | solution.py:363
  325.5 4.9 %collective-permute-done.79 = bf16[48,1536]{1,0:T(8,128)(2,1)S(1)} collective-permute-done((bf16[48,1536]{1,0:T(8,128)(2,1)S(1)}, bf16[48,1536]{1,0:T(8,128)(2,1)S(1)}, u32[]{:S(2)}, u32[]{:S(2)}) %collective-permute-start.79) | collective-permute-done | bytes 147488 | tf_op jit(solution)/shard_map/ppermute | solution.py:367
  332.1 2.8 collective-permute-start.74
  334.9 6.5 %collective-permute-done.80 = bf16[48,1536]{1,0:T(8,128)(2,1)S(1)} collective-permute-done((bf16[48,1536]{1,0:T(8,128)(2,1)S(1)}, bf16[48,1536]{1,0:T(8,128)(2,1)S(1)}, u32[]{:S(2)}, u32[]{:S(2)}) %collective-permute-start.80) | collective-permute-done | bytes 147488 | tf_op jit(solution)/shard_map/ppermute | solution.py:367
  347.1 1.6 collective-permute-start.89
  348.8 22.0 %collective-permute-done.83 = bf16[2,96,3072]{2,1,0:T(8,128)(2,1)S(1)} collective-permute-done((bf16[2,96,3072]{2,1,0:T(8,128)(2,1)S(1)}, bf16[2,96,3072]{2,1,0:T(8,128)(2,1)S(1)}, u32[]{:S(2)}, u32[]{:S(2)}) %collective-permute-start.83) | collective-permute-done | bytes 1179680 | tf_op jit(solution)/shard_map/ppermute | solution.py:363
  372.1 2.1 collective-permute-start.84
  375.0 10.4 %collective-permute-done.84 = bf16[96,3072]{1,0:T(8,128)(2,1)S(1)} collective-permute-done((bf16[96,3072]{1,0:T(8,128)(2,1)S(1)}, bf16[96,3072]{1,0:T(8,128)(2,1)S(1)}, u32[]{:S(2)}, u32[]{:S(2)}) %collective-permute-start.84) | collective-permute-done | bytes 589856 | tf_op jit(solution)/shard_map/ppermute | solution.py:363
  386.8 1.8 collective-permute-start.85
  389.3 9.8 %collective-permute-done.85 = bf16[48,3072]{1,0:T(8,128)(2,1)S(1)} collective-permute-done((bf16[48,3072]{1,0:T(8,128)(2,1)S(1)}, bf16[48,3072]{1,0:T(8,128)(2,1)S(1)}, u32[]{:S(2)}, u32[]{:S(2)}) %collective-permute-start.85) | collective-permute-done | bytes 294944 | tf_op jit(solution)/shard_map/ppermute | solution.py:367
  400.0 2.6 collective-permute-done.91
  402.6 1.8 collective-permute-start.92
  404.4 13.3 %collective-permute-done.86 = bf16[48,3072]{1,0:T(8,128)(2,1)S(1)} collective-permute-done((bf16[48,3072]{1,0:T(8,128)(2,1)S(1)}, bf16[48,3072]{1,0:T(8,128)(2,1)S(1)}, u32[]{:S(2)}, u32[]{:S(2)}) %collective-permute-start.86) | collective-permute-done | bytes 294944 | tf_op jit(solution)/shard_map/ppermute | solution.py:367
  418.8 2.1 collective-permute-done.92
  421.1 6.1 %collective-permute-done.87 = bf16[48,3072]{1,0:T(8,128)(2,1)S(1)} collective-permute-done((bf16[48,3072]{1,0:T(8,128)(2,1)S(1)}, bf16[48,3072]{1,0:T(8,128)(2,1)S(1)}, u32[]{:S(2)}, u32[]{:S(2)}) %collective-permute-start.87) | collective-permute-done | bytes 294944 | tf_op jit(solution)/shard_map/ppermute | solution.py:367
  428.4 1.9 collective-permute-done.93
  (456 shorter events, 114.0 us)
Async XLA Ops:
  2.9 19.1 %collective-permute-start = (bf16[16,128]{1,0:T(8,128)(2,1)S(1)}, bf16[16,128]{1,0:T(8,128)(2,1)S(1)}, u32[]{:S(2)}, u32[]{:S(2)}) collective-permute-start(bf16[16,128]{1,0:T(8,128)(2,1)S(1)} %pad.4), channel_id=1, source_target_pairs={{0,4},{4,0},{8,12},{12,8},{16,20},{20,16},{24,28},{28,24},{1,5},{5... | collective-permute-start | bytes 12296 | tf_op jit(solution)/shard_map/ppermute | solution.py:363
  3.4 21.2 %collective-permute-start.1 = (bf16[16,128]{1,0:T(8,128)(2,1)S(1)}, bf16[16,128]{1,0:T(8,128)(2,1)S(1)}, u32[]{:S(2)}, u32[]{:S(2)}) collective-permute-start(bf16[16,128]{1,0:T(8,128)(2,1)S(1)} %pad.4), channel_id=1, source_target_pairs={{0,8},{4,12},{8,0},{12,4},{16,24},{20,28},{24,16},{28,20},{1,9},{5... | collective-permute-start | bytes 12296 | tf_op jit(solution)/shard_map/ppermute | solution.py:363
  6.0 18.8 %collective-permute-start.2 = (bf16[16,128]{1,0:T(8,128)(2,1)S(1)}, bf16[16,128]{1,0:T(8,128)(2,1)S(1)}, u32[]{:S(2)}, u32[]{:S(2)}) collective-permute-start(bf16[16,128]{1,0:T(8,128)(2,1)S(1)} %pad.4), channel_id=1, source_target_pairs={{0,12},{4,8},{8,4},{12,0},{16,28},{20,24},{24,20},{28,16},{1,13},{... | collective-permute-start | bytes 12296 | tf_op jit(solution)/shard_map/ppermute | solution.py:363
  6.1 20.4 %collective-permute-start.3 = (bf16[16,128]{1,0:T(8,128)(2,1)S(1)}, bf16[16,128]{1,0:T(8,128)(2,1)S(1)}, u32[]{:S(2)}, u32[]{:S(2)}) collective-permute-start(bf16[16,128]{1,0:T(8,128)(2,1)S(1)} %pad.4), channel_id=1, source_target_pairs={{0,16},{4,20},{8,24},{12,28},{16,0},{20,4},{24,8},{28,12},{1,17},{... | collective-permute-start | bytes 12296 | tf_op jit(solution)/shard_map/ppermute | solution.py:363
  7.8 20.1 %collective-permute-start.4 = (bf16[16,128]{1,0:T(8,128)(2,1)S(1)}, bf16[16,128]{1,0:T(8,128)(2,1)S(1)}, u32[]{:S(2)}, u32[]{:S(2)}) collective-permute-start(bf16[16,128]{1,0:T(8,128)(2,1)S(1)} %pad.4), channel_id=1, source_target_pairs={{0,20},{4,16},{8,28},{12,24},{16,4},{20,0},{24,12},{28,8},{1,21},{... | collective-permute-start | bytes 12296 | tf_op jit(solution)/shard_map/ppermute | solution.py:363
  24.8 33.1 %collective-permute-start.7 = (bf16[96,2304]{1,0:T(8,128)(2,1)}, bf16[96,2304]{1,0:T(8,128)(2,1)S(1)}, u32[]{:S(2)}, u32[]{:S(2)}) collective-permute-start(bf16[96,2304]{1,0:T(8,128)(2,1)} %refs_0_.9), channel_id=1, source_target_pairs={{0,8},{4,12},{8,0},{12,4},{16,24},{20,28},{24,16},{28,20},{1,9},{5... | collective-permute-start | bytes 1327112 | tf_op jit(solution)/shard_map/ppermute | solution.py:363
  26.4 31.5 %collective-permute-start.8 = (bf16[96,2304]{1,0:T(8,128)(2,1)}, bf16[96,2304]{1,0:T(8,128)(2,1)}, u32[]{:S(2)}, u32[]{:S(2)}) collective-permute-start(bf16[96,2304]{1,0:T(8,128)(2,1)} %refs_0_.9), channel_id=1, source_target_pairs={{0,16},{4,20},{8,24},{12,28},{16,0},{20,4},{24,8},{28,12},{1,17},{... | collective-permute-start | bytes 1327112 | tf_op jit(solution)/shard_map/ppermute | solution.py:363
  28.0 12.7 %collective-permute-start.51 = (bf16[80,768]{1,0:T(8,128)(2,1)}, bf16[80,768]{1,0:T(8,128)(2,1)S(1)}, u32[]{:S(2)}, u32[]{:S(2)}) collective-permute-start(bf16[80,768]{1,0:T(8,128)(2,1)} %bitcast.235), channel_id=1, source_target_pairs={{0,8},{4,12},{8,0},{12,4},{16,24},{20,28},{24,16},{28,20},{1,9},{5... | collective-permute-start | bytes 368648 | tf_op jit(solution)/shard_map/ppermute | solution.py:363
  28.5 13.8 %collective-permute-start.53 = (bf16[80,768]{1,0:T(8,128)(2,1)}, bf16[80,768]{1,0:T(8,128)(2,1)}, u32[]{:S(2)}, u32[]{:S(2)}) collective-permute-start(bf16[80,768]{1,0:T(8,128)(2,1)} %bitcast.236), channel_id=1, source_target_pairs={{0,16},{4,20},{8,24},{12,28},{16,0},{20,4},{24,8},{28,12},{1,17},{... | collective-permute-start | bytes 368648 | tf_op jit(solution)/shard_map/ppermute | solution.py:363
  28.9 21.0 %collective-permute-start.16 = (bf16[96,768]{1,0:T(8,128)(2,1)}, bf16[96,768]{1,0:T(8,128)(2,1)}, u32[]{:S(2)}, u32[]{:S(2)}) collective-permute-start(bf16[96,768]{1,0:T(8,128)(2,1)} %refs_0_.8), channel_id=1, source_target_pairs={{0,8},{4,12},{8,0},{12,4},{16,24},{20,28},{24,16},{28,20},{1,9},{5... | collective-permute-start | bytes 442376 | tf_op jit(solution)/shard_map/ppermute | solution.py:363
  40.6 9.7 %collective-permute-start.17 = (bf16[96,768]{1,0:T(8,128)(2,1)}, bf16[96,768]{1,0:T(8,128)(2,1)}, u32[]{:S(2)}, u32[]{:S(2)}) collective-permute-start(bf16[96,768]{1,0:T(8,128)(2,1)} %refs_0_.8), channel_id=1, source_target_pairs={{0,16},{4,20},{8,24},{12,28},{16,0},{20,4},{24,8},{28,12},{1,17},{... | collective-permute-start | bytes 442376 | tf_op jit(solution)/shard_map/ppermute | solution.py:363
  55.9 9.1 %collective-permute-start.20 = (bf16[96,768]{1,0:T(8,128)(2,1)}, bf16[96,768]{1,0:T(8,128)(2,1)}, u32[]{:S(2)}, u32[]{:S(2)}) collective-permute-start(bf16[96,768]{1,0:T(8,128)(2,1)} %refs_0_.8), channel_id=1, source_target_pairs={{0,4},{4,0},{8,12},{12,8},{16,20},{20,16},{24,28},{28,24},{1,5},{5... | collective-permute-start | bytes 442376 | tf_op jit(solution)/shard_map/ppermute | solution.py:363
  56.9 9.8 %collective-permute-start.19 = (bf16[48,768]{1,0:T(8,128)(2,1)}, bf16[48,768]{1,0:T(8,128)(2,1)S(1)}, u32[]{:S(2)}, u32[]{:S(2)}) collective-permute-start(bf16[48,768]{1,0:T(8,128)(2,1)} %slice.362), channel_id=1, source_target_pairs={{0,8},{4,12},{8,0},{12,4},{16,24},{20,28},{24,16},{28,20},{1,9},{5... | collective-permute-start | bytes 221192 | tf_op jit(solution)/shard_map/ppermute | solution.py:363
  57.9 10.2 %collective-permute-start.21 = (bf16[96,768]{1,0:T(8,128)(2,1)}, bf16[96,768]{1,0:T(8,128)(2,1)}, u32[]{:S(2)}, u32[]{:S(2)}) collective-permute-start(bf16[96,768]{1,0:T(8,128)(2,1)} %collective-permute-done.16.refs_1_), channel_id=1, source_target_pairs={{0,4},{4,0},{8,12},{12,8},{16,20},{20,16},{24,28},{28,24},{1,5},{5... | collective-permute-start | bytes 442376 | tf_op jit(solution)/shard_map/ppermute | solution.py:363
  58.0 10.2 %collective-permute-start.22 = (bf16[96,768]{1,0:T(8,128)(2,1)}, bf16[96,768]{1,0:T(8,128)(2,1)}, u32[]{:S(2)}, u32[]{:S(2)}) collective-permute-start(bf16[96,768]{1,0:T(8,128)(2,1)} %collective-permute-done.17.refs_2_), channel_id=1, source_target_pairs={{0,4},{4,0},{8,12},{12,8},{16,20},{20,16},{24,28},{28,24},{1,5},{5... | collective-permute-start | bytes 442376 | tf_op jit(solution)/shard_map/ppermute | solution.py:363
  65.0 10.7 %collective-permute-start.11 = (bf16[96,2304]{1,0:T(8,128)(2,1)}, bf16[96,2304]{1,0:T(8,128)(2,1)S(1)}, u32[]{:S(2)}, u32[]{:S(2)}) collective-permute-start(bf16[96,2304]{1,0:T(8,128)(2,1)} %refs_0_.9), channel_id=1, source_target_pairs={{0,4},{4,0},{8,12},{12,8},{16,20},{20,16},{24,28},{28,24},{1,5},{5... | collective-permute-start | bytes 1327112 | tf_op jit(solution)/shard_map/ppermute | solution.py:363
  75.7 27.1 %collective-permute-start.50 = (bf16[80,768]{1,0:T(8,128)(2,1)S(1)}, bf16[80,768]{1,0:T(8,128)(2,1)S(1)}, u32[]{:S(2)}, u32[]{:S(2)}) collective-permute-start(bf16[80,768]{1,0:T(8,128)(2,1)S(1)} %bitcast.239), channel_id=1, source_target_pairs={{0,4},{4,0},{8,12},{12,8},{16,20},{20,16},{24,28},{28,24},{1,5},{5... | collective-permute-start | bytes 368648 | tf_op jit(solution)/shard_map/ppermute | solution.py:363
  76.3 28.1 %collective-permute-start.52 = (bf16[80,768]{1,0:T(8,128)(2,1)S(1)}, bf16[80,768]{1,0:T(8,128)(2,1)S(1)}, u32[]{:S(2)}, u32[]{:S(2)}) collective-permute-start(bf16[80,768]{1,0:T(8,128)(2,1)S(1)} %copy-done.51), channel_id=1, source_target_pairs={{0,4},{4,0},{8,12},{12,8},{16,20},{20,16},{24,28},{28,24},{1,5},{5... | collective-permute-start | bytes 368648 | tf_op jit(solution)/shard_map/ppermute | solution.py:363
  76.4 28.6 %collective-permute-start.54 = (bf16[80,768]{1,0:T(8,128)(2,1)}, bf16[80,768]{1,0:T(8,128)(2,1)S(1)}, u32[]{:S(2)}, u32[]{:S(2)}) collective-permute-start(bf16[80,768]{1,0:T(8,128)(2,1)} %collective-permute-done.53.refs_12_), channel_id=1, source_target_pairs={{0,4},{4,0},{8,12},{12,8},{16,20},{20,16},{24,28},{28,24},{1,5},{5... | collective-permute-start | bytes 368648 | tf_op jit(solution)/shard_map/ppermute | solution.py:363
  76.9 18.7 %collective-permute-start.23 = (bf16[48,768]{1,0:T(8,128)(2,1)}, bf16[48,768]{1,0:T(8,128)(2,1)S(1)}, u32[]{:S(2)}, u32[]{:S(2)}) collective-permute-start(bf16[48,768]{1,0:T(8,128)(2,1)} %collective-permute-done.18.refs_3_), channel_id=1, source_target_pairs={{0,4},{4,0},{8,12},{12,8},{16,20},{20,16},{24,28},{28,24},{1,5},{5... | collective-permute-start | bytes 221192 | tf_op jit(solution)/shard_map/ppermute | solution.py:363
  77.6 18.3 %collective-permute-start.24 = (bf16[48,768]{1,0:T(8,128)(2,1)S(1)}, bf16[48,768]{1,0:T(8,128)(2,1)S(1)}, u32[]{:S(2)}, u32[]{:S(2)}) collective-permute-start(bf16[48,768]{1,0:T(8,128)(2,1)S(1)} %collective-permute-done.19.refs_4_), channel_id=1, source_target_pairs={{0,4},{4,0},{8,12},{12,8},{16,20},{20,16},{24,28},{28,24},{1,5},{5... | collective-permute-start | bytes 221192 | tf_op jit(solution)/shard_map/ppermute | solution.py:363
  95.6 11.1 %collective-permute-start.56 = (bf16[80,768]{1,0:T(8,128)(2,1)S(1)}, bf16[80,768]{1,0:T(8,128)(2,1)S(1)}, u32[]{:S(2)}, u32[]{:S(2)}) collective-permute-start(bf16[80,768]{1,0:T(8,128)(2,1)S(1)} %copy-done.53), channel_id=1, source_target_pairs={{0,4},{4,0},{8,12},{12,8},{16,20},{20,16},{24,28},{28,24},{1,5},{5... | collective-permute-start | bytes 368648 | tf_op jit(solution)/shard_map/ppermute | solution.py:363
  95.8 18.0 %collective-permute-start.42 = (bf16[4,96,384]{2,1,0:T(8,128)(2,1)S(1)}, bf16[4,96,384]{2,1,0:T(8,128)(2,1)S(1)}, u32[]{:S(2)}, u32[]{:S(2)}) collective-permute-start(bf16[4,96,384]{2,1,0:T(8,128)(2,1)S(1)} %bitcast.226), channel_id=1, source_target_pairs={{0,4},{4,0},{8,12},{12,8},{16,20},{20,16},{24,28},{28,24},{1,5},{5... | collective-permute-start | bytes 884744 | tf_op jit(solution)/shard_map/ppermute | solution.py:363
  113.9 13.8 %collective-permute-start.25 = (bf16[96,3072]{1,0:T(8,128)(2,1)}, bf16[96,3072]{1,0:T(8,128)(2,1)S(1)}, u32[]{:S(2)}, u32[]{:S(2)}) collective-permute-start(bf16[96,3072]{1,0:T(8,128)(2,1)} %refs_0_.7), channel_id=1, source_target_pairs={{0,4},{4,0},{8,12},{12,8},{16,20},{20,16},{24,28},{28,24},{1,5},{5... | collective-permute-start | bytes 1769480 | tf_op jit(solution)/shard_map/ppermute | solution.py:363
  113.9 15.9 %collective-permute-start.26 = (bf16[96,3072]{1,0:T(8,128)(2,1)}, bf16[96,3072]{1,0:T(8,128)(2,1)S(1)}, u32[]{:S(2)}, u32[]{:S(2)}) collective-permute-start(bf16[96,3072]{1,0:T(8,128)(2,1)} %refs_0_.7), channel_id=1, source_target_pairs={{0,8},{4,12},{8,0},{12,4},{16,24},{20,28},{24,16},{28,20},{1,9},{5... | collective-permute-start | bytes 1769480 | tf_op jit(solution)/shard_map/ppermute | solution.py:363
  114.5 26.5 %collective-permute-start.28 = (bf16[96,3072]{1,0:T(8,128)(2,1)}, bf16[96,3072]{1,0:T(8,128)(2,1)}, u32[]{:S(2)}, u32[]{:S(2)}) collective-permute-start(bf16[96,3072]{1,0:T(8,128)(2,1)} %refs_0_.7), channel_id=1, source_target_pairs={{0,16},{4,20},{8,24},{12,28},{16,0},{20,4},{24,8},{28,12},{1,17},{... | collective-permute-start | bytes 1769480 | tf_op jit(solution)/shard_map/ppermute | solution.py:363
  115.6 27.3 %collective-permute-start.35 = (bf16[384,768]{1,0:T(8,128)(2,1)}, bf16[384,768]{1,0:T(8,128)(2,1)}, u32[]{:S(2)}, u32[]{:S(2)}) collective-permute-start(bf16[384,768]{1,0:T(8,128)(2,1)} %refs_8_.1), channel_id=1, source_target_pairs={{0,16},{4,20},{8,24},{12,28},{16,0},{20,4},{24,8},{28,12},{1,17},{... | collective-permute-start | bytes 1769480 | tf_op jit(solution)/shard_map/ppermute | solution.py:363
  124.6 8.6 %collective-permute-start.94 = (bf16[4,96,384]{2,1,0:T(8,128)(2,1)S(1)}, bf16[4,96,384]{2,1,0:T(8,128)(2,1)S(1)}, u32[]{:S(2)}, u32[]{:S(2)}) collective-permute-start(bf16[4,96,384]{2,1,0:T(8,128)(2,1)S(1)} %dynamic-slice_bitcast_fusion.1), channel_id=1, source_target_pairs={{0,1},{1,0},{2,3},{3,2},{4,5},{5,4},{6,7},{7,6},{8,9},{9,8},{10,11... | collective-permute-start | bytes 884744 | tf_op jit(solution)/shard_map/ppermute | solution.py:367
  128.4 14.6 %collective-permute-start.57 = (bf16[4,80,768]{2,1,0:T(8,128)(2,1)}, bf16[4,80,768]{2,1,0:T(8,128)(2,1)S(1)}, u32[]{:S(2)}, u32[]{:S(2)}) collective-permute-start(bf16[4,80,768]{2,1,0:T(8,128)(2,1)} %get-tuple-element.58), channel_id=1, source_target_pairs={{0,4},{4,0},{8,12},{12,8},{16,20},{20,16},{24,28},{28,24},{1,5},{5... | collective-permute-start | bytes 1474568 | tf_op jit(solution)/shard_map/ppermute | solution.py:363
  129.8 13.8 %collective-permute-start.61 = (bf16[4,80,768]{2,1,0:T(8,128)(2,1)}, bf16[4,80,768]{2,1,0:T(8,128)(2,1)S(1)}, u32[]{:S(2)}, u32[]{:S(2)}) collective-permute-start(bf16[4,80,768]{2,1,0:T(8,128)(2,1)} %get-tuple-element.61), channel_id=1, source_target_pairs={{0,4},{4,0},{8,12},{12,8},{16,20},{20,16},{24,28},{28,24},{1,5},{5... | collective-permute-start | bytes 1474568 | tf_op jit(solution)/shard_map/ppermute | solution.py:363
  141.2 16.4 %collective-permute-start.33 = (bf16[384,768]{1,0:T(8,128)(2,1)}, bf16[384,768]{1,0:T(8,128)(2,1)S(1)}, u32[]{:S(2)}, u32[]{:S(2)}) collective-permute-start(bf16[384,768]{1,0:T(8,128)(2,1)} %refs_8_.1), channel_id=1, source_target_pairs={{0,8},{4,12},{8,0},{12,4},{16,24},{20,28},{24,16},{28,20},{1,9},{5... | collective-permute-start | bytes 1769480 | tf_op jit(solution)/shard_map/ppermute | solution.py:363
  142.9 17.3 %collective-permute-start.27 = (bf16[96,3072]{1,0:T(8,128)(2,1)S(1)}, bf16[96,3072]{1,0:T(8,128)(2,1)S(1)}, u32[]{:S(2)}, u32[]{:S(2)}) collective-permute-start(bf16[96,3072]{1,0:T(8,128)(2,1)S(1)} %copy-done.38), channel_id=1, source_target_pairs={{0,4},{4,0},{8,12},{12,8},{16,20},{20,16},{24,28},{28,24},{1,5},{5... | collective-permute-start | bytes 1769480 | tf_op jit(solution)/shard_map/ppermute | solution.py:363
  143.0 18.6 %collective-permute-start.30 = (bf16[96,3072]{1,0:T(8,128)(2,1)S(1)}, bf16[96,3072]{1,0:T(8,128)(2,1)S(1)}, u32[]{:S(2)}, u32[]{:S(2)}) collective-permute-start(bf16[96,3072]{1,0:T(8,128)(2,1)S(1)} %copy-done.38), channel_id=1, source_target_pairs={{0,16},{4,20},{8,24},{12,28},{16,0},{20,4},{24,8},{28,12},{1,17},{... | collective-permute-start | bytes 1769480 | tf_op jit(solution)/shard_map/ppermute | solution.py:363
  143.7 26.5 %collective-permute-start.37 = (bf16[384,768]{1,0:T(8,128)(2,1)}, bf16[384,768]{1,0:T(8,128)(2,1)S(1)}, u32[]{:S(2)}, u32[]{:S(2)}) collective-permute-start(bf16[384,768]{1,0:T(8,128)(2,1)} %collective-permute-done.35.refs_12_), channel_id=1, source_target_pairs={{0,8},{4,12},{8,0},{12,4},{16,24},{20,28},{24,16},{28,20},{1,9},{5... | collective-permute-start | bytes 1769480 | tf_op jit(solution)/shard_map/ppermute | solution.py:363
  145.1 27.3 %collective-permute-start.95 = (bf16[4,96,384]{2,1,0:T(8,128)(2,1)S(1)}, bf16[4,96,384]{2,1,0:T(8,128)(2,1)S(1)}, u32[]{:S(2)}, u32[]{:S(2)}) collective-permute-start(bf16[4,96,384]{2,1,0:T(8,128)(2,1)S(1)} %fusion.5), channel_id=1, source_target_pairs={{0,2},{1,3},{2,0},{3,1},{4,6},{5,7},{6,4},{7,5},{8,10},{9,11},{10,... | collective-permute-start | bytes 884744 | tf_op jit(solution)/shard_map/ppermute | solution.py:367
  157.6 16.3 %collective-permute-start.102 = (bf16[192,768]{1,0:T(8,128)(2,1)S(1)}, bf16[192,768]{1,0:T(8,128)(2,1)S(1)}, u32[]{:S(2)}, u32[]{:S(2)}) collective-permute-start(bf16[192,768]{1,0:T(8,128)(2,1)S(1)} %fusion.4), channel_id=1, source_target_pairs={{0,2},{1,3},{2,0},{3,1},{4,6},{5,7},{6,4},{7,5},{8,10},{9,11},{10,... | collective-permute-start | bytes 884744 | tf_op jit(solution)/shard_map/ppermute | solution.py:367
  160.2 13.6 %collective-permute-start.60 = (bf16[80,768]{1,0:T(8,128)(2,1)S(1)}, bf16[80,768]{1,0:T(8,128)(2,1)S(1)}, u32[]{:S(2)}, u32[]{:S(2)}) collective-permute-start(bf16[80,768]{1,0:T(8,128)(2,1)S(1)} %get-tuple-element.114), channel_id=1, source_target_pairs={{0,24},{4,28},{8,16},{12,20},{16,8},{20,12},{24,0},{28,4},{1,25},{... | collective-permute-start | bytes 368648 | tf_op jit(solution)/shard_map/ppermute | solution.py:363
  161.6 12.7 %collective-permute-start.59 = (bf16[80,768]{1,0:T(8,128)(2,1)S(1)}, bf16[80,768]{1,0:T(8,128)(2,1)S(1)}, u32[]{:S(2)}, u32[]{:S(2)}) collective-permute-start(bf16[80,768]{1,0:T(8,128)(2,1)S(1)} %get-tuple-element.115), channel_id=1, source_target_pairs={{0,16},{4,20},{8,24},{12,28},{16,0},{20,4},{24,8},{28,12},{1,17},{... | collective-permute-start | bytes 368648 | tf_op jit(solution)/shard_map/ppermute | solution.py:363
  176.8 31.0 %collective-permute-start.62 = (bf16[80,768]{1,0:T(8,128)(2,1)S(1)}, bf16[80,768]{1,0:T(8,128)(2,1)S(1)}, u32[]{:S(2)}, u32[]{:S(2)}) collective-permute-start(bf16[80,768]{1,0:T(8,128)(2,1)S(1)} %get-tuple-element.111), channel_id=1, source_target_pairs={{0,8},{4,12},{8,0},{12,4},{16,24},{20,28},{24,16},{28,20},{1,9},{5... | collective-permute-start | bytes 368648 | tf_op jit(solution)/shard_map/ppermute | solution.py:363
  177.7 30.1 %collective-permute-start.63 = (bf16[80,768]{1,0:T(8,128)(2,1)S(1)}, bf16[80,768]{1,0:T(8,128)(2,1)S(1)}, u32[]{:S(2)}, u32[]{:S(2)}) collective-permute-start(bf16[80,768]{1,0:T(8,128)(2,1)S(1)} %get-tuple-element.110), channel_id=1, source_target_pairs={{0,16},{4,20},{8,24},{12,28},{16,0},{20,4},{24,8},{28,12},{1,17},{... | collective-permute-start | bytes 368648 | tf_op jit(solution)/shard_map/ppermute | solution.py:363
  179.0 28.9 %collective-permute-start.64 = (bf16[80,768]{1,0:T(8,128)(2,1)S(1)}, bf16[80,768]{1,0:T(8,128)(2,1)S(1)}, u32[]{:S(2)}, u32[]{:S(2)}) collective-permute-start(bf16[80,768]{1,0:T(8,128)(2,1)S(1)} %get-tuple-element.109), channel_id=1, source_target_pairs={{0,24},{4,28},{8,16},{12,20},{16,8},{20,12},{24,0},{28,4},{1,25},{... | collective-permute-start | bytes 368648 | tf_op jit(solution)/shard_map/ppermute | solution.py:363
  180.3 96.6 %collective-permute-start.96 = (bf16[4,96,384]{2,1,0:T(8,128)(2,1)S(1)}, bf16[4,96,384]{2,1,0:T(8,128)(2,1)}, u32[]{:S(2)}, u32[]{:S(2)}) collective-permute-start(bf16[4,96,384]{2,1,0:T(8,128)(2,1)S(1)} %add_convert_fusion.9), channel_id=1, source_target_pairs={{0,1},{1,0},{2,3},{3,2},{4,5},{5,4},{6,7},{7,6},{8,9},{9,8},{10,11... | collective-permute-start | bytes 884744 | tf_op jit(solution)/shard_map/ppermute | solution.py:367
  181.3 97.5 %collective-permute-start.103 = (bf16[192,768]{1,0:T(8,128)(2,1)S(1)}, bf16[192,768]{1,0:T(8,128)(2,1)}, u32[]{:S(2)}, u32[]{:S(2)}) collective-permute-start(bf16[192,768]{1,0:T(8,128)(2,1)S(1)} %add_convert_fusion.8), channel_id=1, source_target_pairs={{0,1},{1,0},{2,3},{3,2},{4,5},{5,4},{6,7},{7,6},{8,9},{9,8},{10,11... | collective-permute-start | bytes 884744 | tf_op jit(solution)/shard_map/ppermute | solution.py:367
  266.5 27.7 %collective-permute-start.76 = (bf16[4,96,1536]{2,1,0:T(8,128)(2,1)}, bf16[4,96,1536]{2,1,0:T(8,128)(2,1)}, u32[]{:S(2)}, u32[]{:S(2)}) collective-permute-start(bf16[4,96,1536]{2,1,0:T(8,128)(2,1)} %get-tuple-element.76), channel_id=1, source_target_pairs={{0,4},{4,0},{8,12},{12,8},{16,20},{20,16},{24,28},{28,24},{1,5},{5... | collective-permute-start | bytes 3538952 | tf_op jit(solution)/shard_map/ppermute | solution.py:363
  266.5 30.0 %collective-permute-start.70 = (bf16[4,96,1536]{2,1,0:T(8,128)(2,1)}, bf16[4,96,1536]{2,1,0:T(8,128)(2,1)}, u32[]{:S(2)}, u32[]{:S(2)}) collective-permute-start(bf16[4,96,1536]{2,1,0:T(8,128)(2,1)} %get-tuple-element.74), channel_id=1, source_target_pairs={{0,4},{4,0},{8,12},{12,8},{16,20},{20,16},{24,28},{28,24},{1,5},{5... | collective-permute-start | bytes 3538952 | tf_op jit(solution)/shard_map/ppermute | solution.py:363
  281.5 9.1 %collective-permute-start.99 = (bf16[96,768]{1,0:T(8,128)(2,1)S(1)}, bf16[96,768]{1,0:T(8,128)(2,1)S(1)}, u32[]{:S(2)}, u32[]{:S(2)}) collective-permute-start(bf16[96,768]{1,0:T(8,128)(2,1)S(1)} %get-tuple-element.97), channel_id=1, source_target_pairs={{0,16},{4,20},{8,24},{12,28},{16,0},{20,4},{24,8},{28,12},{1,17},{... | collective-permute-start | bytes 442376 | tf_op jit(solution)/shard_map/ppermute | solution.py:363
  287.8 55.8 %collective-permute-start.82 = (bf16[4,96,3072]{2,1,0:T(8,128)(2,1)}, bf16[4,96,3072]{2,1,0:T(8,128)(2,1)}, u32[]{:S(2)}, u32[]{:S(2)}) collective-permute-start(bf16[4,96,3072]{2,1,0:T(8,128)(2,1)} %get-tuple-element.78), channel_id=1, source_target_pairs={{0,4},{4,0},{8,12},{12,8},{16,20},{20,16},{24,28},{28,24},{1,5},{5... | collective-permute-start | bytes 7077896 | tf_op jit(solution)/shard_map/ppermute | solution.py:363
  290.5 56.2 %collective-permute-start.88 = (bf16[4,384,768]{2,1,0:T(8,128)(2,1)}, bf16[4,384,768]{2,1,0:T(8,128)(2,1)S(1)}, u32[]{:S(2)}, u32[]{:S(2)}) collective-permute-start(bf16[4,384,768]{2,1,0:T(8,128)(2,1)} %get-tuple-element.80), channel_id=1, source_target_pairs={{0,4},{4,0},{8,12},{12,8},{16,20},{20,16},{24,28},{28,24},{1,5},{5... | collective-permute-start | bytes 7077896 | tf_op jit(solution)/shard_map/ppermute | solution.py:363
  295.6 15.8 %collective-permute-start.77 = (bf16[2,96,1536]{2,1,0:T(8,128)(2,1)S(1)}, bf16[2,96,1536]{2,1,0:T(8,128)(2,1)S(1)}, u32[]{:S(2)}, u32[]{:S(2)}) collective-permute-start(bf16[2,96,1536]{2,1,0:T(8,128)(2,1)S(1)} %add_convert_fusion.4), channel_id=1, source_target_pairs={{0,16},{4,20},{8,24},{12,28},{16,0},{20,4},{24,8},{28,12},{1,17},{... | collective-permute-start | bytes 1769480 | tf_op jit(solution)/shard_map/ppermute | solution.py:363
  297.8 15.5 %collective-permute-start.71 = (bf16[2,96,1536]{2,1,0:T(8,128)(2,1)S(1)}, bf16[2,96,1536]{2,1,0:T(8,128)(2,1)S(1)}, u32[]{:S(2)}, u32[]{:S(2)}) collective-permute-start(bf16[2,96,1536]{2,1,0:T(8,128)(2,1)S(1)} %add_convert_fusion.5), channel_id=1, source_target_pairs={{0,8},{4,12},{8,0},{12,4},{16,24},{20,28},{24,16},{28,20},{1,9},{5... | collective-permute-start | bytes 1769480 | tf_op jit(solution)/shard_map/ppermute | solution.py:363
  312.4 8.7 %collective-permute-start.78 = (bf16[96,1536]{1,0:T(8,128)(2,1)S(1)}, bf16[96,1536]{1,0:T(8,128)(2,1)S(1)}, u32[]{:S(2)}, u32[]{:S(2)}) collective-permute-start(bf16[96,1536]{1,0:T(8,128)(2,1)S(1)} %fusion.11), channel_id=1, source_target_pairs={{0,8},{4,12},{8,0},{12,4},{16,24},{20,28},{24,16},{28,20},{1,9},{5... | collective-permute-start | bytes 884744 | tf_op jit(solution)/shard_map/ppermute | solution.py:363
  314.4 9.0 %collective-permute-start.72 = (bf16[96,1536]{1,0:T(8,128)(2,1)S(1)}, bf16[96,1536]{1,0:T(8,128)(2,1)S(1)}, u32[]{:S(2)}, u32[]{:S(2)}) collective-permute-start(bf16[96,1536]{1,0:T(8,128)(2,1)S(1)} %fusion.10), channel_id=1, source_target_pairs={{0,16},{4,20},{8,24},{12,28},{16,0},{20,4},{24,8},{28,12},{1,17},{... | collective-permute-start | bytes 884744 | tf_op jit(solution)/shard_map/ppermute | solution.py:363
  330.5 10.9 %collective-permute-start.80 = (bf16[48,1536]{1,0:T(8,128)(2,1)S(1)}, bf16[48,1536]{1,0:T(8,128)(2,1)S(1)}, u32[]{:S(2)}, u32[]{:S(2)}) collective-permute-start(bf16[48,1536]{1,0:T(8,128)(2,1)S(1)} %fusion.12), channel_id=1, source_target_pairs={{0,2},{1,3},{2,0},{3,1},{4,6},{5,7},{6,4},{7,5},{8,10},{9,11},{10,... | collective-permute-start | bytes 442376 | tf_op jit(solution)/shard_map/ppermute | solution.py:367
  332.1 10.9 %collective-permute-start.74 = (bf16[48,1536]{1,0:T(8,128)(2,1)S(1)}, bf16[48,1536]{1,0:T(8,128)(2,1)S(1)}, u32[]{:S(2)}, u32[]{:S(2)}) collective-permute-start(bf16[48,1536]{1,0:T(8,128)(2,1)S(1)} %fusion.13), channel_id=1, source_target_pairs={{0,2},{1,3},{2,0},{3,1},{4,6},{5,7},{6,4},{7,5},{8,10},{9,11},{10,... | collective-permute-start | bytes 442376 | tf_op jit(solution)/shard_map/ppermute | solution.py:367
  345.4 25.4 %collective-permute-start.83 = (bf16[2,96,3072]{2,1,0:T(8,128)(2,1)S(1)}, bf16[2,96,3072]{2,1,0:T(8,128)(2,1)S(1)}, u32[]{:S(2)}, u32[]{:S(2)}) collective-permute-start(bf16[2,96,3072]{2,1,0:T(8,128)(2,1)S(1)} %add_convert_fusion.1), channel_id=1, source_target_pairs={{0,8},{4,12},{8,0},{12,4},{16,24},{20,28},{24,16},{28,20},{1,9},{5... | collective-permute-start | bytes 3538952 | tf_op jit(solution)/shard_map/ppermute | solution.py:363
  347.1 27.2 %collective-permute-start.89 = (bf16[2,384,768]{2,1,0:T(8,128)(2,1)S(1)}, bf16[2,384,768]{2,1,0:T(8,128)(2,1)S(1)}, u32[]{:S(2)}, u32[]{:S(2)}) collective-permute-start(bf16[2,384,768]{2,1,0:T(8,128)(2,1)S(1)} %add_convert_fusion), channel_id=1, source_target_pairs={{0,16},{4,20},{8,24},{12,28},{16,0},{20,4},{24,8},{28,12},{1,17},{... | collective-permute-start | bytes 3538952 | tf_op jit(solution)/shard_map/ppermute | solution.py:363
  372.1 13.3 %collective-permute-start.84 = (bf16[96,3072]{1,0:T(8,128)(2,1)S(1)}, bf16[96,3072]{1,0:T(8,128)(2,1)S(1)}, u32[]{:S(2)}, u32[]{:S(2)}) collective-permute-start(bf16[96,3072]{1,0:T(8,128)(2,1)S(1)} %fusion.2), channel_id=1, source_target_pairs={{0,16},{4,20},{8,24},{12,28},{16,0},{20,4},{24,8},{28,12},{1,17},{... | collective-permute-start | bytes 1769480 | tf_op jit(solution)/shard_map/ppermute | solution.py:363
  374.6 14.1 %collective-permute-start.90 = (bf16[384,768]{1,0:T(8,128)(2,1)S(1)}, bf16[384,768]{1,0:T(8,128)(2,1)S(1)}, u32[]{:S(2)}, u32[]{:S(2)}) collective-permute-start(bf16[384,768]{1,0:T(8,128)(2,1)S(1)} %fusion.3), channel_id=1, source_target_pairs={{0,8},{4,12},{8,0},{12,4},{16,24},{20,28},{24,16},{28,20},{1,9},{5... | collective-permute-start | bytes 1769480 | tf_op jit(solution)/shard_map/ppermute | solution.py:363
  386.8 12.3 %collective-permute-start.85 = (bf16[48,3072]{1,0:T(8,128)(2,1)S(1)}, bf16[48,3072]{1,0:T(8,128)(2,1)S(1)}, u32[]{:S(2)}, u32[]{:S(2)}) collective-permute-start(bf16[48,3072]{1,0:T(8,128)(2,1)S(1)} %dynamic-slice_bitcast_fusion.3), channel_id=1, source_target_pairs={{0,1},{1,0},{2,3},{3,2},{4,5},{5,4},{6,7},{7,6},{8,9},{9,8},{10,11... | collective-permute-start | bytes 884744 | tf_op jit(solution)/shard_map/ppermute | solution.py:367
  389.0 13.6 %collective-permute-start.91 = (bf16[192,768]{1,0:T(8,128)(2,1)S(1)}, bf16[192,768]{1,0:T(8,128)(2,1)S(1)}, u32[]{:S(2)}, u32[]{:S(2)}) collective-permute-start(bf16[192,768]{1,0:T(8,128)(2,1)S(1)} %dynamic-slice_bitcast_fusion.2), channel_id=1, source_target_pairs={{0,1},{1,0},{2,3},{3,2},{4,5},{5,4},{6,7},{7,6},{8,9},{9,8},{10,11... | collective-permute-start | bytes 884744 | tf_op jit(solution)/shard_map/ppermute | solution.py:367
  399.2 18.5 %collective-permute-start.86 = (bf16[48,3072]{1,0:T(8,128)(2,1)S(1)}, bf16[48,3072]{1,0:T(8,128)(2,1)S(1)}, u32[]{:S(2)}, u32[]{:S(2)}) collective-permute-start(bf16[48,3072]{1,0:T(8,128)(2,1)S(1)} %fusion.7), channel_id=1, source_target_pairs={{0,2},{1,3},{2,0},{3,1},{4,6},{5,7},{6,4},{7,5},{8,10},{9,11},{10,... | collective-permute-start | bytes 884744 | tf_op jit(solution)/shard_map/ppermute | solution.py:367
  402.6 18.3 %collective-permute-start.92 = (bf16[192,768]{1,0:T(8,128)(2,1)S(1)}, bf16[192,768]{1,0:T(8,128)(2,1)S(1)}, u32[]{:S(2)}, u32[]{:S(2)}) collective-permute-start(bf16[192,768]{1,0:T(8,128)(2,1)S(1)} %fusion.6), channel_id=1, source_target_pairs={{0,2},{1,3},{2,0},{3,1},{4,6},{5,7},{6,4},{7,5},{8,10},{9,11},{10,... | collective-permute-start | bytes 884744 | tf_op jit(solution)/shard_map/ppermute | solution.py:367
  417.8 9.4 %collective-permute-start.87 = (bf16[48,3072]{1,0:T(8,128)(2,1)S(1)}, bf16[48,3072]{1,0:T(8,128)(2,1)S(1)}, u32[]{:S(2)}, u32[]{:S(2)}) collective-permute-start(bf16[48,3072]{1,0:T(8,128)(2,1)S(1)} %add_convert_fusion.11), channel_id=1, source_target_pairs={{0,1},{1,0},{2,3},{3,2},{4,5},{5,4},{6,7},{7,6},{8,9},{9,8},{10,11... | collective-permute-start | bytes 884744 | tf_op jit(solution)/shard_map/ppermute | solution.py:367
  421.1 9.3 %collective-permute-start.93 = (bf16[192,768]{1,0:T(8,128)(2,1)S(1)}, bf16[192,768]{1,0:T(8,128)(2,1)S(1)}, u32[]{:S(2)}, u32[]{:S(2)}) collective-permute-start(bf16[192,768]{1,0:T(8,128)(2,1)S(1)} %add_convert_fusion.10), channel_id=1, source_target_pairs={{0,1},{1,0},{2,3},{3,2},{4,5},{5,4},{6,7},{7,6},{8,9},{9,8},{10,11... | collective-permute-start | bytes 884744 | tf_op jit(solution)/shard_map/ppermute | solution.py:367
  (112 other events, 661.9 us)

commit v2 on v0

--- a/solution.py
+++ b/solution.py
@@ -1,12 +1,942 @@
+import functools
+import math
+
 import jax
 import jax.numpy as jnp
 from jax import lax
+from jax.experimental import pallas as pl
+from jax.experimental.pallas import tpu as pltpu
 from jax.sharding import PartitionSpec as P
 
 HEAD_DIM = 64
-
-
+BF = jnp.bfloat16
+F32 = jnp.float32
 epsilon = 1e-06
+VMEM_LIMIT = 58 * 1024 * 1024
+
+ITEM = 256
+SCALE = 0.2
+TEXT_AT = 208
+
+
+def cdiv(a, b):
+    return -(-a // b)
+
+
+def dot_nn(a, b):
+    return lax.dot_general(a, b, (((1,), (0,)), ((), ())), preferred_element_type=F32)
+
+
+def dot_nt(a, b):
+    return lax.dot_general(a, b, (((1,), (1,)), ((), ())), preferred_element_type=F32)
+
+
+def dot_tn(a, b):
+    return lax.dot_general(a, b, (((0,), (0,)), ((), ())), preferred_element_type=F32)
+
+
+def gelu_parts(upper):
+    half = 0.5 * (1.0 + lax.erf(upper * math.sqrt(0.5)))
+    slope = half + upper * (jnp.exp(-0.5 * upper * upper) * (1.0 / math.sqrt(2.0 * math.pi)))
+    return upper * half, slope
+
+
+def normalize(hidden):
+    center = hidden - jnp.mean(hidden, axis=-1, keepdims=True)
+    spread = jnp.mean(center * center, axis=-1, keepdims=True)
+    scale = lax.rsqrt(spread + epsilon)
+    return center * scale, scale
+
+
+def start_rows(pieces, target, me, sems):
+    block = target.shape[0] // 8
+    copies = []
+    for index, (slot, first, ref) in enumerate(pieces):
+        row = pl.multiple_of((me ^ slot) * block + first, 16)
+        copy = pltpu.make_async_copy(ref, target.at[pl.ds(row, ref.shape[0])], sems.at[index])
+        copy.start()
+        copies.append(copy)
+    return copies
+
+
+def mixed_in(tok, mask, vec, rows):
+    keep = mask[rows, :]
+    return keep * vec[0:1, :] + (1.0 - keep) * tok[rows, :].astype(F32)
+
+
+def gate_kernel(count, *refs):
+    del count, refs
+
+
+def gate(arrays, after):
+    count = len(arrays)
+    return pl.pallas_call(
+        functools.partial(gate_kernel, count),
+        out_shape=[jax.ShapeDtypeStruct(a.shape, a.dtype) for a in arrays],
+        in_specs=[pl.BlockSpec(memory_space=pl.ANY)] * (count + len(after)),
+        out_specs=[pl.BlockSpec(memory_space=pl.ANY)] * count,
+        input_output_aliases={i: i for i in range(count)},
+        cost_estimate=pl.CostEstimate(flops=1000, bytes_accessed=1000, transcendentals=0),
+    )(*arrays, *after)
+
+
+def tick_kernel(*refs):
+    refs[-1][...] = jnp.zeros(refs[-1].shape, F32)
+
+
+def tick(after):
+    return pl.pallas_call(
+        tick_kernel,
+        out_shape=jax.ShapeDtypeStruct((8, 128), F32),
+        in_specs=[pl.BlockSpec(memory_space=pl.ANY)] * len(after),
+        out_specs=pl.BlockSpec(memory_space=pltpu.VMEM),
+        cost_estimate=pl.CostEstimate(flops=1000, bytes_accessed=1000, transcendentals=0),
+    )(*after)
+
+
+def prep_kernel(text_rows, info, tokens, out_grad, w_out, down, up, text_up, *outs):
+    tok, grad, grad_v, grad_t, sums, out_copy, down_copy, up_mine, up_other, strip0, te1, te2, te3 = outs
+    items, row_count, width = tokens.shape
+    patches = row_count - text_rows
+    tail = ITEM - TEXT_AT - text_rows
+    zeros = lambda n: jnp.zeros((n, width), F32)
+    totals = [zeros(1), zeros(1)]
+    texts = []
+    for i in range(items):
+        for source, target in ((tokens, tok), (out_grad, grad)):
+            whole = source[i].astype(F32)
+            patch, text = whole[:patches], whole[patches:]
+            full = jnp.concatenate([patch, zeros(TEXT_AT - patches), text, zeros(tail)], axis=0)
+            target[pl.ds(i * ITEM, ITEM), :] = full.astype(BF)
+            if target is grad:
+                grad_v[pl.ds(i * TEXT_AT, TEXT_AT), :] = full[:TEXT_AT].astype(BF)
+                texts.append(text)
+                totals[0] = totals[0] + jnp.sum(patch, axis=0, keepdims=True)
+                totals[1] = totals[1] + jnp.sum(text, axis=0, keepdims=True)
+    slots = jnp.concatenate(texts, axis=0).astype(BF)
+    grad_t[...] = slots
+    sums[0:1, :] = totals[0]
+    sums[1:2, :] = totals[1]
+    out_copy[...] = w_out[...]
+    down_copy[...] = down[...]
+    chip = info[0] // 2
+    side = chip % 2
+    block = up.shape[0]
+    pair = 2 * down.shape[0]
+    strip = lambda ref, c: ref[:, pl.ds(pl.multiple_of(c * pair, 128), pair)]
+    for k in range(2):
+        up_mine[:, k * pair : (k + 1) * pair] = strip(up, side + 2 * k)
+        up_other[:, k * pair : (k + 1) * pair] = strip(up, 1 - side + 2 * k)
+    strip0[...] = strip(text_up, chip)
+    for k, target in ((1, te1), (2, te2), (3, te3)):
+        target[pl.ds(0, block), :] = strip(text_up, chip ^ k)
+        target[pl.ds(block, slots.shape[0]), :] = slots
+
+
+def norm_kernel(info, tok, mask, even, odd, *refs):
+    n1, vec, up_bias, shards = refs[-4:]
+    me = info[0]
+    total, width = tok.shape
+    block = width // 8
+    for slot in range(8):
+        shards[me ^ slot] = (even, odd)[slot % 2][slot // 2]
+    wide = jnp.concatenate([shards[b] for b in range(8)], axis=1)
+    lane = lax.broadcasted_iota(jnp.int32, (1024, width), 0)
+    to = lax.broadcasted_iota(jnp.int32, (1024, width), 1)
+    spread = ((lane // 128) * block + lane % 128 == to) & (lane % 128 < block)
+    vec[...] = dot_nn(wide, jnp.where(spread, 1.0, 0.0).astype(BF))
+    hid = up_bias.shape[1] // 4
+    for q in range(4):
+        b = (q // 2) * 4 + q % 2 + ((me // 2) % 2) * 2
+        for r in range(hid // 128):
+            at = q * hid + r * 128
+            up_bias[0:1, at : at + 128] = shards[b, 10 + r : 11 + r, :].astype(F32)
+
+    @pl.loop(0, total // 64)
+    def _(step):
+        rows = pl.ds(pl.multiple_of(step * 64, 64), 64)
+        normal, _unused = normalize(mixed_in(tok, mask, vec, rows))
+        n1[rows, :] = (normal * vec[1:2, :] + vec[2:3, :]).astype(BF)
+
+
+def qkv_kernel(slots, info, n1, vec, *refs):
+    count = len(slots)
+    pieces = refs[:count]
+    qkv, weight, bias, sems = refs[-4:]
+    width = n1.shape[1]
+    copies = start_rows([(s, f, r) for (s, f), r in zip(slots, pieces)], weight, info[0], sems)
+    bias[0:1, 0:width] = vec[3:4, :]
+    bias[0:1, width : 2 * width] = jnp.zeros((1, width), F32)
+    bias[0:1, 2 * width : 3 * width] = vec[4:5, :]
+    for copy in copies:
+        copy.wait()
+
+    @pl.loop(0, 3 * width // 256)
+    def _(step):
+        cols = pl.ds(pl.multiple_of(step * 256, 256), 256)
+        factor = jnp.where(step < width // 256, 0.125, 1.0).astype(F32)
+        out = dot_nn(n1[...], weight[:, cols])
+        qkv[:, cols] = ((out + bias[0:1, cols]) * factor).astype(BF)
+
+
+def attn_kernel(info, qkv, *refs):
+    probs, ctx = refs[-2:]
+    total, width = ctx.shape
+    items = total // ITEM
+    pairs = width // 128
+    patches = info[3]
+
+    @pl.loop(0, items * pairs)
+    def _(step):
+        item, pair = step // pairs, step % pairs
+        rows = pl.ds(pl.multiple_of(item * ITEM, ITEM), ITEM)
+        lane = lambda part: pl.ds(pl.multiple_of(part * width + pair * 128, 128), 128)
+        q2, k2, v2 = qkv[rows, lane(0)], qkv[rows, lane(1)], qkv[rows, lane(2)]
+        low = lax.broadcasted_iota(jnp.int32, (ITEM, 128), 1) < HEAD_DIM
+        zero = jnp.zeros_like(q2)
+        both = jnp.concatenate([jnp.where(low, q2, zero), jnp.where(low, zero, q2)], axis=0)
+        scores = dot_nt(both, k2)
+        col = lax.broadcasted_iota(jnp.int32, (1, ITEM), 1)
+        valid = (col < patches) | ((col >= TEXT_AT) & (col < TEXT_AT + info[1 + item]))
+        scores = jnp.where(valid, scores, -1000000000.0)
+        expo = jnp.exp(scores - jnp.max(scores, axis=-1, keepdims=True))
+        prob = (expo * (1.0 / jnp.sum(expo, axis=-1, keepdims=True))).astype(BF)
+        probs[step] = prob
+        wide = jnp.concatenate([prob[:ITEM], prob[ITEM:]], axis=1)
+        values = jnp.concatenate([jnp.where(low, v2, zero), jnp.where(low, zero, v2)], axis=0)
+        ctx[rows, pl.ds(pl.multiple_of(pair * 128, 128), 128)] = dot_nn(wide, values).astype(BF)
+
+
+def out_kernel(text_rows, info, tok, mask, vec, ctx, out_w, *refs):
+    h1, n2t, *n2v = refs[-2 - tok.shape[0] // ITEM :]
+    items = tok.shape[0] // ITEM
+    texts = []
+    for i in range(items):
+        for at, size in ((0, TEXT_AT), (TEXT_AT, ITEM - TEXT_AT)):
+            rows = pl.ds(i * ITEM + at, size)
+            attended = dot_nn(ctx[rows, :], out_w[...]) + vec[5:6, :]
+            hidden = mixed_in(tok, mask, vec, rows) + attended
+            h1[rows, :] = hidden
+            normal, _unused = normalize(hidden)
+            second = normal * vec[6:7, :] + vec[7:8, :]
+            if at == 0:
+                n2v[i][...] = second.astype(BF)
+            else:
+                texts.append(second[:text_rows])
+    n2t[...] = jnp.concatenate(texts, axis=0).astype(BF)
+
+
+def pack_kernel(info, strip0, te1, te2, te3, grad_t, pack):
+    block, hid = strip0.shape[0], strip0.shape[1] // 2
+    rows = grad_t.shape[0]
+    other = pl.ds(pl.multiple_of((1 - info[0] % 2) * hid, 128), hid)
+    for k, ref in enumerate((strip0, te1, te2, te3)):
+        at = (k // 2) * block
+        pack[at : at + block, (k % 2) * hid : (k % 2 + 1) * hid] = ref[pl.ds(0, block), other]
+        there = pl.ds(2 * block + k * rows, rows)
+        pack[there, :] = grad_t[...] if k == 0 else ref[pl.ds(block, rows), :]
+
+
+def up_rows(me, pieces, target, sems):
+    block = target.shape[0] // 8
+    copies = []
+    for index, (base, ref) in enumerate(pieces):
+        for k in range(2):
+            row = pl.multiple_of((me ^ (base + 2 * k)) * block, 16)
+            sem = sems.at[2 * index + k]
+            copies.append(pltpu.make_async_copy(ref.at[k], target.at[pl.ds(row, block)], sem))
+    for copy in copies:
+        copy.start()
+    return copies
+
+
+def place_of(me):
+    return (me // 4) * 2 + me % 2
+
+
+def vision_kernel(pair, items, info, grad, up_bias, *refs):
+    parts, refs = refs[:items], refs[items:]
+    ups, downs = refs[:4], refs[4:6]
+    branch, gn2, act, low, up_w, down_w, rows_in, sems = refs[-8:]
+    me = info[0]
+    block = downs[0].shape[1]
+    copies = up_rows(me, list(zip((0, 4, 1, 5), ups)), up_w, sems)
+    place = place_of(me)
+    for j in range(4):
+        row = pl.multiple_of((place ^ j) * block, 16)
+        copy = pltpu.make_async_copy(downs[j % 2].at[j // 2], down_w.at[pl.ds(row, block)], sems.at[8 + j])
+        copy.start()
+        copies.append(copy)
+    for copy in copies:
+        copy.wait()
+    mine = grad.at[(me // 2) % 2 ^ 1] if pair else grad
+    for i, part in enumerate(parts):
+        rows_in[pl.ds(i * TEXT_AT, TEXT_AT), :] = part[...]
+    chunk = 512
+    for step in range(down_w.shape[0] // chunk):
+        cols = slice(step * chunk, (step + 1) * chunk)
+        upper = dot_nn(rows_in[...], up_w[:, cols]) + up_bias[0:1, cols]
+        active, slope = gelu_parts(upper)
+        active = active.astype(BF)
+        act[:, cols] = active
+        back = (dot_nt(mine[...], down_w[cols, :]) * slope).astype(BF)
+        low[:, cols] = back
+        if step == 0:
+            sum_branch = dot_nn(active, down_w[cols, :])
+            sum_gn2 = dot_nt(back, up_w[:, cols])
+        else:
+            sum_branch = sum_branch + dot_nn(active, down_w[cols, :])
+            sum_gn2 = sum_gn2 + dot_nt(back, up_w[:, cols])
+    branch[...] = sum_branch.astype(branch.dtype)
+    gn2[...] = sum_gn2.astype(gn2.dtype)
+
+
+def vision_grad_kernel(items, info, *refs):
+    ins = refs[:items], refs[items : 2 * items]
+    grads, refs = refs[2 * items], refs[2 * items + 1 :]
+    acts, lows = refs[:2], refs[2:4]
+    up_keep, up_send, down_keep, down_send, bias_sums = refs[-11:-6]
+    left_t, act_t, right, low, turn0, turn1 = refs[-6:]
+    me = info[0]
+    rows, width = items * ins[0][0].shape[0], ins[0][0].shape[1]
+    block = width // 8
+    half = down_keep.shape[1]
+    place, core = place_of(me), me % 2
+    for k in range(2):
+        at = pl.ds(k * rows, rows)
+        right[at, :] = grads[(me // 2) % 2 ^ k]
+        low[at, :] = lows[k][...]
+        turned = jnp.concatenate([ref[...] for ref in ins[k]], axis=0).T
+        turn = (turn0, turn1)[k]
+        for b in range(8):
+            spot = pl.multiple_of((me ^ b) * block, 16)
+            turn[pl.ds(spot, block), :] = turned[b * block : (b + 1) * block]
+        left_t[:, at] = turn[...]
+        act_t[:, at] = acts[k][...].T
+    chunk = 512
+    for step in range(4 * half // chunk):
+        cols = slice(step * chunk, (step + 1) * chunk)
+        grad_up = dot_nn(left_t[...], low[:, cols])
+        bias_sums[0:1, cols] = jnp.sum(low[:, cols].astype(F32), axis=0, keepdims=True)
+        grad_up = grad_up.astype(BF)
+        for b in range(4):
+            up_keep[b, :, cols] = grad_up[2 * b * block : (2 * b + 1) * block]
+            up_send[b, :, cols] = grad_up[(2 * b + 1) * block : (2 * b + 2) * block]
+    for q in range(4):
+        grad_down = dot_nn(act_t[q * half : (q + 1) * half, :], right[...]).astype(BF)
+        side = (q // 2) ^ (place // 2)
+
+        @pl.when(core == q % 2)
+        def _():
+            down_keep[side] = grad_down
+
+        @pl.when(core != q % 2)
+        def _():
+            down_send[side] = grad_down
+
+
+def text_kernel(info, down, up_bias, strip0, te1, te2, te3, far, even, odd, *refs):
+    grad0, refs = refs[0], refs[1:]
+    branch_keep, branch_send, gn2_keep, gn2_send, up_keep, up_send, grad_down, bias_sums = refs[-12:-4]
+    up_w, left, right, left_t = refs[-4:]
+    me = info[0]
+    width = down.shape[1]
+    hid = down.shape[0]
+    block = width // 8
+    rows = even.shape[1]
+    mine = pl.ds(pl.multiple_of((me % 2) * hid, 128), hid)
+    spot = lambda slot: pl.ds(pl.multiple_of((me ^ slot) * block, 16), block)
+    up_w[spot(0), :] = strip0[:, mine]
+    for s, te in ((2, te1), (4, te2), (6, te3)):
+        up_w[spot(s), :] = te[pl.ds(0, block), mine]
+        right[pl.ds(s * rows, rows), :] = te[pl.ds(block, rows), :]
+    up_w[spot(1), :] = far[pl.ds(0, block), pl.ds(0, hid)]
+    up_w[spot(3), :] = far[pl.ds(0, block), pl.ds(hid, hid)]
+    up_w[spot(5), :] = far[pl.ds(block, block), pl.ds(0, hid)]
+    up_w[spot(7), :] = far[pl.ds(block, block), pl.ds(hid, hid)]
+    right[pl.ds(0, rows), :] = grad0[...]
+    for k in range(4):
+        right[pl.ds((2 * k + 1) * rows, rows), :] = far[pl.ds(2 * block + k * rows, rows), :]
+    for slot in range(8):
+        left[pl.ds(slot * rows, rows), :] = (even, odd)[slot % 2][slot // 2]
+    turned = left[...].T
+    for b in range(8):
+        left_t[spot(b), :] = turned[b * block : (b + 1) * block]
+    upper = dot_nn(left[...], up_w[...]) + up_bias[...]
+    active, slope = gelu_parts(upper)
+    act = active.astype(BF)
+    low = (dot_nt(right[...], down[...]) * slope).astype(BF)
+    bias_sums[...] = jnp.sum(low.astype(F32), axis=0, keepdims=True)
+    gn2 = dot_nt(low, up_w[...]).astype(BF)
+    branch = dot_nn(act, down[...]).astype(BF)
+    for s in range(4):
+        gn2_keep[s] = gn2[2 * s * rows : (2 * s + 1) * rows]
+        gn2_send[s] = gn2[(2 * s + 1) * rows : (2 * s + 2) * rows]
+        branch_keep[s] = branch[2 * s * rows : (2 * s + 1) * rows]
+        branch_send[s] = branch[(2 * s + 1) * rows : (2 * s + 2) * rows]
+    grad_down[...] = dot_tn(act, right[...]).astype(BF)
+    grad_up = dot_nn(left_t[...], low).astype(BF)
+    for b in range(4):
+        up_keep[b] = grad_up[2 * b * block : (2 * b + 1) * block]
+        up_send[b] = grad_up[(2 * b + 1) * block : (2 * b + 2) * block]
+
+
+def attn_bwd_kernel(text_rows, info, gn2v, gn2x, t0, t1, t2, t3, grad, h1, vec, qkv, probs, weight, *refs):
+    gh1, low, stacked, sums, gn2, gctx = refs[-6:]
+    total, width = h1.shape
+    items = total // ITEM
+    text = (
+        t0[0].astype(F32) + t1[...].astype(F32) + t2[...].astype(F32) + t3[...].astype(F32)
+    )
+    for i in range(items):
+        part = pl.ds(i * TEXT_AT, TEXT_AT)
+        gn2[pl.ds(i * ITEM, TEXT_AT), :] = gn2v[part, :] + gn2x[part, :].astype(F32)
+        gn2[pl.ds(i * ITEM + TEXT_AT, text_rows), :] = text[i * text_rows : (i + 1) * text_rows]
+        pad = ITEM - TEXT_AT - text_rows
+        gn2[pl.ds(i * ITEM + TEXT_AT + text_rows, pad), :] = jnp.zeros((pad, width), F32)
+    sums[...] = jnp.zeros_like(sums)
+
+    @pl.loop(0, total // 64)
+    def _(step):
+        rows = pl.ds(pl.multiple_of(step * 64, 64), 64)
+        normal, scale = normalize(h1[rows, :])
+        above = gn2[rows, :]
+        inner = above * vec[6:7, :]
+        back = scale * (
+            inner
+            - jnp.mean(inner, axis=-1, keepdims=True)
+            - normal * jnp.mean(inner * normal, axis=-1, keepdims=True)
+        )
+        out = grad[rows, :].astype(F32)
+        hidden = out + back
+        gh1[rows, :] = hidden
+        low[rows, :] = hidden.astype(BF)
+        sums[0:1, :] += jnp.sum(above * normal, axis=0, keepdims=True)
+        sums[1:2, :] += jnp.sum(above, axis=0, keepdims=True)
+        sums[2:3, :] += jnp.sum(hidden.astype(BF).astype(F32), axis=0, keepdims=True)
+
+    gctx[...] = dot_nt(low[...], weight[...]).astype(BF)
+    pairs = width // 128
+
+    @pl.loop(0, items * pairs)
+    def _(step):
+        item, pair = step // pairs, step % pairs
+        rows = pl.ds(pl.multiple_of(item * ITEM, ITEM), ITEM)
+        lane = lambda part: pl.ds(pl.multiple_of(part * width + pair * 128, 128), 128)
+        q2, k2, v2 = qkv[rows, lane(0)], qkv[rows, lane(1)], qkv[rows, lane(2)]
+        g2 = gctx[rows, pl.ds(pl.multiple_of(pair * 128, 128), 128)]
+        lower = lax.broadcasted_iota(jnp.int32, (ITEM, 128), 1) < HEAD_DIM
+        zero = jnp.zeros_like(q2)
+        split = lambda a: jnp.concatenate([jnp.where(lower, a, zero), jnp.where(lower, zero, a)], axis=0)
+        both_g = split(g2)
+        prob_b = probs[step]
+        prob = prob_b.astype(F32)
+        gprob = dot_nt(both_g, v2)
+        weighted = prob * gprob
+        gscore = (weighted - prob * jnp.sum(weighted, axis=-1, keepdims=True)).astype(BF)
+        stacked[rows, lane(2)] = dot_tn(prob_b, both_g).astype(BF)
+        stacked[rows, lane(1)] = dot_tn(gscore, split(q2)).astype(BF)
+        wide = jnp.concatenate([gscore[:ITEM], gscore[ITEM:]], axis=1)
+        gquery = dot_nn(wide, split(k2)).astype(BF).astype(F32) * 0.125
+        stacked[rows, lane(0)] = gquery.astype(BF)
+
+    for part in (0, 2):
+        cols = stacked[:, part * width : (part + 1) * width].astype(F32)
+        sums[3 + part // 2 : 4 + part // 2, :] = jnp.sum(cols, axis=0, keepdims=True)
+
+
+def attn_grad_kernel(last, info, left, stacked, other_left, other, *refs):
+    me = info[0]
+    width = left.shape[1]
+    block = width // 8
+    keep, send, left_t, other_t = refs[-4:]
+    first = 2 if last else 0
+    for source, target in ((left, left_t), (other_left, other_t))[:2] if last else ((left, left_t),):
+        turned = source[...].T
+        for b in range(8):
+            place = pl.multiple_of((me ^ b) * block, 16)
+            target[pl.ds(place, block), :] = turned[b * block : (b + 1) * block]
+    for part in range(2):
+        cols = slice(part * width, (part + 1) * width)
+        if last and part == 1:
+            value = dot_nn(other_t[...], other[...]).astype(BF)
+        else:
+            right = stacked[:, (first + part) * width : (first + part + 1) * width]
+            value = dot_nn(left_t[...], right).astype(BF)
+        for b in range(4):
+            keep[b, :, cols] = value[2 * b * block : (2 * b + 1) * block]
+            send[b, :, cols] = value[(2 * b + 1) * block : (2 * b + 2) * block]
+
+
+def last_kernel(slots, info, stacked, gh1, tok, mask, vec, *refs):
+    count = len(slots)
+    pieces = refs[:count]
+    gtok, sums, weight, sems = refs[-4:]
+    copies = start_rows([(s, f, r) for (s, f), r in zip(slots, pieces)], weight, info[0], sems)
+    sums[...] = jnp.zeros_like(sums)
+    for copy in copies:
+        copy.wait()
+
+    @pl.loop(0, tok.shape[0] // 128)
+    def _(step):
+        rows = pl.ds(pl.multiple_of(step * 128, 128), 128)
+        above = dot_nt(stacked[rows, :], weight[...])
+        normal, scale = normalize(mixed_in(tok, mask, vec, rows))
+        inner = above * vec[1:2, :]
+        back = scale * (
+            inner
+            - jnp.mean(inner, axis=-1, keepdims=True)
+            - normal * jnp.mean(inner * normal, axis=-1, keepdims=True)
+        )
+        hidden = gh1[rows, :] + back
+        keep = mask[rows, :]
+        gtok[rows, :] = hidden * (1.0 - keep)
+        sums[0:1, :] += jnp.sum(hidden * keep, axis=0, keepdims=True)
+        sums[1:2, :] += jnp.sum(above * normal, axis=0, keepdims=True)
+        sums[2:3, :] += jnp.sum(above, axis=0, keepdims=True)
+
+
+def call(kernel, outs, scratch, args, pieces=(), us=1):
+    in_specs = [pl.BlockSpec(memory_space=pltpu.SMEM)]
+    in_specs += [pl.BlockSpec(memory_space=pltpu.VMEM)] * (len(args) - 1)
+    in_specs += [pl.BlockSpec(memory_space=pl.ANY)] * len(pieces)
+    return pl.pallas_call(
+        kernel,
+        out_shape=[jax.ShapeDtypeStruct(s, d) for s, d in outs],
+        in_specs=in_specs,
+        out_specs=[pl.BlockSpec(memory_space=pltpu.VMEM)] * len(outs),
+        scratch_shapes=scratch,
+        compiler_params=pltpu.CompilerParams(vmem_limit_bytes=VMEM_LIMIT),
+        cost_estimate=pl.CostEstimate(flops=int(us * SCALE * 1.1e9), bytes_accessed=int(us * SCALE * 1e6), transcendentals=0),
+    )(*args, *pieces)
+
+
+def swap(array, mask):
+    return lax.ppermute(array, "fsdp", [(i, i ^ mask) for i in range(8)])
+
+
+def along_rep(array, pairs):
+    return lax.ppermute(array, "rep", pairs)
+
+
+def add(*terms):
+    out = terms[0].astype(F32)
+    for term in terms[1:]:
+        out = out + term.astype(F32)
+    return out.astype(BF)
+
+
+def planned(
+    tokens,
+    out_grad,
+    masked,
+    lengths,
+    mask_vec,
+    norm1_gain,
+    norm1_shift,
+    w_qkv,
+    query_bias,
+    value_bias,
+    w_out,
+    out_bias,
+    norm2_gain,
+    norm2_shift,
+    vision_up,
+    vision_up_bias,
+    vision_down,
+    vision_down_bias,
+    text_up,
+    text_up_bias,
+    text_down,
+    text_down_bias,
+):
+    items, row_count, width = tokens.shape
+    text_rows = masked.shape[1]
+    patches = row_count - text_rows
+    block = width // 8
+    half = block // 2
+    hid = vision_down.shape[0]
+    pair = 2 * hid
+    hidden = 8 * hid
+    total = items * ITEM
+    vision_rows = items * TEXT_AT
+    slot_rows = items * text_rows
+    te_rows = block + slot_rows
+    me = lax.axis_index("fsdp").astype(jnp.int32)
+    rep = lax.axis_index("rep").astype(jnp.int32)
+    core, chip, side = me % 2, me // 2, (me // 2) % 2
+    sem = lambda n: pltpu.SemaphoreType.DMA((n,))
+    quad = lambda r, c: ((4, r, c), BF)
+
+    names = (
+        mask_vec,
+        norm1_gain,
+        norm1_shift,
+        query_bias,
+        value_bias,
+        out_bias,
+        norm2_gain,
+        norm2_shift,
+        vision_down_bias,
+        text_down_bias,
+    )
+    own_vec = jnp.pad(jnp.stack(names), ((0, 0), (0, 128 - block)))
+    own_vec = jnp.concatenate([own_vec, vision_up_bias.reshape(-1, 128)], axis=0)
+    own_vec = jnp.pad(own_vec, ((0, 16 - own_vec.shape[0]), (0, 0)))[None]
+    vx, vy, vxy = swap(own_vec, 2), swap(own_vec, 4), swap(own_vec, 6)
+    qx, qy = swap(w_qkv, 2), swap(w_qkv, 4)
+    mask = jnp.concatenate(
+        [
+            jnp.zeros((items, TEXT_AT), F32),
+            masked.astype(F32),
+            jnp.zeros((items, ITEM - TEXT_AT - text_rows), F32),
+        ],
+        axis=1,
+    ).reshape(total, 1)
+    info = jnp.concatenate([me[None], lengths, jnp.full((1,), patches, jnp.int32)])
+    tok, grad, grad_v, grad_t, grad_sums, own_out, own_down, up_mine, up_other, strip0, te1, te2, te3 = call(
+        functools.partial(prep_kernel, text_rows),
+        [
+            ((total, width), BF),
+            ((total, width), BF),
+            ((vision_rows, width), BF),
+            ((slot_rows, width), BF),
+            ((2, width), F32),
+            ((block, width), BF),
+            ((hid, width), BF),
+            ((block, 2 * pair), BF),
+            ((block, 2 * pair), BF),
+            ((block, pair), BF),
+            ((te_rows, width), BF),
+            ((te_rows, width), BF),
+            ((te_rows, width), BF),
+        ],
+        [],
+        [info, tokens, out_grad, w_out, vision_down, vision_up, text_up],
+        us=5,
+    )
+    vec_four = jnp.concatenate([own_vec, vx, vy, vxy], axis=0)
+    vec_arrays = [vec_four, swap(vec_four, 1)]
+    part1, part2 = gate([qx[:half], qy[half:]], [tok, vec_arrays[1]])
+
+    far1, far2 = swap(part1, 4), swap(part2, 2)
+    near = [swap(a, 1) for a in (w_qkv, qx, qy)]
+    n1, vec, up_bias = call(
+        norm_kernel,
+        [((total, width), BF), ((16, width), F32), ((1, 4 * hid), F32)],
+        [pltpu.VMEM((8, 16, 128), BF)],
+        [info, tok, mask, *vec_arrays],
+        [part1],
+        us=5,
+    )
+    far1, far2, up_other, own_down, own_out, grad_v = gate(
+        [far1, far2, up_other, own_down, own_out, grad_v], [n1, *near]
+    )
+    out_all = lax.all_gather(own_out, "fsdp", tiled=True)
+    attn = [(0, 0, w_qkv), (2, 0, qx), (4, 0, qy), (6, 0, far1), (6, half, far2)]
+    attn += [(1, 0, near[0]), (3, 0, near[1]), (5, 0, near[2]), (7, 0, swap(far1, 1)), (7, half, swap(far2, 1))]
+    attn_slots = tuple((p[0], p[1]) for p in attn)
+    attn_arrays = [p[2] for p in attn]
+
+    up_x, down_y = swap(up_other, 2), swap(own_down, 4)
+    (qkv,) = call(
+        functools.partial(qkv_kernel, attn_slots),
+        [((total, 3 * width), BF)],
+        [pltpu.VMEM((width, 3 * width), BF), pltpu.VMEM((1, 3 * width), F32), sem(len(attn))],
+        [info, n1, vec],
+        attn_arrays,
+        us=8,
+    )
+    t = tick([qkv, up_x, down_y])
+
+    up_x, down_y, te1, te2, te3 = gate([up_x, down_y, te1, te2, te3], [t])
+    up_two = jnp.stack([up_mine, up_x])
+    up_y, up_c = swap(up_two, 4), swap(up_two, 1)
+    te1, te3 = swap(te1, 2), swap(te3, 6)
+    probs, ctx = call(
+        attn_kernel,
+        [((items * width // 128, 2 * ITEM, ITEM), BF), ((total, width), BF)],
+        [],
+        [info, qkv],
+        [t],
+        us=10,
+    )
+    t = tick([ctx, up_y, up_c, te1, te3])
+
+    up_y, te1, te2, te3, down_y = gate([up_y, te1, te2, te3, down_y], [t])
+    te2 = swap(te2, 4)
+    down_two = jnp.stack([own_down, down_y])
+    up_yc, down_c = swap(up_y, 1), swap(down_two, 1)
+    h1, n2t, *n2v = call(
+        functools.partial(out_kernel, text_rows),
+        [((total, width), F32), ((slot_rows, width), BF)] + [((TEXT_AT, width), BF)] * items,
+        [],
+        [info, tok, mask, vec, ctx, out_all],
+        [t],
+        us=5,
+    )
+    t = tick([n2t, te2, up_yc, down_c])
+
+    te1, te2, te3, n2t_sent, *n2v_sent = gate([te1, te2, te3, n2t, *n2v], [t])
+    (pack,) = call(
+        pack_kernel,
+        [((2 * block + 4 * slot_rows, width), BF)],
+        [],
+        [info, strip0, te1, te2, te3, grad_t],
+    )
+    text_in = [swap(n2t_sent, 2), swap(n2t_sent, 4), swap(n2t_sent, 6)]
+    n2x = [swap(n2v_sent[0], 2)]
+    far = swap(pack, 1)
+    weights = [up_two, up_y, up_c, up_yc, down_two, down_c]
+
+    def vision(rows_in, grads, kind, after):
+        return call(
+            functools.partial(vision_kernel, kind == BF, items),
+            [
+                ((vision_rows, width), kind),
+                ((vision_rows, width), kind),
+                ((vision_rows, 4 * hid), BF),
+                ((vision_rows, 4 * hid), BF),
+            ],
+            [
+                pltpu.VMEM((width, 4 * hid), BF),
+                pltpu.VMEM((4 * hid, width), BF),
+                pltpu.VMEM((vision_rows, width), BF),
+                sem(12),
+            ],
+            [info, grads, up_bias, *rows_in],
+            [*weights, *after],
+            us=9,
+        )
+
+    branch_own, gn2_own, act_own, low_own = vision(n2v, grad_v, F32, [pack])
+    pairs = [[0, 2], [1, 3], [4, 6], [5, 7]]
+    grad_pair = lax.all_gather(grad_v, "fsdp", axis_index_groups=pairs)
+    t = tick([gn2_own, *text_in, n2x[0], far])
+
+    far, *rest = gate([far, *text_in, *n2v_sent[1:]], [t])
+    text_four = jnp.stack([n2t, *rest[:3]])
+    text_odd = swap(text_four, 1)
+    n2x += [swap(a, 2) for a in rest[3:]]
+    branch_keep, branch_send, gn2_keep, gn2_send, tu_keep, tu_send, td, text_bias_sum = call(
+        text_kernel,
+        [
+            quad(slot_rows, width),
+            quad(slot_rows, width),
+            quad(slot_rows, width),
+            quad(slot_rows, width),
+            quad(block, hid),
+            quad(block, hid),
+            ((hid, width), BF),
+            ((1, hid), F32),
+        ],
+        [
+            pltpu.VMEM((width, hid), BF),
+            pltpu.VMEM((8 * slot_rows, width), BF),
+            pltpu.VMEM((8 * slot_rows, width), BF),
+            pltpu.VMEM((width, 8 * slot_rows), BF),
+        ],
+        [
+            info,
+            text_down,
+            text_up_bias.astype(F32).reshape(1, hid),
+            strip0,
+            te1,
+            te2,
+            te3,
+            far,
+            text_four,
+            text_odd,
+            grad_t,
+        ],
+        us=6,
+    )
+    t = tick([gn2_keep, *n2x, grad_pair])
+
+    gn2_send, *n2x = gate([gn2_send, *n2x], [t])
+    gn2_sum = add(gn2_keep, swap(gn2_send, 1))
+    gn2_text = [gn2_sum] + [swap(gn2_sum[s], 2 * s) for s in (1, 2, 3)]
+    branch_x, gn2_x, act_x, low_x = vision(n2x, grad_pair, BF, [gn2_sum])
+    t = tick([gn2_x, *gn2_text[1:]])
+
+    (gn2_x,) = gate([gn2_x], [t])
+    gn2_back = swap(gn2_x, 2)
+    vu_keep, vu_send, vd_keep, vd_send, vu_bias_sum = call(
+        functools.partial(vision_grad_kernel, items),
+        [
+            quad(block, 4 * hid),
+            quad(block, 4 * hid),
+            ((2, hid, width), BF),
+            ((2, hid, width), BF),
+            ((1, 4 * hid), F32),
+        ],
+        [
+            pltpu.VMEM((width, 2 * vision_rows), BF),
+            pltpu.VMEM((4 * hid, 2 * vision_rows), BF),
+            pltpu.VMEM((2 * vision_rows, width), BF),
+            pltpu.VMEM((2 * vision_rows, 4 * hid), BF),
+            pltpu.VMEM((width, vision_rows), BF),
+            pltpu.VMEM((width, vision_rows), BF),
+        ],
+        [info, *n2v, *n2x, grad_pair, act_own, act_x, low_own, low_x],
+        [t],
+        us=12,
+    )
+    t = tick([vu_bias_sum, gn2_back])
+
+    vu_send, vd_send, branch_x, branch_send, gn2_back = gate([vu_send, vd_send, branch_x, branch_send, gn2_back], [t])
+    vu_got, vd_got = swap(vu_send, 1), swap(vd_send, 1)
+    vd_near, vd_far = add(vd_keep[0], vd_got[0]), add(vd_keep[1], vd_got[1])
+    vu_far = [add(vu_keep[k], vu_got[k]) for k in (2, 3)]
+    vd_y, vu_y1 = swap(vd_far, 4), swap(vu_far[1], 4)
+    branch_back = swap(branch_x, 2)
+    branch_got = swap(branch_send, 1)
+    gh1, low_attn, stacked, sums_two = call(
+        functools.partial(attn_bwd_kernel, text_rows),
+        [((total, width), F32), ((total, width), BF), ((total, 3 * width), BF), ((8, width), F32)],
+        [pltpu.VMEM((total, width), F32), pltpu.VMEM((total, width), BF)],
+        [info, gn2_own, gn2_back, *gn2_text, grad, h1, vec, qkv, probs, out_all],
+        [vd_far, *vu_far],
+        us=18,
+    )
+    t = tick([stacked, vd_y, vu_y1, branch_back, branch_got])
+
+    vd_y, vu_y1, vu_far0, branch_got = gate([vd_y, vu_y1, vu_far[0], branch_got], [t])
+    vd = lax.psum(add(vd_near, vd_y), "rep", axis_index_groups=[[1, 0, 2, 3]])
+    vu_x = swap(add(vu_keep[1], vu_got[1], vu_y1), 2)
+    vu_y0 = swap(vu_far0, 4)
+
+    def attn_grads(last, after):
+        return call(
+            functools.partial(attn_grad_kernel, last),
+            [quad(block, 2 * width), quad(block, 2 * width)],
+            [pltpu.VMEM((width, total), BF), pltpu.VMEM((width, total), BF)],
+            [info, n1, stacked, ctx, low_attn],
+            after,
+            us=5,
+        )
+
+    a_keep, a_send = attn_grads(False, [t])
+    t = tick([a_keep, vu_x, vu_y0])
+    (a_send,) = gate([a_send], [t])
+    a_got = swap(a_send, 1)
+    branch_sum = add(branch_keep, branch_got)
+    vu_both = jnp.stack([add(vu_keep[0], vu_got[0], vu_y0), vu_x])
+    vu = lax.psum(vu_both, "rep", axis_index_groups=[[0, 1, 3, 2]])
+    b_keep, b_send = attn_grads(True, [t])
+    t = tick([b_keep, a_got])
+    a_got, b_send, branch_sum = gate([a_got, b_send, branch_sum], [t])
+    b_got = swap(b_send, 1)
+
+    def begin(keep, got, one):
+        i = one // 2
+        return add(jnp.stack([keep[i], keep[3]]), jnp.stack([got[i], got[3]]))
+
+    a_first, b_first = begin(a_keep, a_got, 2), begin(b_keep, b_got, 4)
+    a_there, b_there = swap(a_first, 2), swap(b_first, 4)
+    branch_t = [branch_sum] + [swap(branch_sum[s], 2 * s) for s in (1, 2, 3)]
+    gtok, sums_one = call(
+        functools.partial(last_kernel, attn_slots),
+        [((total, width), F32), ((8, width), F32)],
+        [pltpu.VMEM((width, 3 * width), BF), sem(len(attn))],
+        [info, stacked, gh1, tok, mask, vec],
+        attn_arrays + [a_first, b_first],
+        us=12,
+    )
+    t = tick([sums_one, a_there, b_there, *branch_t[1:]])
+
+    a_there, b_there, sums_one = gate([a_there, b_there, sums_one], [t])
+    a_beyond = swap(add(a_keep[2], a_got[2], a_there[1]), 4)
+    b_beyond = swap(add(b_keep[1], b_got[1], b_there[1]), 2)
+    ga = add(a_keep[0], a_got[0], a_there[0], a_beyond)
+    gb = add(b_keep[0], b_got[0], b_there[0], b_beyond)
+
+    inner = (rep == 1) | (rep == 2)
+
+    def rep_sum(array):
+        part = add(array, along_rep(array, [(0, 1), (3, 2)]))
+        whole = add(part, along_rep(part, [(1, 2), (2, 1)]))
+        return jnp.where(inner, whole, along_rep(whole, [(1, 0), (2, 3)]))
+
+    ga, gb = rep_sum(ga), rep_sum(gb)
+    tu_keep, tu_send, td = lax.psum((tu_keep, tu_send, td), "rep")
+    tu_keep, tu_send, td = gate([tu_keep, tu_send, td], [t])
+    tu_got = swap(tu_send, 1)
+    tu_wide = jnp.where(
+        core == 0,
+        jnp.concatenate([tu_keep, tu_got], axis=-1),
+        jnp.concatenate([tu_got, tu_keep], axis=-1),
+    )
+    tu_all = [tu_wide[0]] + [swap(tu_wide[s], 2 * s) for s in (1, 2, 3)]
+    tu_x = [jnp.where(side == 0, tu_all[k], tu_all[k ^ 1]) for k in range(4)]
+    tu_y = [jnp.where(me // 4 == 0, tu_x[k], tu_x[k ^ 2]) for k in range(4)]
+    grad_text_up = jnp.concatenate(tu_y, axis=1).astype(F32)
+    grad_text_down = td.astype(F32)
+
+    vu_sum = vu_bias_sum.reshape(2, 1, pair)
+    vu_sum = jnp.where(
+        side == 0,
+        jnp.concatenate([vu_sum, jnp.zeros_like(vu_sum)], axis=1),
+        jnp.concatenate([jnp.zeros_like(vu_sum), vu_sum], axis=1),
+    )
+    vu_sum = vu_sum.reshape(8, hid // block, block).transpose(1, 0, 2).reshape(-1, width)
+    flat = jnp.concatenate(
+        [sums_one[0:3], sums_two[3:5], sums_two[2:3], sums_two[0:2], grad_sums, vu_sum], axis=0
+    )
+    for m in (1, 2, 4):
+        flat = flat + swap(flat, m)
+    mine = lax.dynamic_slice_in_dim(flat, me * block, block, axis=1)
+    mine = jnp.concatenate([mine, text_bias_sum.reshape(-1, block)], axis=0)
+    for m in (1, 2):
+        mine = mine + along_rep(mine, [(i, i ^ m) for i in range(4)])
+    count = len(names)
+    rows = hid // block
+    vec_grad = [mine[i] for i in range(count)]
+    vu_bias_grad = mine[count : count + rows].reshape(-1)
+    tu_bias_grad = mine[count + rows : count + 2 * rows].reshape(-1)
+
+    vu, vd = gate([vu, vd], [ga, gb])
+    ga, gb = ga.astype(F32), gb.astype(F32)
+    grad_w_qkv = jnp.concatenate([ga, gb[:, :width]], axis=1)
+    grad_w_out = gb[:, width:]
+    vu_s = [jnp.where(side == 0, vu[k], vu[1 - k]) for k in range(2)]
+    grad_vision_up = jnp.concatenate(
+        [vu_s[0][:, :pair], vu_s[1][:, :pair], vu_s[0][:, pair:], vu_s[1][:, pair:]], axis=1
+    ).astype(F32)
+    grad_vision_down = vd.astype(F32)
+    h1 = h1.reshape(items, ITEM, width)
+    branch_v = (branch_own + branch_back.astype(F32)).reshape(items, TEXT_AT, width)[:, :patches]
+    mixed_v = h1[:, :patches] + branch_v + vec[8][None, None]
+    branch_t = branch_t[0][0].astype(F32) + sum(b.astype(F32) for b in branch_t[1:])
+    branch_t = branch_t.reshape(items, text_rows, width)
+    mixed_t = h1[:, TEXT_AT : TEXT_AT + text_rows] + branch_t + vec[9][None, None]
+    mixed = jnp.concatenate([mixed_v.astype(BF), mixed_t.astype(BF)], axis=1)
+    gtok = gtok.reshape(items, ITEM, width)
+    grad_tokens = jnp.concatenate(
+        [gtok[:, :patches], gtok[:, TEXT_AT : TEXT_AT + text_rows]], axis=1
+    )
+    return (
+        mixed,
+        grad_tokens,
+        vec_grad[0],
+        vec_grad[1],
+        vec_grad[2],
+        grad_w_qkv,
+        vec_grad[3],
+        vec_grad[4],
+        grad_w_out,
+        vec_grad[5],
+        vec_grad[6],
+        vec_grad[7],
+        grad_vision_up,
+        vu_bias_grad,
+        grad_vision_down,
+        vec_grad[8],
+        grad_text_up,
+        tu_bias_grad,
+        grad_text_down,
+        vec_grad[9],
+    )
 
 
 def layer_norm(hidden, gain, shift):
@@ -43,7 +973,7 @@
     return (grad_up, grad_up_shift, grad_down, grad_down_shift, grad_rows)
 
 
-def local(
+def general(
     tokens,
     out_grad,
     masked,
@@ -416,8 +1346,12 @@
 
 
 def solution(mesh):
+    if mesh.shape["fsdp"] == 8 and mesh.shape["rep"] == 4:
+        body = planned
+    else:
+        body = general
     return jax.shard_map(
-        local,
+        body,
         mesh=mesh,
         in_specs=(
             P(("fsdp", "rep"), None, None),

time: 898 us -> 379 us (0.42)
  waiting for transfers between devices: 441 us -> 94.2 us
  blocking collectives: 196 us -> 0 us
  Pallas kernels: 0 us -> 121 us
  matrix products: 118 us -> 0 us
  starting transfers between devices: 1.15 us -> 60.4 us
  local copies, waits for them, and re-layouts: 67.9 us -> 43.8 us
    reduce_scatter x12 -> x0, waiting for transfers between devices: 316 us -> none  [the longest x1 78 us: local(): lax.psum_scatter(vision_grads[2], 'fsdp', scatter_dimension=0, tiled=True)]
    all_gather x8 -> x0, blocking collectives: 125 us -> none  [the longest x1 20.2 us: local(): lax.all_gather(quarter[16].astype(jnp.bfloat16), 'rep', axis=0, tiled=True)]
    pallas_call x0 -> x40, Pallas kernels: none -> 121 us  [the longest x14 115 us: call(): pl.pallas_call(kernel, out_shape=[jax.ShapeDtypeStruct(s, d) for s, d in...]
    all_gather x6 -> x2, waiting for transfers between devices: 120 us -> 0.02 us  [the longest x1 0.02 us: planned(): grad_pair = lax.all_gather(grad_v, 'fsdp', axis_index_groups=pairs)]
    dot_general x24 -> x0, matrix products: 118 us -> none  [the longest x2 22.7 us: expert_backward(): jnp.einsum('rd,fd->rf', grad_b, down_matrix, preferred_element_type=jnp.f...]
    ppermute x0 -> x66, waiting for transfers between devices: none -> 93.6 us  [the longest x8 52 us: along_rep(): return lax.ppermute(array, 'rep', pairs)]
    unnamed x4 -> x0, blocking collectives: 70.2 us -> none
    ppermute x0 -> x66, starting transfers between devices: none -> 59.8 us  [the longest x58 48 us: swap(): return lax.ppermute(array, 'fsdp', [(i, i ^ mask) for i in range(8)])]
  transfers between devices with their start and end apart: 18 -> 71, of which waited for: 15 -> 22; matrix products, arithmetic and copies ran while one was open for 19% -> 14% of each run, Pallas kernels for 0% -> 31%
where the time goes in v2:
time: 379 us; the launch traced here: 373 us
  Pallas kernels  121 us (32%)
  waiting for transfers between devices  94.2 us (25%)
  starting transfers between devices  60.4 us (16%)
  local copies, waits for them, and re-layouts  43.8 us (12%)
  other arithmetic  36.6 us (10%)
  between operations  16.7 us (4%)
    pallas_call x14, Pallas kernels, call(): pl.pallas_call(kernel, out_shape=[jax.ShapeDtypeStruct(s, d) for s, d in...  115 us
    ppermute x8, waiting for transfers between devices, along_rep(): return lax.ppermute(array, 'rep', pairs)  52 us
    ppermute x58, starting transfers between devices, swap(): return lax.ppermute(array, 'fsdp', [(i, i ^ mask) for i in range(8)])  48 us
    ppermute x58, waiting for transfers between devices, swap(): return lax.ppermute(array, 'fsdp', [(i, i ^ mask) for i in range(8)])  41.7 us
    unnamed x197, local copies, waits for them, and re-layouts  29.1 us
    ppermute x8, starting transfers between devices, along_rep(): return lax.ppermute(array, 'rep', pairs)  11.8 us
    convert_element_type x15, other arithmetic, add(): return out.astype(BF)  11.3 us
  transfers between devices with their start and end apart: 71, of which 22 were waited for; matrix products, arithmetic and copies ran while one was open for 14% of the time, Pallas kernels for 31%

profile of v2, /device:TPU:0, one launch (start us, length us, event | category | flops | bytes accessed | tf_op | source)
XLA Modules:
  0.0 372.8 jit_solution(18074141036755685864)
XLA Ops:
  8.1 3.0 collective-permute-start.5
  11.1 1.5 collective-permute-start.4
  12.6 1.5 stack.97
  15.5 2.9 collective-permute-start.2
  19.6 2.1 copy.117.tokens
  24.2 4.2 %shard_map.365 = (bf16[512,768]{1,0:T(8,128)(2,1)}, bf16[512,768]{1,0:T(8,128)(2,1)}, bf16[416,768]{1,0:T(8,128)(2,1)}, bf16[80,768]{1,0:T(8,128)(2,1)}, f32[2,7...) custom-call(s32[4]{0:T(128)} %pad_add_fusion.info, ...), custom_call_target="tpu_custom_call" | custom-call | flops 1100000000 | bytes 1000000 | tf_op jit(solution)/shard_map/pallas_call | solution.py:503
  31.0 1.5 collective-permute-start.7
  33.5 4.7 %shard_map.367 = (bf16[512,768]{1,0:T(8,128)(2,1)}, f32[16,768]{1,0:T(8,128)}, f32[1,1536]{1,0:T(1,128)}) custom-call(s32[4]{0:T(128)} %pad_add_fusion.info, bf16[512,768]{1,0:T(8,128)(2,1)} %get-tuple-element.125.refs_2_.tok, f32[512,1]{1,0:T(8,128)} %bitcast.147, bf16[4,16,128]{2,1,0:T(8,128)(2,1)} %copy-done.88, bf16[4,16,128]{2,1,0:T(8,128)(2,1)} %copy-done.86, ...), custom_call_target="tpu_custom_call" | custom-call | flops 1100000000 | bytes 1000000 | tf_op jit(solution)/shard_map/pallas_call | solution.py:503
  41.5 1.5 collective-permute-start.13
  43.8 8.0 %shard_map.369.refs_0_.qkv = bf16[512,2304]{1,0:T(8,128)(2,1)} custom-call(s32[4]{0:T(128)} %pad_add_fusion.info, bf16[512,768]{1,0:T(8,128)(2,1)} %get-tuple-element.128.refs_6_.n1.left, f32[16,768]{1,0:T(8,128)} %get-tuple-element.127.vec, bf16[96,2304]{1,0:T(8,128)(2,1)} %refs_0_.3, bf16[96,2304]{1,0:T(8,128)(2,1)} %copy-done.59, ...), custom_call_target="tpu_custom_call" | custom-call | flops 1760000000 | bytes 1600000 | tf_op jit(solution)/shard_map/pallas_call | solution.py:503
  51.8 4.5 %collective-permute-done.14.refs_2_.refs_1_ = bf16[384,768]{1,0:T(8,128)(2,1)S(1)} collective-permute-done((bf16[384,768]{1,0:T(8,128)(2,1)}, bf16[384,768]{1,0:T(8,128)(2,1)S(1)}, u32[]{:S(2)}, u32[]{:S(2)}) %collective-permute-start.14) | collective-permute-done | bytes 589856 | tf_op jit(solution)/shard_map/ppermute | solution.py:515
  61.9 1.5 collective-permute-start.18
  63.3 11.4 %shard_map.371 = (bf16[12,512,256]{2,1,0:T(8,128)(2,1)}, bf16[512,768]{1,0:T(8,128)(2,1)}) custom-call(s32[4]{0:T(128)} %pad_add_fusion.info, bf16[512,2304]{1,0:T(8,128)(2,1)} %shard_map.369.refs_0_.qkv, f32[8,128]{1,0:T(8,128)} %shard_map.370.refs_0_.refs_5_), custom_call_target="tpu_custom_call" | custom-call | flops 2200000000 | bytes 2000000 | tf_op jit(solution)/shard_map/pallas_call | solution.py:503
  74.7 4.2 %collective-permute-done.18.refs_4_.refs_3_ = bf16[176,768]{1,0:T(8,128)(2,1)S(1)} collective-permute-done((bf16[176,768]{1,0:T(8,128)(2,1)S(1)}, bf16[176,768]{1,0:T(8,128)(2,1)S(1)}, u32[]{:S(2)}, u32[]{:S(2)}) %collective-permute-start.18) | collective-permute-done | bytes 270368 | tf_op jit(solution)/shard_map/ppermute | solution.py:515
  78.9 2.7 collective-permute-done.15.refs_1_.refs_0_
  86.1 1.7 collective-permute-start.21
  87.9 4.5 %shard_map.374 = (f32[512,768]{1,0:T(8,128)}, bf16[80,768]{1,0:T(8,128)(2,1)}, bf16[208,768]{1,0:T(8,128)(2,1)}, bf16[208,768]{1,0:T(8,128)(2,1)}) custom-call(s32[4]{0:T(128)} %pad_add_fusion.info, bf16[512,768]{1,0:T(8,128)(2,1)} %get-tuple-element.125.refs_2_.tok, f32[512,1]{1,0:T(8,128)} %bitcast.148, f32[16,768]{1,0:T(8,128)} %get-tuple-element.127.vec, ...), custom_call_target="tpu_custom_call" | custom-call | flops 1100000000 | bytes 1000000 | tf_op jit(solution)/shard_map/pallas_call | solution.py:503
  92.4 1.7 copy.172.refs_4_
  94.2 1.7 copy.173.refs_5_
  97.8 2.2 shard_map.378.refs_8_
  100.4 2.0 collective-permute-start.23
  103.9 10.3 %shard_map.379 = (f32[416,768]{1,0:T(8,128)}, f32[416,768]{1,0:T(8,128)}, bf16[416,1536]{1,0:T(8,128)(2,1)}, bf16[416,1536]{1,0:T(8,128)(2,1)}) custom-call(s32[4]{0:T(128)} %pad_add_fusion.info, bf16[416,768]{1,0:T(8,128)(2,1)} %get-tuple-element.148.grad, f32[1,1536]{1,0:T(1,128)} %get-tuple-element.149.up_bias, ...), custom_call_target="tpu_custom_call" | custom-call | flops 1980000000 | bytes 1800000 | tf_op jit(solution)/shard_map/pallas_call | solution.py:503
  114.2 2.8 collective-permute-done.23.refs_1_
  117.0 3.4 collective-permute-done.25.refs_3_
  126.7 6.4 %shard_map.382 = (bf16[4,80,768]{2,1,0:T(8,128)(2,1)}, bf16[4,80,768]{2,1,0:T(8,128)(2,1)}, bf16[4,80,768]{2,1,0:T(8,128)(2,1)}, bf16[4,80,768]{2,1,0:T(8,128)(2...) custom-call(s32[4]{0:T(128)} %pad_add_fusion.info, ...), custom_call_target="tpu_custom_call" | custom-call | flops 1320000000 | bytes 1200000 | tf_op jit(solution)/shard_map/pallas_call | solution.py:503
  133.1 3.0 collective-permute-done.28.refs_2_
  137.5 2.1 collective-permute-done.29
  141.1 2.1 collective-permute-start.32
  143.3 10.1 %shard_map.385 = (bf16[416,768]{1,0:T(8,128)(2,1)}, bf16[416,768]{1,0:T(8,128)(2,1)}, bf16[416,1536]{1,0:T(8,128)(2,1)}, bf16[416,1536]{1,0:T(8,128)(2,1)}) custom-call(s32[4]{0:T(128)} %pad_add_fusion.info, bf16[2,416,768]{2,1,0:T(8,128)(2,1)} %bitcast.138, f32[1,1536]{1,0:T(1,128)} %get-tuple-element.149.up_bias, ...), custom_call_target="tpu_custom_call" | custom-call | flops 1980000000 | bytes 1800000 | tf_op jit(solution)/shard_map/pallas_call | solution.py:503
  154.9 12.6 %shard_map.387 = (bf16[4,96,1536]{2,1,0:T(8,128)(2,1)}, bf16[4,96,1536]{2,1,0:T(8,128)(2,1)}, bf16[2,384,768]{2,1,0:T(8,128)(2,1)}, bf16[2,384,768]{2,1,0:T(8,128)(2,1)}, f32[1,1536]{1,0:T(1,128)}) custom-call(s32[4]{0:T(128)} %pad_add_fusion.info, bf16[208,768]{1,0:T(8,128)(2,1)} %get-tuple-element.150.refs_0_, ...), custom_call_target="tpu_custom_call" | custom-call | flops 2640000000 | bytes 2400000 | tf_op jit(solution)/shard_map/pallas_call | solution.py:503
  167.5 3.0 collective-permute-done.33.refs_1_.refs_4_
  172.8 2.2 collective-permute-done.35
  178.8 17.9 %shard_map.391 = (f32[512,768]{1,0:T(8,128)}, bf16[512,768]{1,0:T(8,128)(2,1)}, bf16[512,2304]{1,0:T(8,128)(2,1)}, f32[8,768]{1,0:T(8,128)}) custom-call(s32[4]{0:T(128)} %pad_add_fusion.info, f32[416,768]{1,0:T(8,128)} %get-tuple-element.168.refs_0_.gn2v, bf16[416,768]{1,0:T(8,128)(2,1)} %get-tuple-element.191.gn2x, bf16[4,80,768]{2,1,0:T(8,128)(2,1)} %copy-done.34, ...), custom_call_target="tpu_custom_call" | custom-call | flops 3960000000 | bytes 3600000 | tf_op jit(solution)/shard_map/pallas_call | solution.py:503
  199.6 8.0 %collective-permute-done.41.refs_2_ = bf16[96,1536]{1,0:T(8,128)(2,1)S(1)} collective-permute-done((bf16[96,1536]{1,0:T(8,128)(2,1)}, bf16[96,1536]{1,0:T(8,128)(2,1)S(1)}, u32[]{:S(2)}, u32[]{:S(2)}) %collective-permute-start.41) | collective-permute-done | bytes 294944 | tf_op jit(solution)/shard_map/ppermute | solution.py:515
  207.6 2.0 fusion.13
  210.0 1.4 slice_reduce_fusion.1
  212.7 5.3 %shard_map.393 = (bf16[4,96,1536]{2,1,0:T(8,128)(2,1)}, bf16[4,96,1536]{2,1,0:T(8,128)(2,1)}) custom-call(s32[4]{0:T(128)} %pad_add_fusion.info, bf16[512,768]{1,0:T(8,128)(2,1)} %get-tuple-element.128.refs_6_.n1.left, bf16[512,2304]{1,0:T(8,128)(2,1)} %get-tuple-element.198.refs_0_.stacked, bf16[512,768]{1,0:T(8,128)(2,1)} %get-tuple-element.138.refs_0_.ctx.other_left, ...), custom_call_target="tpu_custom_call" | custom-call | flops 1100000000 | bytes 1000000 | tf_op jit(solution)/shard_map/pallas_call | solution.py:503
  220.4 1.4 convert_add_fusion
  221.9 1.8 fusion.1
  227.2 5.4 %shard_map.397 = (bf16[4,96,1536]{2,1,0:T(8,128)(2,1)}, bf16[4,96,1536]{2,1,0:T(8,128)(2,1)}) custom-call(s32[4]{0:T(128)} %pad_add_fusion.info, bf16[512,768]{1,0:T(8,128)(2,1)} %get-tuple-element.128.refs_6_.n1.left, bf16[512,2304]{1,0:T(8,128)(2,1)} %get-tuple-element.198.refs_0_.stacked, bf16[512,768]{1,0:T(8,128)(2,1)} %get-tuple-element.138.refs_0_.ctx.other_left, ...), custom_call_target="tpu_custom_call" | custom-call | flops 1100000000 | bytes 1000000 | tf_op jit(solution)/shard_map/pallas_call | solution.py:503
  236.8 1.7 collective-permute-start.47
  244.9 2.0 collective-permute-start.45
  247.0 11.7 %shard_map.400 = (f32[512,768]{1,0:T(8,128)}, f32[8,768]{1,0:T(8,128)}) custom-call(s32[4]{0:T(128)} %pad_add_fusion.info, bf16[512,2304]{1,0:T(8,128)(2,1)} %get-tuple-element.198.refs_0_.stacked, f32[512,768]{1,0:T(8,128)} %get-tuple-element.210.gh1, bf16[512,768]{1,0:T(8,128)(2,1)} %get-tuple-element.125.refs_2_.tok, f32[512,1]{1,0:T(8,128)} %bitcast.149, ...), custom_call_target="tpu_custom_call" | custom-call | flops 2640000000 | bytes 2400000 | tf_op jit(solution)/shard_map/pallas_call | solution.py:503
  258.7 1.7 collective-permute-done.44.refs_4_
  264.5 1.4 concatenate.53
  267.2 1.5 collective-permute-start.50
  268.7 1.8 pad_maximum_fusion.3
  272.4 1.7 pad_maximum_fusion
  274.2 1.4 collective-permute-done.51
  275.6 1.4 collective-permute-start.52
  277.1 1.8 fusion.11
  281.0 3.0 collective-permute-start.53
  284.0 1.8 fusion.12
  285.8 1.4 collective-permute-start.58
  287.8 1.3 reshape.147
  290.3 1.4 maximum_select_fusion
  293.6 1.7 collective-permute-start.65
  296.5 2.1 collective-permute-start.55
  299.8 1.3 collective-permute-start.59
  302.4 15.9 %collective-permute-done.59 = bf16[96,1536]{1,0:T(8,128)(2,1)S(1)} collective-permute-done((bf16[96,1536]{1,0:T(8,128)(2,1)S(1)}, bf16[96,1536]{1,0:T(8,128)(2,1)S(1)}, u32[]{:S(2)}, u32[]{:S(2)}) %collective-permute-start.59) | collective-permute-done | bytes 294944 | tf_op jit(solution)/shard_map/ppermute | solution.py:519
  319.9 1.3 collective-permute-start.61
  321.3 1.3 collective-permute-start.57
  322.6 24.9 %collective-permute-done.61 = bf16[96,1536]{1,0:T(8,128)(2,1)S(1)} collective-permute-done((bf16[96,1536]{1,0:T(8,128)(2,1)S(1)}, bf16[96,1536]{1,0:T(8,128)(2,1)S(1)}, u32[]{:S(2)}, u32[]{:S(2)}) %collective-permute-start.61) | collective-permute-done | bytes 294944 | tf_op jit(solution)/shard_map/ppermute | solution.py:519
  348.4 11.1 %collective-permute-done.57 = bf16[96,1536]{1,0:T(8,128)(2,1)S(1)} collective-permute-done((bf16[96,1536]{1,0:T(8,128)(2,1)S(1)}, bf16[96,1536]{1,0:T(8,128)(2,1)S(1)}, u32[]{:S(2)}, u32[]{:S(2)}) %collective-permute-start.57) | collective-permute-done | bytes 294944 | tf_op jit(solution)/shard_map/ppermute | solution.py:519
  (403 shorter events, 89.2 us)
Async XLA Ops:
  8.0 79.8 %all-gather.4.cloned.1.call-start = ((), (), s32[]{:S(2)}) async-start(), calls=%async_computation | async-start | bytes 1327104 | tf_op jit(solution)/shard_map/all_gather | solution.py:635
  8.1 15.0 %collective-permute-start.5 = (bf16[96,2304]{1,0:T(8,128)(2,1)}, bf16[96,2304]{1,0:T(8,128)(2,1)S(1)}, u32[]{:S(2)}, u32[]{:S(2)}) collective-permute-start(bf16[96,2304]{1,0:T(8,128)(2,1)} %refs_0_.3), channel_id=1, source_target_pairs={{0,16},{4,20},{8,24},{12,28},{16,0},{20,4},{24,8},{28,12},{1,17},{... | collective-permute-start | bytes 1327112 | tf_op jit(solution)/shard_map/ppermute | solution.py:515
  11.1 12.5 %collective-permute-start.4 = (bf16[96,2304]{1,0:T(8,128)(2,1)}, bf16[96,2304]{1,0:T(8,128)(2,1)S(1)}, u32[]{:S(2)}, u32[]{:S(2)}) collective-permute-start(bf16[96,2304]{1,0:T(8,128)(2,1)} %refs_0_.3), channel_id=1, source_target_pairs={{0,8},{4,12},{8,0},{12,4},{16,24},{20,28},{24,16},{28,20},{1,9},{5... | collective-permute-start | bytes 1327112 | tf_op jit(solution)/shard_map/ppermute | solution.py:515
  14.8 8.3 %collective-permute-start = (bf16[1,16,128]{2,1,0:T(8,128)(2,1)S(1)}, bf16[1,16,128]{2,1,0:T(8,128)(2,1)S(1)}, u32[]{:S(2)}, u32[]{:S(2)}) collective-permute-start(bf16[1,16,128]{2,1,0:T(8,128)(2,1)S(1)} %pad_bitcast_fusion), channel_id=1, source_target_pairs={{0,8},{4,12},{8,0},{12,4},{16,24},{20,28},{24,16},{28,20},{1,9},{5... | collective-permute-start | bytes 12296 | tf_op jit(solution)/shard_map/ppermute | solution.py:515
  15.4 8.3 %collective-permute-start.1 = (bf16[1,16,128]{2,1,0:T(8,128)(2,1)S(1)}, bf16[1,16,128]{2,1,0:T(8,128)(2,1)S(1)}, u32[]{:S(2)}, u32[]{:S(2)}) collective-permute-start(bf16[1,16,128]{2,1,0:T(8,128)(2,1)S(1)} %pad_bitcast_fusion), channel_id=1, source_target_pairs={{0,16},{4,20},{8,24},{12,28},{16,0},{20,4},{24,8},{28,12},{1,17},{... | collective-permute-start | bytes 12296 | tf_op jit(solution)/shard_map/ppermute | solution.py:515
  15.5 8.2 %collective-permute-start.2 = (bf16[1,16,128]{2,1,0:T(8,128)(2,1)S(1)}, bf16[1,16,128]{2,1,0:T(8,128)(2,1)S(1)}, u32[]{:S(2)}, u32[]{:S(2)}) collective-permute-start(bf16[1,16,128]{2,1,0:T(8,128)(2,1)S(1)} %pad_bitcast_fusion), channel_id=1, source_target_pairs={{0,24},{4,28},{8,16},{12,20},{16,8},{20,12},{24,0},{28,4},{1,25},{... | collective-permute-start | bytes 12296 | tf_op jit(solution)/shard_map/ppermute | solution.py:515
  23.1 15.1 %collective-permute-start.8 = (bf16[96,2304]{1,0:T(8,128)(2,1)S(1)}, bf16[96,2304]{1,0:T(8,128)(2,1)S(1)}, u32[]{:S(2)}, u32[]{:S(2)}) collective-permute-start(bf16[96,2304]{1,0:T(8,128)(2,1)S(1)} %copy-done.73), channel_id=1, source_target_pairs={{0,4},{4,0},{8,12},{12,8},{16,20},{20,16},{24,28},{28,24},{1,5},{5... | collective-permute-start | bytes 1327112 | tf_op jit(solution)/shard_map/ppermute | solution.py:515
  23.1 15.7 %collective-permute-start.10 = (bf16[96,2304]{1,0:T(8,128)(2,1)S(1)}, bf16[96,2304]{1,0:T(8,128)(2,1)S(1)}, u32[]{:S(2)}, u32[]{:S(2)}) collective-permute-start(bf16[96,2304]{1,0:T(8,128)(2,1)S(1)} %collective-permute-done.5.refs_2_), channel_id=1, source_target_pairs={{0,4},{4,0},{8,12},{12,8},{16,20},{20,16},{24,28},{28,24},{1,5},{5... | collective-permute-start | bytes 1327112 | tf_op jit(solution)/shard_map/ppermute | solution.py:515
  23.6 15.2 %collective-permute-start.9 = (bf16[96,2304]{1,0:T(8,128)(2,1)S(1)}, bf16[96,2304]{1,0:T(8,128)(2,1)S(1)}, u32[]{:S(2)}, u32[]{:S(2)}) collective-permute-start(bf16[96,2304]{1,0:T(8,128)(2,1)S(1)} %collective-permute-done.4.refs_1_), channel_id=1, source_target_pairs={{0,4},{4,0},{8,12},{12,8},{16,20},{20,16},{24,28},{28,24},{1,5},{5... | collective-permute-start | bytes 1327112 | tf_op jit(solution)/shard_map/ppermute | solution.py:515
  23.7 6.2 %collective-permute-start.3 = (bf16[4,16,128]{2,1,0:T(8,128)(2,1)S(1)}, bf16[4,16,128]{2,1,0:T(8,128)(2,1)S(1)}, u32[]{:S(2)}, u32[]{:S(2)}) collective-permute-start(bf16[4,16,128]{2,1,0:T(8,128)(2,1)S(1)} %pad_maximum_fusion.7.even), channel_id=1, source_target_pairs={{0,4},{4,0},{8,12},{12,8},{16,20},{20,16},{24,28},{28,24},{1,5},{5... | collective-permute-start | bytes 49160 | tf_op jit(solution)/shard_map/ppermute | solution.py:515
  30.6 7.7 %collective-permute-start.6 = (bf16[48,2304]{1,0:T(8,128)(2,1)}, bf16[48,2304]{1,0:T(8,128)(2,1)S(1)}, u32[]{:S(2)}, u32[]{:S(2)}) collective-permute-start(bf16[48,2304]{1,0:T(8,128)(2,1)} %get-tuple-element.126.refs_0_), channel_id=1, source_target_pairs={{0,16},{4,20},{8,24},{12,28},{16,0},{20,4},{24,8},{28,12},{1,17},{... | collective-permute-start | bytes 663560 | tf_op jit(solution)/shard_map/ppermute | solution.py:515
  31.0 7.7 %collective-permute-start.7 = (bf16[48,2304]{1,0:T(8,128)(2,1)}, bf16[48,2304]{1,0:T(8,128)(2,1)S(1)}, u32[]{:S(2)}, u32[]{:S(2)}) collective-permute-start(bf16[48,2304]{1,0:T(8,128)(2,1)} %get-tuple-element.129), channel_id=1, source_target_pairs={{0,8},{4,12},{8,0},{12,4},{16,24},{20,28},{24,16},{28,20},{1,9},{5... | collective-permute-start | bytes 663560 | tf_op jit(solution)/shard_map/ppermute | solution.py:515
  39.8 16.5 %collective-permute-start.14 = (bf16[384,768]{1,0:T(8,128)(2,1)}, bf16[384,768]{1,0:T(8,128)(2,1)S(1)}, u32[]{:S(2)}, u32[]{:S(2)}) collective-permute-start(bf16[384,768]{1,0:T(8,128)(2,1)} %get-tuple-element.137), channel_id=1, source_target_pairs={{0,16},{4,20},{8,24},{12,28},{16,0},{20,4},{24,8},{28,12},{1,17},{... | collective-permute-start | bytes 1769480 | tf_op jit(solution)/shard_map/ppermute | solution.py:515
  41.5 10.3 %collective-permute-start.13 = (bf16[96,1536]{1,0:T(8,128)(2,1)}, bf16[96,1536]{1,0:T(8,128)(2,1)S(1)}, u32[]{:S(2)}, u32[]{:S(2)}) collective-permute-start(bf16[96,1536]{1,0:T(8,128)(2,1)} %get-tuple-element.136), channel_id=1, source_target_pairs={{0,8},{4,12},{8,0},{12,4},{16,24},{20,28},{24,16},{28,20},{1,9},{5... | collective-permute-start | bytes 884744 | tf_op jit(solution)/shard_map/ppermute | solution.py:515
  43.0 90.1 %all-gather.6.cloned.1.call-start = ((), (), s32[]{:S(2)}) async-start(), calls=%async_computation.3 | async-start | bytes 1916928 | tf_op jit(solution)/shard_map/all_gather | solution.py:714
  59.8 21.8 %collective-permute-start.15 = (bf16[2,96,1536]{2,1,0:T(8,128)(2,1)S(1)}, bf16[2,96,1536]{2,1,0:T(8,128)(2,1)S(1)}, u32[]{:S(2)}, u32[]{:S(2)}) collective-permute-start(bf16[2,96,1536]{2,1,0:T(8,128)(2,1)S(1)} %pad_maximum_fusion.4.refs_2_), channel_id=1, source_target_pairs={{0,16},{4,20},{8,24},{12,28},{16,0},{20,4},{24,8},{28,12},{1,17},{... | collective-permute-start | bytes 1769480 | tf_op jit(solution)/shard_map/ppermute | solution.py:515
  61.0 20.6 %collective-permute-start.16 = (bf16[2,96,1536]{2,1,0:T(8,128)(2,1)S(1)}, bf16[2,96,1536]{2,1,0:T(8,128)(2,1)S(1)}, u32[]{:S(2)}, u32[]{:S(2)}) collective-permute-start(bf16[2,96,1536]{2,1,0:T(8,128)(2,1)S(1)} %pad_maximum_fusion.4.refs_2_), channel_id=1, source_target_pairs={{0,4},{4,0},{8,12},{12,8},{16,20},{20,16},{24,28},{28,24},{1,5},{5... | collective-permute-start | bytes 1769480 | tf_op jit(solution)/shard_map/ppermute | solution.py:515
  61.0 13.7 %collective-permute-start.17 = (bf16[176,768]{1,0:T(8,128)(2,1)S(1)}, bf16[176,768]{1,0:T(8,128)(2,1)S(1)}, u32[]{:S(2)}, u32[]{:S(2)}) collective-permute-start(bf16[176,768]{1,0:T(8,128)(2,1)S(1)} %copy-done.76), channel_id=1, source_target_pairs={{0,8},{4,12},{8,0},{12,4},{16,24},{20,28},{24,16},{28,20},{1,9},{5... | collective-permute-start | bytes 811016 | tf_op jit(solution)/shard_map/ppermute | solution.py:515
  61.9 17.0 %collective-permute-start.18 = (bf16[176,768]{1,0:T(8,128)(2,1)S(1)}, bf16[176,768]{1,0:T(8,128)(2,1)S(1)}, u32[]{:S(2)}, u32[]{:S(2)}) collective-permute-start(bf16[176,768]{1,0:T(8,128)(2,1)S(1)} %copy-done.77), channel_id=1, source_target_pairs={{0,24},{4,28},{8,16},{12,20},{16,8},{20,12},{24,0},{28,4},{1,25},{... | collective-permute-start | bytes 811016 | tf_op jit(solution)/shard_map/ppermute | solution.py:515
  85.5 11.0 %collective-permute-start.20 = (bf16[2,384,768]{2,1,0:T(8,128)(2,1)S(1)}, bf16[2,384,768]{2,1,0:T(8,128)(2,1)}, u32[]{:S(2)}, u32[]{:S(2)}) collective-permute-start(bf16[2,384,768]{2,1,0:T(8,128)(2,1)S(1)} %pad_maximum_fusion.1.refs_6_), channel_id=1, source_target_pairs={{0,4},{4,0},{8,12},{12,8},{16,20},{20,16},{24,28},{28,24},{1,5},{5... | collective-permute-start | bytes 3538952 | tf_op jit(solution)/shard_map/ppermute | solution.py:515
  85.6 10.9 %collective-permute-start.19 = (bf16[2,96,1536]{2,1,0:T(8,128)(2,1)S(1)}, bf16[2,96,1536]{2,1,0:T(8,128)(2,1)}, u32[]{:S(2)}, u32[]{:S(2)}) collective-permute-start(bf16[2,96,1536]{2,1,0:T(8,128)(2,1)S(1)} %copy-done.28), channel_id=1, source_target_pairs={{0,4},{4,0},{8,12},{12,8},{16,20},{20,16},{24,28},{28,24},{1,5},{5... | collective-permute-start | bytes 1769480 | tf_op jit(solution)/shard_map/ppermute | solution.py:515
  86.1 10.4 %collective-permute-start.21 = (bf16[176,768]{1,0:T(8,128)(2,1)S(1)}, bf16[176,768]{1,0:T(8,128)(2,1)S(1)}, u32[]{:S(2)}, u32[]{:S(2)}) collective-permute-start(bf16[176,768]{1,0:T(8,128)(2,1)S(1)} %copy-done.57), channel_id=1, source_target_pairs={{0,16},{4,20},{8,24},{12,28},{16,0},{20,4},{24,8},{28,12},{1,17},{... | collective-permute-start | bytes 811016 | tf_op jit(solution)/shard_map/ppermute | solution.py:515
  100.0 20.4 %collective-permute-start.22 = (bf16[512,768]{1,0:T(8,128)(2,1)}, bf16[512,768]{1,0:T(8,128)(2,1)S(1)}, u32[]{:S(2)}, u32[]{:S(2)}) collective-permute-start(bf16[512,768]{1,0:T(8,128)(2,1)} %shard_map.378.refs_8_), channel_id=1, source_target_pairs={{0,4},{4,0},{8,12},{12,8},{16,20},{20,16},{24,28},{28,24},{1,5},{5... | collective-permute-start | bytes 2359304 | tf_op jit(solution)/shard_map/ppermute | solution.py:515
  100.1 174.1 %all-reduce.13.cloned.1.call-start = ((), (), s32[]{:S(2)}) async-start(), calls=%async_computation.4 | async-start | bytes 2359296 | tf_op jit(solution)/shard_map/psum | solution.py:862
  100.3 20.1 %collective-permute-start.26 = (bf16[208,768]{1,0:T(8,128)(2,1)S(1)}, bf16[208,768]{1,0:T(8,128)(2,1)S(1)}, u32[]{:S(2)}, u32[]{:S(2)}) collective-permute-start(bf16[208,768]{1,0:T(8,128)(2,1)S(1)} %copy-done.37), channel_id=1, source_target_pairs={{0,8},{4,12},{8,0},{12,4},{16,24},{20,28},{24,16},{28,20},{1,9},{5... | collective-permute-start | bytes 958472 | tf_op jit(solution)/shard_map/ppermute | solution.py:515
  100.4 16.6 %collective-permute-start.23 = (bf16[80,768]{1,0:T(8,128)(2,1)S(1)}, bf16[80,768]{1,0:T(8,128)(2,1)S(1)}, u32[]{:S(2)}, u32[]{:S(2)}) collective-permute-start(bf16[80,768]{1,0:T(8,128)(2,1)S(1)} %copy-done.72), channel_id=1, source_target_pairs={{0,8},{4,12},{8,0},{12,4},{16,24},{20,28},{24,16},{28,20},{1,9},{5... | collective-permute-start | bytes 368648 | tf_op jit(solution)/shard_map/ppermute | solution.py:515
  102.4 14.6 %collective-permute-start.24 = (bf16[80,768]{1,0:T(8,128)(2,1)S(1)}, bf16[80,768]{1,0:T(8,128)(2,1)S(1)}, u32[]{:S(2)}, u32[]{:S(2)}) collective-permute-start(bf16[80,768]{1,0:T(8,128)(2,1)S(1)} %copy-done.72), channel_id=1, source_target_pairs={{0,16},{4,20},{8,24},{12,28},{16,0},{20,4},{24,8},{28,12},{1,17},{... | collective-permute-start | bytes 368648 | tf_op jit(solution)/shard_map/ppermute | solution.py:515
  102.7 17.7 %collective-permute-start.25 = (bf16[80,768]{1,0:T(8,128)(2,1)S(1)}, bf16[80,768]{1,0:T(8,128)(2,1)S(1)}, u32[]{:S(2)}, u32[]{:S(2)}) collective-permute-start(bf16[80,768]{1,0:T(8,128)(2,1)S(1)} %copy-done.72), channel_id=1, source_target_pairs={{0,24},{4,28},{8,16},{12,20},{16,8},{20,12},{24,0},{28,4},{1,25},{... | collective-permute-start | bytes 368648 | tf_op jit(solution)/shard_map/ppermute | solution.py:515
  124.1 12.0 %collective-permute-start.28 = (bf16[208,768]{1,0:T(8,128)(2,1)}, bf16[208,768]{1,0:T(8,128)(2,1)S(1)}, u32[]{:S(2)}, u32[]{:S(2)}) collective-permute-start(bf16[208,768]{1,0:T(8,128)(2,1)} %get-tuple-element.175), channel_id=1, source_target_pairs={{0,8},{4,12},{8,0},{12,4},{16,24},{20,28},{24,16},{28,20},{1,9},{5... | collective-permute-start | bytes 958472 | tf_op jit(solution)/shard_map/ppermute | solution.py:515
  139.7 13.6 %collective-permute-start.30 = (bf16[80,768]{1,0:T(8,128)(2,1)S(1)}, bf16[80,768]{1,0:T(8,128)(2,1)S(1)}, u32[]{:S(2)}, u32[]{:S(2)}) collective-permute-start(bf16[80,768]{1,0:T(8,128)(2,1)S(1)} %get-tuple-element.259), channel_id=1, source_target_pairs={{0,8},{4,12},{8,0},{12,4},{16,24},{20,28},{24,16},{28,20},{1,9},{5... | collective-permute-start | bytes 368648 | tf_op jit(solution)/shard_map/ppermute | solution.py:515
  140.0 13.3 %collective-permute-start.31 = (bf16[80,768]{1,0:T(8,128)(2,1)S(1)}, bf16[80,768]{1,0:T(8,128)(2,1)S(1)}, u32[]{:S(2)}, u32[]{:S(2)}) collective-permute-start(bf16[80,768]{1,0:T(8,128)(2,1)S(1)} %get-tuple-element.258), channel_id=1, source_target_pairs={{0,16},{4,20},{8,24},{12,28},{16,0},{20,4},{24,8},{28,12},{1,17},{... | collective-permute-start | bytes 368648 | tf_op jit(solution)/shard_map/ppermute | solution.py:515
  141.1 12.2 %collective-permute-start.32 = (bf16[80,768]{1,0:T(8,128)(2,1)S(1)}, bf16[80,768]{1,0:T(8,128)(2,1)S(1)}, u32[]{:S(2)}, u32[]{:S(2)}) collective-permute-start(bf16[80,768]{1,0:T(8,128)(2,1)S(1)} %get-tuple-element.257), channel_id=1, source_target_pairs={{0,24},{4,28},{8,16},{12,20},{16,8},{20,12},{24,0},{28,4},{1,25},{... | collective-permute-start | bytes 368648 | tf_op jit(solution)/shard_map/ppermute | solution.py:515
  154.7 15.8 %collective-permute-start.33 = (bf16[416,768]{1,0:T(8,128)(2,1)}, bf16[416,768]{1,0:T(8,128)(2,1)S(1)}, u32[]{:S(2)}, u32[]{:S(2)}) collective-permute-start(bf16[416,768]{1,0:T(8,128)(2,1)} %shard_map.388), channel_id=1, source_target_pairs={{0,8},{4,12},{8,0},{12,4},{16,24},{20,28},{24,16},{28,20},{1,9},{5... | collective-permute-start | bytes 1916936 | tf_op jit(solution)/shard_map/ppermute | solution.py:515
  171.9 3.1 collective-permute-start.35
  171.9 4.7 %collective-permute-start.36 = (bf16[4,96,1536]{2,1,0:T(8,128)(2,1)}, bf16[4,96,1536]{2,1,0:T(8,128)(2,1)S(1)}, u32[]{:S(2)}, u32[]{:S(2)}) collective-permute-start(bf16[4,96,1536]{2,1,0:T(8,128)(2,1)} %get-tuple-element.197), channel_id=1, source_target_pairs={{0,4},{4,0},{8,12},{12,8},{16,20},{20,16},{24,28},{28,24},{1,5},{5... | collective-permute-start | bytes 3538952 | tf_op jit(solution)/shard_map/ppermute | solution.py:515
  172.4 24.4 %collective-permute-start.34 = (bf16[416,768]{1,0:T(8,128)(2,1)}, bf16[416,768]{1,0:T(8,128)(2,1)S(1)}, u32[]{:S(2)}, u32[]{:S(2)}) collective-permute-start(bf16[416,768]{1,0:T(8,128)(2,1)} %get-tuple-element.190), channel_id=1, source_target_pairs={{0,8},{4,12},{8,0},{12,4},{16,24},{20,28},{24,16},{28,20},{1,9},{5... | collective-permute-start | bytes 1916936 | tf_op jit(solution)/shard_map/ppermute | solution.py:515
  172.8 24.0 %collective-permute-start.39 = (bf16[4,80,768]{2,1,0:T(8,128)(2,1)}, bf16[4,80,768]{2,1,0:T(8,128)(2,1)S(1)}, u32[]{:S(2)}, u32[]{:S(2)}) collective-permute-start(bf16[4,80,768]{2,1,0:T(8,128)(2,1)} %get-tuple-element.200), channel_id=1, source_target_pairs={{0,4},{4,0},{8,12},{12,8},{16,20},{20,16},{24,28},{28,24},{1,5},{5... | collective-permute-start | bytes 1474568 | tf_op jit(solution)/shard_map/ppermute | solution.py:515
  175.1 21.8 %collective-permute-start.37 = (bf16[384,768]{1,0:T(8,128)(2,1)S(1)}, bf16[384,768]{1,0:T(8,128)(2,1)S(1)}, u32[]{:S(2)}, u32[]{:S(2)}) collective-permute-start(bf16[384,768]{1,0:T(8,128)(2,1)S(1)} %fusion.3.refs_0_), channel_id=1, source_target_pairs={{0,16},{4,20},{8,24},{12,28},{16,0},{20,4},{24,8},{28,12},{1,17},{... | collective-permute-start | bytes 1769480 | tf_op jit(solution)/shard_map/ppermute | solution.py:515
  177.8 19.1 %collective-permute-start.38 = (bf16[96,1536]{1,0:T(8,128)(2,1)S(1)}, bf16[96,1536]{1,0:T(8,128)(2,1)S(1)}, u32[]{:S(2)}, u32[]{:S(2)}) collective-permute-start(bf16[96,1536]{1,0:T(8,128)(2,1)S(1)} %get-tuple-element.239.refs_2_), channel_id=1, source_target_pairs={{0,16},{4,20},{8,24},{12,28},{16,0},{20,4},{24,8},{28,12},{1,17},{... | collective-permute-start | bytes 884744 | tf_op jit(solution)/shard_map/ppermute | solution.py:515
  198.7 9.0 %collective-permute-start.41 = (bf16[96,1536]{1,0:T(8,128)(2,1)}, bf16[96,1536]{1,0:T(8,128)(2,1)S(1)}, u32[]{:S(2)}, u32[]{:S(2)}) collective-permute-start(bf16[96,1536]{1,0:T(8,128)(2,1)} %get-tuple-element.204), channel_id=1, source_target_pairs={{0,16},{4,20},{8,24},{12,28},{16,0},{20,4},{24,8},{28,12},{1,17},{... | collective-permute-start | bytes 884744 | tf_op jit(solution)/shard_map/ppermute | solution.py:515
  209.7 8.3 %collective-permute-start.40 = (bf16[96,1536]{1,0:T(8,128)(2,1)S(1)}, bf16[96,1536]{1,0:T(8,128)(2,1)S(1)}, u32[]{:S(2)}, u32[]{:S(2)}) collective-permute-start(bf16[96,1536]{1,0:T(8,128)(2,1)S(1)} %get-tuple-element.238), channel_id=1, source_target_pairs={{0,8},{4,12},{8,0},{12,4},{16,24},{20,28},{24,16},{28,20},{1,9},{5... | collective-permute-start | bytes 884744 | tf_op jit(solution)/shard_map/ppermute | solution.py:515
  212.4 147.9 %all-reduce.11.cloned.1.call-start = ((), (), s32[]{:S(2)}) async-start(), calls=%async_computation.2 | async-start | bytes 1179648 | tf_op jit(solution)/shard_map/psum | solution.py:805
  219.3 13.3 %collective-permute-start.42 = (bf16[4,96,1536]{2,1,0:T(8,128)(2,1)}, bf16[4,96,1536]{2,1,0:T(8,128)(2,1)S(1)}, u32[]{:S(2)}, u32[]{:S(2)}) collective-permute-start(bf16[4,96,1536]{2,1,0:T(8,128)(2,1)} %shard_map.396), channel_id=1, source_target_pairs={{0,4},{4,0},{8,12},{12,8},{16,20},{20,16},{24,28},{28,24},{1,5},{5... | collective-permute-start | bytes 3538952 | tf_op jit(solution)/shard_map/ppermute | solution.py:515
  226.0 134.8 %all-reduce.9.cloned.1.call-start = ((), (), s32[]{:S(2)}) async-start(), calls=%async_computation.1 | async-start | bytes 1179648 | tf_op jit(solution)/shard_map/psum | solution.py:825
  234.2 4.3 %collective-permute-start.46 = (bf16[4,96,1536]{2,1,0:T(8,128)(2,1)}, bf16[4,96,1536]{2,1,0:T(8,128)(2,1)S(1)}, u32[]{:S(2)}, u32[]{:S(2)}) collective-permute-start(bf16[4,96,1536]{2,1,0:T(8,128)(2,1)} %get-tuple-element.212), channel_id=1, source_target_pairs={{0,4},{4,0},{8,12},{12,8},{16,20},{20,16},{24,28},{28,24},{1,5},{5... | collective-permute-start | bytes 3538952 | tf_op jit(solution)/shard_map/ppermute | solution.py:515
  236.8 23.5 %collective-permute-start.47 = (bf16[2,96,1536]{2,1,0:T(8,128)(2,1)}, bf16[2,96,1536]{2,1,0:T(8,128)(2,1)S(1)}, u32[]{:S(2)}, u32[]{:S(2)}) collective-permute-start(bf16[2,96,1536]{2,1,0:T(8,128)(2,1)} %add_convert_fusion.2.refs_10_), channel_id=1, source_target_pairs={{0,8},{4,12},{8,0},{12,4},{16,24},{20,28},{24,16},{28,20},{1,9},{5... | collective-permute-start | bytes 1769480 | tf_op jit(solution)/shard_map/ppermute | solution.py:515
  240.5 19.9 %collective-permute-start.48 = (bf16[2,96,1536]{2,1,0:T(8,128)(2,1)}, bf16[2,96,1536]{2,1,0:T(8,128)(2,1)S(1)}, u32[]{:S(2)}, u32[]{:S(2)}) collective-permute-start(bf16[2,96,1536]{2,1,0:T(8,128)(2,1)} %add_convert_fusion.1.refs_11_), channel_id=1, source_target_pairs={{0,16},{4,20},{8,24},{12,28},{16,0},{20,4},{24,8},{28,12},{1,17},{... | collective-permute-start | bytes 1769480 | tf_op jit(solution)/shard_map/ppermute | solution.py:515
  243.4 15.2 %collective-permute-start.43 = (bf16[80,768]{1,0:T(8,128)(2,1)S(1)}, bf16[80,768]{1,0:T(8,128)(2,1)S(1)}, u32[]{:S(2)}, u32[]{:S(2)}) collective-permute-start(bf16[80,768]{1,0:T(8,128)(2,1)S(1)} %get-tuple-element.254), channel_id=1, source_target_pairs={{0,8},{4,12},{8,0},{12,4},{16,24},{20,28},{24,16},{28,20},{1,9},{5... | collective-permute-start | bytes 368648 | tf_op jit(solution)/shard_map/ppermute | solution.py:515
  243.9 16.4 %collective-permute-start.44 = (bf16[80,768]{1,0:T(8,128)(2,1)S(1)}, bf16[80,768]{1,0:T(8,128)(2,1)S(1)}, u32[]{:S(2)}, u32[]{:S(2)}) collective-permute-start(bf16[80,768]{1,0:T(8,128)(2,1)S(1)} %get-tuple-element.256), channel_id=1, source_target_pairs={{0,16},{4,20},{8,24},{12,28},{16,0},{20,4},{24,8},{28,12},{1,17},{... | collective-permute-start | bytes 368648 | tf_op jit(solution)/shard_map/ppermute | solution.py:515
  244.9 15.4 %collective-permute-start.45 = (bf16[80,768]{1,0:T(8,128)(2,1)S(1)}, bf16[80,768]{1,0:T(8,128)(2,1)S(1)}, u32[]{:S(2)}, u32[]{:S(2)}) collective-permute-start(bf16[80,768]{1,0:T(8,128)(2,1)S(1)} %get-tuple-element.255), channel_id=1, source_target_pairs={{0,24},{4,28},{8,16},{12,20},{16,8},{20,12},{24,0},{28,4},{1,25},{... | collective-permute-start | bytes 368648 | tf_op jit(solution)/shard_map/ppermute | solution.py:515
  267.2 4.2 %collective-permute-start.50 = (f32[14,768]{1,0:T(8,128)S(1)}, f32[14,768]{1,0:T(8,128)S(1)}, u32[]{:S(2)}, u32[]{:S(2)}) collective-permute-start(f32[14,768]{1,0:T(8,128)S(1)} %add.209), channel_id=1, source_target_pairs={{0,8},{4,12},{8,0},{12,4},{16,24},{20,28},{24,16},{28,20},{1,9},{5... | collective-permute-start | bytes 129032 | tf_op jit(solution)/shard_map/ppermute | solution.py:515
  271.4 4.2 %collective-permute-start.51 = (f32[14,768]{1,0:T(8,128)S(1)}, f32[14,768]{1,0:T(8,128)S(1)}, u32[]{:S(2)}, u32[]{:S(2)}) collective-permute-start(f32[14,768]{1,0:T(8,128)S(1)} %add.210), channel_id=1, source_target_pairs={{0,16},{4,20},{8,24},{12,28},{16,0},{20,4},{24,8},{28,12},{1,17},{... | collective-permute-start | bytes 129032 | tf_op jit(solution)/shard_map/ppermute | solution.py:515
  274.2 16.2 %collective-permute-start.62 = (bf16[4,96,384]{2,1,0:T(8,128)(2,1)}, bf16[4,96,384]{2,1,0:T(8,128)(2,1)}, u32[]{:S(2)}, u32[]{:S(2)}) collective-permute-start(bf16[4,96,384]{2,1,0:T(8,128)(2,1)} %get-tuple-element.228), channel_id=1, source_target_pairs={{0,4},{4,0},{8,12},{12,8},{16,20},{20,16},{24,28},{28,24},{1,5},{5... | collective-permute-start | bytes 884744 | tf_op jit(solution)/shard_map/ppermute | solution.py:515
  275.6 5.4 %collective-permute-start.52 = (f32[18,96]{1,0:T(8,128)S(1)}, f32[18,96]{1,0:T(8,128)S(1)}, u32[]{:S(2)}, u32[]{:S(2)}) collective-permute-start(f32[18,96]{1,0:T(8,128)S(1)} %pad_maximum_fusion.8), channel_id=1, source_target_pairs={{0,1},{1,0},{2,3},{3,2},{4,5},{5,4},{6,7},{7,6},{8,9},{9,8},{10,11... | collective-permute-start | bytes 20744 | tf_op jit(solution)/shard_map/ppermute | solution.py:519
  279.9 15.4 %collective-permute-start.54 = (bf16[96,1536]{1,0:T(8,128)(2,1)}, bf16[96,1536]{1,0:T(8,128)(2,1)}, u32[]{:S(2)}, u32[]{:S(2)}) collective-permute-start(bf16[96,1536]{1,0:T(8,128)(2,1)} %fusion.11), channel_id=1, source_target_pairs={{0,16},{4,20},{8,24},{12,28},{16,0},{20,4},{24,8},{28,12},{1,17},{... | collective-permute-start | bytes 884744 | tf_op jit(solution)/shard_map/ppermute | solution.py:515
  281.0 6.2 %collective-permute-start.53 = (f32[18,96]{1,0:T(8,128)S(1)}, f32[18,96]{1,0:T(8,128)S(1)}, u32[]{:S(2)}, u32[]{:S(2)}) collective-permute-start(f32[18,96]{1,0:T(8,128)S(1)} %fusion.18), channel_id=1, source_target_pairs={{0,2},{1,3},{2,0},{3,1},{4,6},{5,7},{6,4},{7,5},{8,10},{9,11},{10,... | collective-permute-start | bytes 20744 | tf_op jit(solution)/shard_map/ppermute | solution.py:519
  285.8 12.8 %collective-permute-start.58 = (bf16[96,1536]{1,0:T(8,128)(2,1)}, bf16[96,1536]{1,0:T(8,128)(2,1)}, u32[]{:S(2)}, u32[]{:S(2)}) collective-permute-start(bf16[96,1536]{1,0:T(8,128)(2,1)} %fusion.12), channel_id=1, source_target_pairs={{0,8},{4,12},{8,0},{12,4},{16,24},{20,28},{24,16},{28,20},{1,9},{5... | collective-permute-start | bytes 884744 | tf_op jit(solution)/shard_map/ppermute | solution.py:515
  291.7 9.4 %collective-permute-start.63 = (bf16[96,768]{1,0:T(8,128)(2,1)S(1)}, bf16[96,768]{1,0:T(8,128)(2,1)S(1)}, u32[]{:S(2)}, u32[]{:S(2)}) collective-permute-start(bf16[96,768]{1,0:T(8,128)(2,1)S(1)} %get-tuple-element.249), channel_id=1, source_target_pairs={{0,8},{4,12},{8,0},{12,4},{16,24},{20,28},{24,16},{28,20},{1,9},{5... | collective-permute-start | bytes 442376 | tf_op jit(solution)/shard_map/ppermute | solution.py:515
  292.5 8.7 %collective-permute-start.64 = (bf16[96,768]{1,0:T(8,128)(2,1)S(1)}, bf16[96,768]{1,0:T(8,128)(2,1)S(1)}, u32[]{:S(2)}, u32[]{:S(2)}) collective-permute-start(bf16[96,768]{1,0:T(8,128)(2,1)S(1)} %get-tuple-element.251), channel_id=1, source_target_pairs={{0,16},{4,20},{8,24},{12,28},{16,0},{20,4},{24,8},{28,12},{1,17},{... | collective-permute-start | bytes 442376 | tf_op jit(solution)/shard_map/ppermute | solution.py:515
  293.6 7.6 %collective-permute-start.65 = (bf16[96,768]{1,0:T(8,128)(2,1)S(1)}, bf16[96,768]{1,0:T(8,128)(2,1)S(1)}, u32[]{:S(2)}, u32[]{:S(2)}) collective-permute-start(bf16[96,768]{1,0:T(8,128)(2,1)S(1)} %get-tuple-element.250), channel_id=1, source_target_pairs={{0,24},{4,28},{8,16},{12,20},{16,8},{20,12},{24,0},{28,4},{1,25},{... | collective-permute-start | bytes 442376 | tf_op jit(solution)/shard_map/ppermute | solution.py:515
  296.5 22.5 %collective-permute-start.55 = (bf16[96,1536]{1,0:T(8,128)(2,1)S(1)}, bf16[96,1536]{1,0:T(8,128)(2,1)S(1)}, u32[]{:S(2)}, u32[]{:S(2)}) collective-permute-start(bf16[96,1536]{1,0:T(8,128)(2,1)S(1)} %fusion.7), channel_id=1, source_target_pairs={{0,1},{3,2},{4,5},{7,6},{8,9},{11,10},{12,13},{15,14},{16,17},{19,... | collective-permute-start | bytes 884744 | tf_op jit(solution)/shard_map/ppermute | solution.py:519
  299.8 18.4 %collective-permute-start.59 = (bf16[96,1536]{1,0:T(8,128)(2,1)S(1)}, bf16[96,1536]{1,0:T(8,128)(2,1)S(1)}, u32[]{:S(2)}, u32[]{:S(2)}) collective-permute-start(bf16[96,1536]{1,0:T(8,128)(2,1)S(1)} %fusion.6), channel_id=1, source_target_pairs={{0,1},{3,2},{4,5},{7,6},{8,9},{11,10},{12,13},{15,14},{16,17},{19,... | collective-permute-start | bytes 884744 | tf_op jit(solution)/shard_map/ppermute | solution.py:519
  319.9 27.6 %collective-permute-start.61 = (bf16[96,1536]{1,0:T(8,128)(2,1)S(1)}, bf16[96,1536]{1,0:T(8,128)(2,1)S(1)}, u32[]{:S(2)}, u32[]{:S(2)}) collective-permute-start(bf16[96,1536]{1,0:T(8,128)(2,1)S(1)} %add_convert_fusion.6), channel_id=1, source_target_pairs={{1,0},{2,3},{5,4},{6,7},{9,8},{10,11},{13,12},{14,15},{17,16},{18,... | collective-permute-start | bytes 884744 | tf_op jit(solution)/shard_map/ppermute | solution.py:519
  321.3 38.2 %collective-permute-start.57 = (bf16[96,1536]{1,0:T(8,128)(2,1)S(1)}, bf16[96,1536]{1,0:T(8,128)(2,1)S(1)}, u32[]{:S(2)}, u32[]{:S(2)}) collective-permute-start(bf16[96,1536]{1,0:T(8,128)(2,1)S(1)} %add_convert_fusion.9), channel_id=1, source_target_pairs={{1,0},{2,3},{5,4},{6,7},{9,8},{10,11},{13,12},{14,15},{17,16},{18,... | collective-permute-start | bytes 884744 | tf_op jit(solution)/shard_map/ppermute | solution.py:519
  (101 other events, 265.7 us)
Sparse Core Ops, SparseCore 0:
  43.1 27.9 all-gather.3
  212.5 57.6 all-reduce.12
  272.6 45.2 all-reduce.10
  320.1 40.5 all-reduce.8
Sparse Core Ops, SparseCore 1:
  100.1 31.0 all-gather.5
